TPU v7x, 256 devices: a whole 4x4x8 slice. The times are simulated.
256 devices in a mesh: dp: 4 (over y_lo, core), px: 8 (over x, y_hi), py: 8 (over z).
Axes of the slice: x: 4, y: 4 (y_hi: 2, y_lo: 2; y = y_hi * 2 + y_lo), z: 8, core: 2. Of those that a mesh axis runs over, the one named last changes fastest.
Arguments:
- state_field: bfloat16 [4, 64, 64, 32, 384], P('dp', 'px', 'py'), may hold values from -6 to 6
- cotangent: bfloat16 [4, 64, 64, 32, 384], P('dp', 'px', 'py'), may hold values from -6 to 6
- first_weight: float32 [2, 4, 96, 96], replicated, may hold values from -0.4375 to 0.4375
- first_bias: float32 [2, 4, 96], replicated, may hold values from -3 to 3
- second_weight: float32 [2, 4, 96, 96], replicated, may hold values from -0.4375 to 0.4375
- second_bias: float32 [2, 4, 96], replicated, may hold values from -3 to 3
Outputs:
- state_grad: bfloat16 [4, 64, 64, 32, 384], P('dp', 'px', 'py')
- first_weight_grad: float32 [2, 4, 96, 96], replicated
- first_bias_grad: float32 [2, 4, 96], replicated
- second_weight_grad: float32 [2, 4, 96, 96], replicated
- second_bias_grad: float32 [2, 4, 96], replicated
All inputs are finite; a program needn't handle non-finite values.
Results may differ from a plain program's by a relative error of at most 0.001.
Values sent between devices are 32-bit elements; how exact they have to be, the bound alone decides.
No kernel may reach another device: no remote copies, remote signals or barrier semaphores. Data moves between devices by JAX's collectives and lax.ppermute only.
A program may use at most 128 MiB of HBM per device.

v0:
```python
import math

import jax
import jax.numpy as jnp
from jax import lax
from jax.sharding import PartitionSpec as P

NX = 64
NY = 64
NZ = 32
NB = 4
BS = 96
KZ = 16


shrink_level = 0.25
highest = lax.Precision.HIGHEST


def complex_table(length, modes):
    row_ids = jnp.arange(length, dtype=jnp.int32)[:, None]
    col_ids = jnp.arange(modes, dtype=jnp.int32)[None, :]
    angles = (row_ids * col_ids % length).astype(jnp.float32) * (2.0 * math.pi / length)
    factor = 1.0 / math.sqrt(length)
    cosine = jnp.cos(angles) * factor
    sine_part = jnp.sin(angles) * factor
    upper_half = jnp.stack([cosine, -sine_part], axis=1)
    lower_half = jnp.stack([sine_part, cosine], axis=1)
    return jnp.stack([upper_half, lower_half], axis=0)


def pair_table(weight):
    real_part = weight[0]
    imag_part = weight[1]
    upper_half = jnp.stack([real_part, imag_part], axis=2)
    lower_half = jnp.stack([-imag_part, real_part], axis=2)
    return jnp.stack([upper_half, lower_half], axis=0)


def fold_pairs(pair_grads):
    return jnp.stack(
        [
            pair_grads[0, :, :, 0] + pair_grads[1, :, :, 1],
            pair_grads[0, :, :, 1] - pair_grads[1, :, :, 0],
        ]
    )


def contract(pattern, left_side, right_side):
    return jnp.einsum(
        pattern, left_side, right_side, precision=highest, preferred_element_type=jnp.float32
    )


def along_rows(spectral, rows_table):
    return contract("rmsxyzc,rxqk->qmskyzc", spectral, rows_table)


def along_cols(spectral, cols_table):
    return contract("rmsxyzc,ryqk->qmsxkzc", spectral, cols_table)


def back_rows(spectral, rows_table):
    return contract("qmskyzc,rxqk->rmsxyzc", spectral, rows_table)


def back_cols(spectral, cols_table):
    return contract("qmsxkzc,ryqk->rmsxyzc", spectral, cols_table)


def back_depth(spectral, depth_table):
    return contract("qmsxykc,zqk->msxyzc", spectral, depth_table)


def to_spectrum(fields, depth_table, rows_table, cols_table):
    spectral = contract("msxyzc,zqk->qmsxykc", fields, depth_table)
    spectral = along_cols(
        lax.all_to_all(spectral, "py", split_axis=5, concat_axis=4, tiled=True),
        cols_table=cols_table,
    )
    spectral = along_rows(
        lax.all_to_all(spectral, "px", split_axis=4, concat_axis=3, tiled=True),
        rows_table=rows_table,
    )
    return spectral


def to_field(spectral, depth_table, rows_table, cols_table):
    spectral = back_rows(spectral, rows_table)
    spectral = back_cols(
        lax.all_to_all(spectral, "px", split_axis=3, concat_axis=4, tiled=True),
        cols_table=cols_table,
    )
    result = back_depth(
        lax.all_to_all(spectral, "py", split_axis=4, concat_axis=5, tiled=True),
        depth_table=depth_table,
    )
    return result


def mix_forward(flat_in, first_table, first_bias, second_table, second_bias):
    pre_one = contract("rfbi,rbiqo->qfbo", flat_in, first_table) + first_bias[:, None]
    outer_one, gelu_back = jax.vjp(jax.nn.gelu, pre_one)
    pre_two = contract("rfbi,rbiqo->qfbo", outer_one, second_table) + second_bias[:, None]
    return (outer_one, gelu_back, pre_two)


def shards(state_field, cotangent, first_weight, first_bias, second_weight, second_bias):
    depth_table = complex_table(NZ, KZ)[0]
    rows_table = complex_table(NX, NX)
    cols_table = complex_table(NY, NY)
    full_first = pair_table(first_weight)
    full_second = pair_table(second_weight)
    group_count = NB
    kz_block = lax.axis_index("py")
    kz_local = KZ // lax.axis_size("py")
    kz_global = kz_block * kz_local + jnp.arange(kz_local, dtype=jnp.int32)
    spectral_in = to_spectrum(state_field[None], depth_table, rows_table, cols_table)
    flat_in = spectral_in.reshape(2, -1, group_count, BS)
    outer_one, gelu_back, pre_two = mix_forward(
        flat_in, full_first, first_bias, full_second, second_bias
    )
    raw_gradient = to_spectrum(cotangent[None], depth_table, rows_table, cols_table)
    shape_full = spectral_in.shape
    doubling = jnp.where(kz_global == 0, 1.0, 2.0).astype(jnp.float32)[:, None]
    gradient_in = (raw_gradient * doubling).reshape(2, -1, group_count, BS)
    grad_two = gradient_in * jnp.tanh(pre_two / shrink_level) ** 2
    table_two = contract("rfbi,qfbo->rbiqo", outer_one, grad_two)
    grad_outer = contract("qfbo,rbiqo->rfbi", grad_two, full_second)
    grad_one = gelu_back(grad_outer)[0]
    table_one = contract("rfbi,qfbo->rbiqo", flat_in, grad_one)
    grad_spec = contract("qfbo,rbiqo->rfbi", grad_one, full_first)
    bias_one = jnp.sum(grad_one, axis=1)
    bias_two = jnp.sum(grad_two, axis=1)
    total_freq = state_field.shape[0] * lax.axis_size("dp") * NX * NY * KZ
    norm_factor = 1.0 / math.sqrt(total_freq)
    sums = lax.psum(
        (
            fold_pairs(table_one) * norm_factor,
            bias_one * norm_factor,
            fold_pairs(table_two) * norm_factor,
            bias_two * norm_factor,
        ),
        ("dp", "px", "py"),
    )
    spatial = to_field(grad_spec.reshape(shape_full), depth_table, rows_table, cols_table)[0]
    state_grad = (cotangent.astype(jnp.float32) + spatial).astype(jnp.bfloat16)
    return (state_grad, sums[0], sums[1], sums[2], sums[3])


def solution(mesh):
    in_specs = (
        P("dp", "px", "py", None, None),
        P("dp", "px", "py", None, None),
        P(),
        P(),
        P(),
        P(),
    )
    out_specs = (P("dp", "px", "py", None, None), P(), P(), P(), P())
    return jax.shard_map(shards, mesh=mesh, in_specs=in_specs, out_specs=out_specs, check_vma=False)
```

profile of v0, /device:TPU:1, one launch (start us, length us, event | category | flops | bytes accessed | tf_op | source)
XLA Modules:
  0.0 701.6 jit_solution(8513858912271601004)
XLA Ops:
  12.8 9.0 %all-to-all-start = ((f32[2,1,1,8,8,16,384]{6,4,3,0,2,1,5:T(8,128)}), f32[2,1,1,8,8,16,384]{6,4,3,0,2,1,5:T(8,128)}, u32[]{:S(2)}, u32[]{:S(2)}) async-start(f32[2,1,1,8,8,16,384]{6,4,3,0,2,1,5:T(8,128)} %copy.73), calls=%async_computation | async-start | bytes 6291456 | tf_op jit(solution)/shard_map/all_to_all | solution.py:78
  25.9 70.3 %all-to-all-done = f32[2,1,1,8,8,16,384]{6,4,3,0,2,1,5:T(8,128)} async-done(((f32[2,1,1,8,8,16,384]{6,4,3,0,2,1,5:T(8,128)}), f32[2,1,1,8,8,16,384]{6,4,3,0,2,1,5:T(8,128)}, u32[]{:S(2)}, u32[]{:S(2)}) %all-to-all-start) | async-done | bytes 3145760 | tf_op jit(solution)/shard_map/all_to_all | solution.py:78
  96.2 3.6 all-to-all-start.2
  100.2 4.9 fusion.46
  105.1 4.2 copy.75
  109.3 60.7 %all-to-all-done.2 = f32[2,1,1,8,8,16,384]{6,4,3,0,2,1,5:T(8,128)S(1)} async-done(((f32[2,1,1,8,8,16,384]{6,4,3,0,2,1,5:T(8,128)}), f32[2,1,1,8,8,16,384]{6,4,3,0,2,1,5:T(8,128)S(1)}, u32[]{:S(2)}, u32[]{:S(2)}) %all-to-all-start.2) | async-done | bytes 3145760 | tf_op jit(solution)/shard_map/all_to_all | solution.py:78
  169.9 16.6 %all-to-all-start.1 = ((f32[2,1,1,8,64,2,384]{6,5,3,0,2,1,4:T(2,128)}), f32[2,1,1,8,64,2,384]{6,5,3,0,2,1,4:T(2,128)}, u32[]{:S(2)}, u32[]{:S(2)}) async-start(f32[2,1,1,8,64,2,384]{6,5,3,0,2,1,4:T(2,128)} %copy.75), calls=%async_computation.1 | async-start | bytes 6291456 | tf_op jit(solution)/shard_map/all_to_all | solution.py:82
  189.5 4.1 copy.80
  193.6 34.4 %all-to-all-done.1 = f32[2,1,1,8,64,2,384]{6,5,3,0,2,1,4:T(2,128)} async-done(((f32[2,1,1,8,64,2,384]{6,5,3,0,2,1,4:T(2,128)}), f32[2,1,1,8,64,2,384]{6,5,3,0,2,1,4:T(2,128)}, u32[]{:S(2)}, u32[]{:S(2)}) %all-to-all-start.1) | async-done | bytes 3145760 | tf_op jit(solution)/shard_map/all_to_all | solution.py:82
  228.0 4.5 all-to-all-start.3
  236.1 4.9 bitcast_multiply_fusion.2
  243.5 6.5 reshape.325
  250.0 5.3 copy.86
  255.2 20.2 %all-to-all-done.3 = f32[2,1,1,8,64,2,384]{6,5,3,0,2,1,4:T(2,128)} async-done(((f32[2,1,1,8,64,2,384]{6,5,3,0,2,1,4:T(2,128)}), f32[2,1,1,8,64,2,384]{6,5,3,0,2,1,4:T(2,128)}, u32[]{:S(2)}, u32[]{:S(2)}) %all-to-all-start.3) | async-done | bytes 3145760 | tf_op jit(solution)/shard_map/all_to_all | solution.py:82
  275.5 4.9 fusion.54
  282.8 6.5 transpose.54
  292.9 4.1 fusion.78
  297.0 5.9 fusion.125
  303.0 6.0 fusion.124
  310.7 4.6 fusion.62
  315.3 5.0 copy.89
  320.3 7.5 %reshape.329 = f32[2,64,8,2,384]{4,3,2,1,0:T(2,128)} reshape(f32[2,1024,4,96]{3,2,1,0:T(4,128)} %copy.89) | data formatting | bytes 6291456 | tf_op jit(solution)/shard_map/reshape.22
  327.8 5.6 fusion.43
  335.8 38.5 %all_to_all.90 = f32[2,1,1,64,8,2,384]{6,5,4,0,2,1,3:T(2,128)S(1)} all-to-all(f32[2,1,1,64,8,2,384]{6,5,4,0,2,1,3:T(2,128)S(1)} %copy.92), channel_id=1, replica_groups=mesh['dp'=4,'px'=8,'py'=8] {'px'}, dimensions={3} | all-to-all | bytes 6291456 | tf_op jit(solution)/shard_map/all_to_all | solution.py:91
  377.3 4.0 copy.95
  381.3 11.1 %all-to-all-start.5 = ((f32[2,1,1,8,64,2,384]{6,5,3,0,2,1,4:T(2,128)}), f32[2,1,1,8,64,2,384]{6,5,3,0,2,1,4:T(2,128)}, u32[]{:S(2)}, u32[]{:S(2)}) async-start(f32[2,1,1,8,64,2,384]{6,5,3,0,2,1,4:T(2,128)} %copy.95), calls=%async_computation.5 | async-start | bytes 6291456 | tf_op jit(solution)/shard_map/all_to_all | solution.py:95
  392.7 7.8 %fusion.69 = f32[2,4,96,2,96]{2,4,1,3,0:T(8,128)S(1)} fusion(f32[2,4,96]{2,0,1:T(2,128)S(1)} %copy-done.23, f32[4,2,96,1024,1]{3,2,4,1,0:T(8,128)} %copy-done.14, f32[2,1024,4,96]{1,3,0,2:T(8,128)} %copy-done.27), kind=kOutput, calls=%fused_computation.63 | convolution fusion | flops 1819017216 | bytes 6884352 | tf_op jit(solution)/shard_map/rfbi,qfbo->rbiqo/dot_general | solution.py:50
  405.9 102.9 %all-reduce = (f32[2,4,96]{2,0,1:T(2,128)S(1)}, f32[2,4,96]{2,0,1:T(2,128)S(1)}) all-reduce(f32[2,4,96]{2,0,1:T(2,128)S(1)} %broadcast_multiply_fusion.1, f32[2,4,96]{2,0,1:T(2,128)S(1)} %broadcast_multiply_fusion), channel_id=1, replica_groups=mesh['dp'=4,'px'=8,'py'=8] {'dp','px','py'}, use_global_device_ids=true, to_apply=%region_2.3 | all-reduce | flops 1536 | bytes 12288 | tf_op jit(solution)/shard_map/psum | solution.py:137
  509.9 164.5 %all-reduce.4.cloned.1.call-done = (f32[2,4,96,96]{2,3,1,0:T(8,128)}, f32[2,4,96,96]{2,3,1,0:T(8,128)}) async-done(((f32[2,4,96,96]{2,3,1,0:T(8,128)}, f32[2,4,96,96]{2,3,1,0:T(8,128)}), (f32[2,4,96,96]{2,3,1,0:T(8,128)}, f32[2,4,96,96]{2,3,1,0:T(8,128)})) %all-reduce.4.cloned.1.call-update) | async-done | bytes 589840 | tf_op jit(solution)/shard_map/psum | solution.py:137
  678.2 5.3 copy.197
  683.6 5.4 reshape.331
  689.0 5.3 fusion.15
  (98 shorter events, 42.7 us)
Async XLA Ops:
  7.2 14.7 %copy-start = (bf16[1,8,8,32,384]{4,3,2,1,0:T(8,128)(2,1)S(1)}, bf16[1,8,8,32,384]{4,3,2,1,0:T(8,128)(2,1)}, u32[]{:S(2)}) copy-start(bf16[1,8,8,32,384]{4,3,2,1,0:T(8,128)(2,1)} %param.6) | copy-start | bytes 4718596
  12.8 83.4 %all-to-all-start = ((f32[2,1,1,8,8,16,384]{6,4,3,0,2,1,5:T(8,128)}), f32[2,1,1,8,8,16,384]{6,4,3,0,2,1,5:T(8,128)}, u32[]{:S(2)}, u32[]{:S(2)}) async-start(f32[2,1,1,8,8,16,384]{6,4,3,0,2,1,5:T(8,128)} %copy.73), calls=%async_computation | async-start | bytes 6291456 | tf_op jit(solution)/shard_map/all_to_all | solution.py:78
  96.2 73.7 %all-to-all-start.2 = ((f32[2,1,1,8,8,16,384]{6,4,3,0,2,1,5:T(8,128)}), f32[2,1,1,8,8,16,384]{6,4,3,0,2,1,5:T(8,128)S(1)}, u32[]{:S(2)}, u32[]{:S(2)}) async-start(f32[2,1,1,8,8,16,384]{6,4,3,0,2,1,5:T(8,128)} %copy.78), calls=%async_computation.2 | async-start | bytes 6291456 | tf_op jit(solution)/shard_map/all_to_all | solution.py:78
  100.2 86.3 %copy-start.6 = (f32[1,64,2,64]{1,3,0,2:T(8,128)}, f32[1,64,2,64]{1,3,0,2:T(8,128)S(1)}, u32[]{:S(2)}) copy-start(f32[1,64,2,64]{1,3,0,2:T(8,128)S(1)} %get-tuple-element.34) | copy-start | bytes 98308
  100.2 86.3 %copy-start.10 = (f32[1,64,2,64]{1,3,0,2:T(8,128)}, f32[1,64,2,64]{1,3,0,2:T(8,128)S(1)}, u32[]{:S(2)}) copy-start(f32[1,64,2,64]{1,3,0,2:T(8,128)S(1)} %get-tuple-element.35) | copy-start | bytes 98308
  169.9 58.1 %all-to-all-start.1 = ((f32[2,1,1,8,64,2,384]{6,5,3,0,2,1,4:T(2,128)}), f32[2,1,1,8,64,2,384]{6,5,3,0,2,1,4:T(2,128)}, u32[]{:S(2)}, u32[]{:S(2)}) async-start(f32[2,1,1,8,64,2,384]{6,5,3,0,2,1,4:T(2,128)} %copy.75), calls=%async_computation.1 | async-start | bytes 6291456 | tf_op jit(solution)/shard_map/all_to_all | solution.py:82
  193.6 38.9 %copy-start.20 = (f32[2,4,96]{2,1,0:T(4,128)S(1)}, f32[2,4,96]{2,1,0:T(4,128)}, u32[]{:S(2)}) copy-start(f32[2,4,96]{2,1,0:T(4,128)} %param.9) | copy-start | bytes 9220
  193.6 39.5 %copy-start.21 = (f32[2,4,96]{2,1,0:T(4,128)S(1)}, f32[2,4,96]{2,1,0:T(4,128)}, u32[]{:S(2)}) copy-start(f32[2,4,96]{2,1,0:T(4,128)} %param.11) | copy-start | bytes 9220
  193.6 40.1 %copy-start.16 = (f32[2,4,96,96]{3,2,1,0:T(8,128)S(1)}, f32[2,4,96,96]{3,2,1,0:T(8,128)}, u32[]{:S(2)}) copy-start(f32[2,4,96,96]{3,2,1,0:T(8,128)} %param.8) | copy-start | bytes 884740
  193.6 40.4 %copy-start.17 = (f32[2,4,96,96]{3,2,1,0:T(8,128)S(1)}, f32[2,4,96,96]{3,2,1,0:T(8,128)}, u32[]{:S(2)}) copy-start(f32[2,4,96,96]{3,2,1,0:T(8,128)} %param.10) | copy-start | bytes 884740
  228.0 47.4 %all-to-all-start.3 = ((f32[2,1,1,8,64,2,384]{6,5,3,0,2,1,4:T(2,128)}), f32[2,1,1,8,64,2,384]{6,5,3,0,2,1,4:T(2,128)}, u32[]{:S(2)}, u32[]{:S(2)}) async-start(f32[2,1,1,8,64,2,384]{6,5,3,0,2,1,4:T(2,128)} %copy.80), calls=%async_computation.3 | async-start | bytes 6291456 | tf_op jit(solution)/shard_map/all_to_all | solution.py:82
  233.8 2.4 copy-start.7
  250.0 25.5 %copy-start.8 = (f32[1,64,2,64]{1,3,0,2:T(8,128)S(1)}, f32[1,64,2,64]{1,3,0,2:T(8,128)}, u32[]{:S(2)}) copy-start(f32[1,64,2,64]{1,3,0,2:T(8,128)} %copy-done.6) | copy-start | bytes 98308
  250.0 25.5 %copy-start.12 = (f32[1,64,2,64]{1,3,0,2:T(8,128)S(1)}, f32[1,64,2,64]{1,3,0,2:T(8,128)}, u32[]{:S(2)}) copy-start(f32[1,64,2,64]{1,3,0,2:T(8,128)} %copy-done.10) | copy-start | bytes 98308
  292.8 4.2 copy-start.15
  292.8 4.2 copy-start.18
  292.8 4.2 copy-start.19
  292.8 4.2 copy-start.22
  292.9 4.2 copy-start.26
  297.0 6.0 copy-start.14
  303.0 6.0 copy-start.27
  303.0 7.8 %copy-start.5 = (f32[1,4,96,2,96]{2,4,0,3,1:T(8,128)S(1)}, f32[1,4,96,2,96]{2,4,0,3,1:T(8,128)}, u32[]{:S(2)}) copy-start(f32[1,4,96,2,96]{2,4,0,3,1:T(8,128)} %get-tuple-element.33) | copy-start | bytes 884740
  320.3 7.5 %copy-start.9 = (f32[1,64,2,64]{1,3,0,2:T(8,128)S(1)}, f32[1,64,2,64]{1,3,0,2:T(8,128)}, u32[]{:S(2)}) copy-start(f32[1,64,2,64]{1,3,0,2:T(8,128)} %copy-done.6) | copy-start | bytes 98308
  320.3 7.5 %copy-start.13 = (f32[1,64,2,64]{1,3,0,2:T(8,128)S(1)}, f32[1,64,2,64]{1,3,0,2:T(8,128)}, u32[]{:S(2)}) copy-start(f32[1,64,2,64]{1,3,0,2:T(8,128)} %copy-done.10) | copy-start | bytes 98308
  381.3 11.4 %copy-start.23 = (f32[2,4,96]{2,0,1:T(2,128)S(1)}, f32[2,4,96]{2,0,1:T(2,128)}, u32[]{:S(2)}) copy-start(f32[2,4,96]{2,0,1:T(2,128)} %copy.84) | copy-start | bytes 9220
  381.3 296.9 %all-to-all-start.5 = ((f32[2,1,1,8,64,2,384]{6,5,3,0,2,1,4:T(2,128)}), f32[2,1,1,8,64,2,384]{6,5,3,0,2,1,4:T(2,128)}, u32[]{:S(2)}, u32[]{:S(2)}) async-start(f32[2,1,1,8,64,2,384]{6,5,3,0,2,1,4:T(2,128)} %copy.95), calls=%async_computation.5 | async-start | bytes 6291456 | tf_op jit(solution)/shard_map/all_to_all | solution.py:95
  392.4 282.0 %all-reduce.4.cloned.1.call-start = ((), (), s32[]{:S(2)}) async-start(), calls=%async_computation.6 | async-start | bytes 1572864 | tf_op jit(solution)/shard_map/psum | solution.py:137
  392.7 8.6 %copy-start.3 = (f32[2,1024,4,96]{1,3,0,2:T(8,128)S(1)}, f32[2,1024,4,96]{1,3,0,2:T(8,128)}, u32[]{:S(2)}) copy-start(f32[2,1024,4,96]{1,3,0,2:T(8,128)} %copy-done.2) | copy-start | bytes 9437188
  401.3 4.5 copy-start.24
  401.3 4.5 copy-start.25
  683.6 5.5 copy-start.4
  683.6 10.7 %copy-start.1 = (bf16[1,8,8,32,384]{4,3,2,1,0:T(8,128)(2,1)S(1)}, bf16[1,8,8,32,384]{4,3,2,1,0:T(8,128)(2,1)}, u32[]{:S(2)}) copy-start(bf16[1,8,8,32,384]{4,3,2,1,0:T(8,128)(2,1)} %param.6) | copy-start | bytes 4718596
  (2 other events, 4.1 us)
Sparse Core Ops, SparseCore 0:
  405.9 268.4 all-reduce.3
where the time goes:
time: 711 us; the launch traced here: 702 us
  waiting for transfers between devices  350 us (49%)
  blocking collectives  141 us (20%)
  local copies, waits for them, and re-layouts  78.4 us (11%)
  matrix products  67.7 us (10%)
  starting transfers between devices  45.1 us (6%)
  between operations  15 us (2%)
    psum x1, waiting for transfers between devices, shards(): lax.psum((fold_pairs(table_one) * norm_factor, bias_one * norm_factor, fo...  164 us
    all_to_all x2, waiting for transfers between devices, to_spectrum(): lax.all_to_all(spectral, 'py', split_axis=5, concat_axis=4, tiled=True)  131 us
    psum x1, blocking collectives, shards(): lax.psum((fold_pairs(table_one) * norm_factor, bias_one * norm_factor, fo...  103 us
    dot_general x15, matrix products, contract(): jnp.einsum(pattern, left_side, right_side, precision=highest, preferred_e...  67.7 us
    all_to_all x2, waiting for transfers between devices, to_spectrum(): lax.all_to_all(spectral, 'px', split_axis=4, concat_axis=3, tiled=True)  54.7 us
    all_to_all x1, blocking collectives, to_field(): lax.all_to_all(spectral, 'px', split_axis=3, concat_axis=4, tiled=True)  38.5 us
    transpose x7, local copies, waits for them, and re-layouts, contract(): jnp.einsum(pattern, left_side, right_side, precision=highest, preferred_e...  25 us
    all_to_all x2, starting transfers between devices, to_spectrum(): lax.all_to_all(spectral, 'px', split_axis=4, concat_axis=3, tiled=True)  21.1 us
  transfers between devices with their start and end apart: 6, of which 5 were waited for; matrix products, arithmetic and copies ran while one was open for 9% of the time, Pallas kernels for 0%

commit v1 on v0

v1 whole, which is shorter than its diff:
```python
import math

import jax
import jax.numpy as jnp
import ml_dtypes
import numpy as np
from jax import lax
from jax.experimental import pallas as pl
from jax.experimental.pallas import tpu as pltpu
from jax.sharding import PartitionSpec as P

NX = 64
NY = 64
NZ = 32
NB = 4
BS = 96
KZ = 16
C = 384
HALF = BS // 2
CELLS = 64
GROUPS = 16
WIDE = 256
PIECE = 640
SHRINK = 0.25
f32 = jnp.float32
bf16 = jnp.bfloat16
BIG = pltpu.CompilerParams(vmem_limit_bytes=56 * 1024 * 1024)
SPECTRAL = jax.ShapeDtypeStruct((64, 2, HALF, 128), f32)
GROUPED = jax.ShapeDtypeStruct((GROUPS, 2 * BS, WIDE), f32)


def np_split(table):
    high = table.astype(np.float32).astype(ml_dtypes.bfloat16)
    low = (table - high.astype(np.float64)).astype(np.float32).astype(ml_dtypes.bfloat16)
    return high, low


def depth_tables():
    k = np.arange(KZ)[:, None]
    z = np.arange(NZ)[None, :]
    angle = 2.0 * np.pi * (k * z % NZ) / NZ
    scale = 1.0 / math.sqrt(NX * NY * NZ)
    pair = np.stack([np.cos(angle), -np.sin(angle)], axis=1) * scale
    eye = np.eye(8)
    forward = np.einsum("kqz,ab->kqabz", pair, eye).reshape(256, 256)
    return np_split(forward), np_split(forward.T.copy())


def plane_tables():
    j = np.arange(8)
    eight = np.exp(-2j * np.pi * np.outer(j, j) / 8.0)
    both = np.einsum("xk,yl->xykl", eight, eight).reshape(64, 64)
    real = np.zeros((2, 64, 2, 64))
    real[0, :, 0] = both.real
    real[0, :, 1] = both.imag
    real[1, :, 0] = -both.imag
    real[1, :, 1] = both.real
    eye = np.eye(2)
    forward = np.einsum("qxpf,kl,cd->kqcxpdlf", real, eye, eye).reshape(512, 512)
    return np_split(forward), np_split(forward.T.copy())


def twiddle_table():
    k2 = np.arange(8)
    j = np.arange(8)
    one = np.exp(-2j * np.pi * np.outer(k2, j) / 64.0)
    both = np.einsum("kx,ly->klxy", one, one).reshape(64, 64)
    both = np.tile(both, (1, 2))
    return np.stack([both.real, both.imag], axis=1).astype(np.float32)


def split(value):
    high = value.astype(bf16)
    low = (value - high.astype(f32)).astype(bf16)
    return high, low


def dot(left, right, dims=((1,), (0,))):
    return lax.dot_general(left, right, (dims, ((), ())), preferred_element_type=f32)


def dot3(left, right, dims=((1,), (0,))):
    return (
        dot(left[0], right[0], dims) + dot(left[0], right[1], dims) + dot(left[1], right[0], dims)
    )


def fft(re, im, sign):
    n = len(re)
    if n == 1:
        return re, im
    even_re, even_im = fft(re[0::2], im[0::2], sign)
    odd_re, odd_im = fft(re[1::2], im[1::2], sign)
    out_re = [None] * n
    out_im = [None] * n
    root = math.sqrt(0.5)
    for k in range(n // 2):
        a, b = odd_re[k], odd_im[k]
        turn = k * (8 // n)
        if turn == 1:
            a, b = (a - sign * b) * root, (b + sign * a) * root
        elif turn == 2:
            a, b = -sign * b, sign * a
        elif turn == 3:
            a, b = (-a - sign * b) * root, (-b + sign * a) * root
        out_re[k], out_im[k] = even_re[k] + a, even_im[k] + b
        out_re[k + n // 2], out_im[k + n // 2] = even_re[k] - a, even_im[k] - b
    return out_re, out_im


def plane_stage_one(src_ref, dst_ref, sign):
    def body(p, carry):
        for tile in range(HALF // 8):
            rows = slice(tile * 8, tile * 8 + 8)
            re = [src_ref[p * 8 + n, 0, rows, :] for n in range(8)]
            im = [src_ref[p * 8 + n, 1, rows, :] for n in range(8)]
            re, im = fft(re, im, sign)
            for n in range(8):
                dst_ref[p * 8 + n, 0, rows, :] = re[n]
                dst_ref[p * 8 + n, 1, rows, :] = im[n]
        return carry

    lax.fori_loop(0, 8, body, 0)


def plane_forward(src_ref, work_ref, twiddle_ref):
    plane_stage_one(src_ref, work_ref, -1.0)

    def body(p, carry):
        for tile in range(HALF // 8):
            rows = slice(tile * 8, tile * 8 + 8)
            re = [work_ref[n * 8 + p, 0, rows, :] for n in range(8)]
            im = [work_ref[n * 8 + p, 1, rows, :] for n in range(8)]
            re, im = fft(re, im, -1.0)
            for n in range(8):
                c = twiddle_ref[n * 8 + p, 0:1, :]
                s = twiddle_ref[n * 8 + p, 1:2, :]
                work_ref[n * 8 + p, 0, rows, :] = re[n] * c - im[n] * s
                work_ref[n * 8 + p, 1, rows, :] = re[n] * s + im[n] * c
        return carry

    lax.fori_loop(0, 8, body, 0)


def plane_backward(work_ref, out_ref, twiddle_ref):
    def body(p, carry):
        for tile in range(HALF // 8):
            rows = slice(tile * 8, tile * 8 + 8)
            re = []
            im = []
            for n in range(8):
                c = twiddle_ref[n * 8 + p, 0:1, :]
                s = twiddle_ref[n * 8 + p, 1:2, :]
                a = work_ref[n * 8 + p, 0, rows, :]
                b = work_ref[n * 8 + p, 1, rows, :]
                re.append(a * c + b * s)
                im.append(b * c - a * s)
            re, im = fft(re, im, 1.0)
            for n in range(8):
                work_ref[n * 8 + p, 0, rows, :] = re[n]
                work_ref[n * 8 + p, 1, rows, :] = im[n]
        return carry

    lax.fori_loop(0, 8, body, 0)
    plane_stage_one(work_ref, out_ref, 1.0)


def load_group(work_ref, group, high_ref, low_ref):
    rows = []
    for pair in range(2):
        rows.append(
            jnp.concatenate(
                [work_ref[group * 4 + pair * 2 + n // 2, n % 2] for n in range(4)], axis=1
            )
        )
    values = dot3(split(jnp.concatenate(rows, axis=0)), (high_ref[...], low_ref[...]))
    halves = []
    for pair in range(2):
        part = values[pair * HALF : (pair + 1) * HALF]
        halves.append(
            jnp.concatenate([part[:, n * 128 : (n + 1) * 128] for n in range(4)], axis=0)
        )
    return jnp.concatenate(halves, axis=1)


def store_group(work_ref, group, spectral, high_ref, low_ref):
    rows = []
    for pair in range(2):
        part = spectral[:, pair * 128 : (pair + 1) * 128]
        rows.append(
            jnp.concatenate([part[n * HALF : (n + 1) * HALF] for n in range(4)], axis=1)
        )
    values = dot3(split(jnp.concatenate(rows, axis=0)), (high_ref[...], low_ref[...]))
    for pair in range(2):
        for n in range(4):
            work_ref[group * 4 + pair * 2 + n // 2, n % 2] = values[
                pair * HALF : (pair + 1) * HALF, n * 128 : (n + 1) * 128
            ]


def depth_kernel(field_ref, high_ref, low_ref, out_ref, work_ref):
    for g in range(8):
        rows = field_ref[g * 256 : (g + 1) * 256, :]
        values = dot(high_ref[...], rows) + dot(low_ref[...], rows)
        work_ref[:, g * 8 : (g + 1) * 8, :] = values.reshape(2 * KZ, 8, C)

    def body(k, carry):
        values = work_ref[pl.ds(2 * k, 2)].reshape(2 * CELLS, C).T
        lane = lax.broadcasted_iota(jnp.int32, (HALF, 128), 1)
        for b in range(NB):
            upper = values[b * BS : b * BS + HALF]
            lower = values[b * BS + HALF : (b + 1) * BS]
            out_ref[b * KZ + k, 0] = jnp.where(lane < 64, upper, pltpu.roll(lower, 64, 1))
            out_ref[b * KZ + k, 1] = jnp.where(lane < 64, pltpu.roll(upper, 64, 1), lower)
        return carry

    lax.fori_loop(0, KZ, body, 0)


def forward_kernel(
    doubling_ref, src_ref, twiddle_ref, th_ref, tl_ref, w1h, w1l, b1, w2h, w2l, b2,
    spec_ref, outer_ref, slope_ref, square_ref, work_ref,
):
    plane_forward(src_ref, work_ref, twiddle_ref)
    root = math.sqrt(2.0 / math.pi)

    def body(g, carry):
        spectral = load_group(work_ref, g, th_ref, tl_ref)
        spec_ref[g] = spectral
        pre = dot3((w1h[...], w1l[...]), split(spectral)) + b1[...]
        pre_sq = pre * pre
        t = jnp.tanh(root * (pre + 0.044715 * (pre * pre_sq)))
        outer = 0.5 * pre * (1.0 + t)
        outer_ref[g] = outer
        slope_ref[g] = 0.5 * (1.0 + t) + 0.5 * pre * (1.0 - t * t) * (
            root * (1.0 + 3.0 * 0.044715 * pre_sq)
        )
        pre_two = dot3((w2h[...], w2l[...]), split(outer)) + b2[...]
        t2 = jnp.tanh(pre_two * (1.0 / SHRINK))
        square_ref[g] = t2 * t2 * doubling_ref[0, 0]
        return carry

    lax.fori_loop(0, GROUPS, body, 0)


def backward_kernel(
    src_ref, twiddle_ref, th_ref, tl_ref, bh_ref, bl_ref, w1h, w1l, w2h, w2l, slope_ref, square_ref,
    two_ref, one_ref, out_ref, work_ref,
):
    plane_forward(src_ref, work_ref, twiddle_ref)

    def body(g, carry):
        grad_two = load_group(work_ref, g, th_ref, tl_ref) * square_ref[g]
        two_ref[g] = grad_two
        grad_one = dot3((w2h[...], w2l[...]), split(grad_two)) * slope_ref[g]
        one_ref[g] = grad_one
        grad_spec = dot3((w1h[...], w1l[...]), split(grad_one))
        store_group(work_ref, g, grad_spec, bh_ref, bl_ref)
        return carry

    lax.fori_loop(0, GROUPS, body, 0)
    plane_backward(work_ref, out_ref, twiddle_ref)


def table_kernel(spec_ref, outer_ref, one_ref, two_ref, t1_ref, b1_ref, t2_ref, b2_ref):
    lanes = ((1,), (1,))
    shape = (2 * BS, 2 * BS)

    def body(g, carry):
        t1, s1, t2, s2 = carry
        one = one_ref[g]
        two = two_ref[g]
        t1 = t1 + dot3(split(spec_ref[g]), split(one), lanes)
        t2 = t2 + dot3(split(outer_ref[g]), split(two), lanes)
        return t1, s1 + one, t2, s2 + two

    zero = jnp.zeros(shape, f32)
    wide = jnp.zeros((2 * BS, WIDE), f32)
    t1, s1, t2, s2 = lax.fori_loop(0, GROUPS, body, (zero, wide, zero, wide))
    t1_ref[...] = t1
    t2_ref[...] = t2
    b1_ref[...] = jnp.sum(s1, axis=1, keepdims=True)
    b2_ref[...] = jnp.sum(s2, axis=1, keepdims=True)


def field_kernel(src_ref, cotangent_ref, high_ref, low_ref, out_ref, work_ref):
    def body(k, carry):
        lane = lax.broadcasted_iota(jnp.int32, (HALF, 128), 1)
        parts = []
        for b in range(NB):
            re = src_ref[b * KZ + k, 0]
            im = src_ref[b * KZ + k, 1]
            parts.append(jnp.where(lane < 64, re, pltpu.roll(im, 64, 1)))
            parts.append(jnp.where(lane < 64, pltpu.roll(re, 64, 1), im))
        values = jnp.concatenate(parts, axis=0).T
        work_ref[pl.ds(2 * k, 2)] = values.reshape(2, CELLS, C)
        return carry

    lax.fori_loop(0, KZ, body, 0)
    for g in range(8):
        rows = work_ref[:, g * 8 : (g + 1) * 8, :].reshape(256, C)
        values = dot3((high_ref[...], low_ref[...]), split(rows))
        span = slice(g * 256, (g + 1) * 256)
        out_ref[span, :] = (cotangent_ref[span, :].astype(f32) + values).astype(bf16)


def vmem(n):
    return [pl.BlockSpec(memory_space=pltpu.VMEM)] * n


def call(kernel, out_shape, args, scratch, flops, moved):
    outs = len(out_shape) if isinstance(out_shape, tuple) else 1
    return pl.pallas_call(
        kernel,
        out_shape=out_shape,
        in_specs=vmem(len(args)),
        out_specs=tuple(vmem(outs)) if isinstance(out_shape, tuple) else vmem(1)[0],
        scratch_shapes=scratch,
        compiler_params=BIG,
        cost_estimate=pl.CostEstimate(flops=flops, bytes_accessed=moved, transcendentals=0),
    )(*args)


def depth_forward(field, tables):
    return call(
        depth_kernel,
        SPECTRAL,
        (field.reshape(2048, C), *tables),
        [pltpu.VMEM((2 * KZ, CELLS, C), f32)],
        800_000_000,
        5_000_000,
    )


def mixing(weight):
    real = weight[0].T
    imag = weight[1].T
    return jnp.concatenate(
        [jnp.concatenate([real, -imag], axis=1), jnp.concatenate([imag, real], axis=1)], axis=0
    )


def jax_split(value):
    high = lax.reduce_precision(value, 8, 7)
    return high.astype(bf16), (value - high).astype(bf16)


def fold(table):
    return jnp.stack(
        [table[:BS, :BS] + table[BS:, BS:], table[:BS, BS:] - table[BS:, :BS]]
    )


def exchange(value):
    return lax.all_to_all(value, ("px", "py"), split_axis=0, concat_axis=0, tiled=True)


def shards(state_field, cotangent, first_weight, first_bias, second_weight, second_bias):
    depth_fwd, depth_bwd = depth_tables()
    plane_fwd, plane_bwd = plane_tables()
    twiddle = twiddle_table()
    owner = lax.axis_index("px") * 8 + lax.axis_index("py")
    block = owner // KZ
    doubling = jnp.where(owner % KZ == 0, 1.0, 2.0).astype(f32).reshape(1, 1)

    first = mixing(lax.dynamic_index_in_dim(first_weight, block, 1, keepdims=False))
    second = mixing(lax.dynamic_index_in_dim(second_weight, block, 1, keepdims=False))
    bias_one = lax.dynamic_index_in_dim(first_bias, block, 1, keepdims=False).reshape(2 * BS, 1)
    bias_two = lax.dynamic_index_in_dim(second_bias, block, 1, keepdims=False).reshape(2 * BS, 1)

    state_spec = exchange(depth_forward(state_field, depth_fwd))
    cot_spec = exchange(depth_forward(cotangent, depth_fwd))
    spec, outer, slope, square = pl.pallas_call(
        forward_kernel,
        out_shape=(GROUPED,) * 4,
        in_specs=[pl.BlockSpec(memory_space=pltpu.SMEM)] + vmem(10),
        out_specs=tuple(vmem(4)),
        scratch_shapes=[pltpu.VMEM((64, 2, HALF, 128), f32)],
        compiler_params=BIG,
        cost_estimate=pl.CostEstimate(
            flops=8_000_000_000, bytes_accessed=16_000_000, transcendentals=1_500_000
        ),
    )(doubling, state_spec, twiddle, *plane_fwd, *jax_split(first), bias_one, *jax_split(second), bias_two)

    grad_two, grad_one, grad_plane = call(
        backward_kernel,
        (GROUPED, GROUPED, SPECTRAL),
        (cot_spec, twiddle, *plane_fwd, *plane_bwd, *jax_split(first.T), *jax_split(second.T), slope, square),
        [pltpu.VMEM((64, 2, HALF, 128), f32)],
        10_000_000_000,
        20_000_000,
    )
    grad_cells = exchange(grad_plane)

    t1, s1, t2, s2 = call(
        table_kernel,
        (
            jax.ShapeDtypeStruct((2 * BS, 2 * BS), f32),
            jax.ShapeDtypeStruct((2 * BS, 1), f32),
        )
        * 2,
        (spec, outer, grad_one, grad_two),
        [],
        4_000_000_000,
        13_000_000,
    )
    norm = 1.0 / math.sqrt(4 * NX * NY * KZ)
    wide = 2 * BS * BS
    flat = jnp.concatenate(
        [fold(t1).reshape(-1), fold(t2).reshape(-1), s1.reshape(-1), s2.reshape(-1)]
    )
    flat = jnp.pad(flat * norm, (0, 64 * PIECE - flat.shape[0])).reshape(64, 5, 128)
    flat = exchange(flat).reshape(NB, KZ, 5, 128).sum(axis=1)
    flat = lax.all_to_all(flat, "dp", split_axis=0, concat_axis=0, tiled=True).sum(axis=0)
    for axis, size in (("py", 8), ("px", 8), ("dp", 4)):
        flat = jnp.broadcast_to(flat.reshape(1, -1, 128), (size, flat.size // 128, 128))
        flat = lax.all_to_all(flat, axis, split_axis=0, concat_axis=0, tiled=True)
    flat = flat.reshape(NB, 64 * PIECE)
    grads_one = flat[:, :wide].reshape(NB, 2, BS, BS).transpose(1, 0, 2, 3)
    grads_two = flat[:, wide : 2 * wide].reshape(NB, 2, BS, BS).transpose(1, 0, 2, 3)
    biases = flat[:, 2 * wide : 2 * wide + 4 * BS].reshape(NB, 2, 2, BS)

    state_grad = call(
        field_kernel,
        jax.ShapeDtypeStruct((2048, C), bf16),
        (grad_cells, cotangent.reshape(2048, C), *depth_bwd),
        [pltpu.VMEM((2 * KZ, CELLS, C), f32)],
        1_200_000_000,
        7_000_000,
    ).reshape(1, 8, 8, NZ, C)
    return (
        state_grad,
        grads_one,
        biases[:, 0].transpose(1, 0, 2),
        grads_two,
        biases[:, 1].transpose(1, 0, 2),
    )


def solution(mesh):
    in_specs = (
        P("dp", "px", "py", None, None),
        P("dp", "px", "py", None, None),
        P(),
        P(),
        P(),
        P(),
    )
    out_specs = (P("dp", "px", "py", None, None), P(), P(), P(), P())
    return jax.shard_map(shards, mesh=mesh, in_specs=in_specs, out_specs=out_specs, check_vma=False)
```

time: 711 us -> 383 us (0.54)
  waiting for transfers between devices: 350 us -> 157 us
  Pallas kernels: 0 us -> 92.4 us
  blocking collectives: 141 us -> 66.1 us
  matrix products: 67.7 us -> 0 us
  local copies, waits for them, and re-layouts: 78.4 us -> 22.7 us
  starting transfers between devices: 45.1 us -> 30.8 us
  between operations: 15 us -> 0.81 us
    psum x1 -> x0, waiting for transfers between devices: 164 us -> none  [shards(): lax.psum((fold_pairs(table_one) * norm_factor, bias_one * norm_factor, fo...]
    psum x1 -> x0, blocking collectives: 103 us -> none  [shards(): lax.psum((fold_pairs(table_one) * norm_factor, bias_one * norm_factor, fo...]
    pallas_call x0 -> x6, Pallas kernels: none -> 92.4 us  [the longest x5 68 us: call(): pl.pallas_call(kernel, out_shape=out_shape, in_specs=vmem(len(args)), out...]
    dot_general x15 -> x0, matrix products: 67.7 us -> none  [contract(): jnp.einsum(pattern, left_side, right_side, precision=highest, preferred_e...]
    transpose x9 -> x2, local copies, waits for them, and re-layouts: 35 us -> 0.84 us  [the longest x1 0.83 us: mixing(): real = weight[0].T]
    all_to_all x5 -> x3, waiting for transfers between devices: 186 us -> 157 us  [exchange(): lax.all_to_all(value, ('px', 'py'), split_axis=0, concat_axis=0, tiled=True)]
    all_to_all x1 -> x5, blocking collectives: 38.5 us -> 66.1 us  [the longest x3 34.5 us: shards(): flat = lax.all_to_all(flat, axis, split_axis=0, concat_axis=0, tiled=True)]
    all_to_all x5 -> x3, starting transfers between devices: 44.8 us -> 30.8 us  [exchange(): lax.all_to_all(value, ('px', 'py'), split_axis=0, concat_axis=0, tiled=True)]
  transfers between devices with their start and end apart: 6 -> 3, of which waited for: 5 -> 3; matrix products, arithmetic and copies ran while one was open for 9% -> 5% of each run, Pallas kernels for 0% -> 9%
where the time goes in v1:
time: 383 us; the launch traced here: 378 us
  waiting for transfers between devices  157 us (41%)
  Pallas kernels  92.4 us (24%)
  blocking collectives  66.1 us (17%)
  starting transfers between devices  30.8 us (8%)
  local copies, waits for them, and re-layouts  22.7 us (6%)
  other arithmetic  8.16 us (2%)
    all_to_all x3, waiting for transfers between devices, exchange(): lax.all_to_all(value, ('px', 'py'), split_axis=0, concat_axis=0, tiled=True)  157 us
    pallas_call x5, Pallas kernels, call(): pl.pallas_call(kernel, out_shape=out_shape, in_specs=vmem(len(args)), out...  68 us
    all_to_all x3, blocking collectives, shards(): flat = lax.all_to_all(flat, axis, split_axis=0, concat_axis=0, tiled=True)  34.5 us
    all_to_all x3, starting transfers between devices, exchange(): lax.all_to_all(value, ('px', 'py'), split_axis=0, concat_axis=0, tiled=True)  30.8 us
    pallas_call x1, Pallas kernels, shards(): pl.pallas_call(forward_kernel, out_shape=(GROUPED,) * 4, in_specs=[pl.Blo...  24.4 us
    all_to_all x1, blocking collectives, exchange(): lax.all_to_all(value, ('px', 'py'), split_axis=0, concat_axis=0, tiled=True)  22.5 us
    unnamed x13, local copies, waits for them, and re-layouts  10.1 us
    all_to_all x1, blocking collectives, shards(): lax.all_to_all(flat, 'dp', split_axis=0, concat_axis=0, tiled=True)  9.08 us
  transfers between devices with their start and end apart: 3, of which 3 were waited for; matrix products, arithmetic and copies ran while one was open for 5% of the time, Pallas kernels for 9%

profile of v1, /device:TPU:1, one launch (start us, length us, event | category | flops | bytes accessed | tf_op | source)
XLA Modules:
  0.0 377.8 jit_solution(11075087088508560422)
XLA Ops:
  0.6 8.0 %shard_map.183 = f32[64,2,48,128]{3,2,1,0:T(8,128)} custom-call(bf16[2048,384]{1,0:T(8,128)(2,1)} %bitcast.58, bf16[256,256]{1,0:T(8,128)(2,1)} %constant.75.clone.high_ref, bf16[256,256]{1,0:T(8,128)(2,1)} %constant.76.clone.low_ref), custom_call_target="tpu_custom_call" | custom-call | flops 800000000 | bytes 5000000 | tf_op jit(solution)/shard_map/pallas_call | solution.py:313
  8.7 15.1 %all-to-all-start.1 = ((f32[64,2,48,128]{3,2,1,0:T(8,128)}), f32[64,2,48,128]{3,2,1,0:T(8,128)S(1)}, u32[]{:S(2)}, u32[]{:S(2)}) async-start(f32[64,2,48,128]{3,2,1,0:T(8,128)} %shard_map.183), calls=%async_computation.1 | async-start | bytes 6291456 | tf_op jit(solution)/shard_map/all_to_all | solution.py:355
  23.8 8.0 %shard_map.182 = f32[64,2,48,128]{3,2,1,0:T(8,128)} custom-call(bf16[2048,384]{1,0:T(8,128)(2,1)} %bitcast.53, bf16[256,256]{1,0:T(8,128)(2,1)} %constant.75.clone.high_ref, bf16[256,256]{1,0:T(8,128)(2,1)} %constant.76.clone.low_ref), custom_call_target="tpu_custom_call" | custom-call | flops 800000000 | bytes 5000000 | tf_op jit(solution)/shard_map/pallas_call | solution.py:313
  31.8 62.4 %all-to-all-done.1.src_ref = f32[64,2,48,128]{3,2,1,0:T(8,128)S(1)} async-done(((f32[64,2,48,128]{3,2,1,0:T(8,128)}), f32[64,2,48,128]{3,2,1,0:T(8,128)S(1)}, u32[]{:S(2)}, u32[]{:S(2)}) %all-to-all-start.1) | async-done | bytes 3145760 | tf_op jit(solution)/shard_map/all_to_all | solution.py:355
  94.1 1.7 copy-done.2
  95.8 10.8 %all-to-all-start = ((f32[64,2,48,128]{3,2,1,0:T(8,128)}), f32[64,2,48,128]{3,2,1,0:T(8,128)S(1)}, u32[]{:S(2)}, u32[]{:S(2)}) async-start(f32[64,2,48,128]{3,2,1,0:T(8,128)} %shard_map.182), calls=%async_computation | async-start | bytes 6291456 | tf_op jit(solution)/shard_map/all_to_all | solution.py:355
  109.0 0.8 dynamic-slice_bitcast_fusion.1
  109.8 0.8 fusion.6
  111.4 1.6 copy.48.w2l
  114.6 1.6 copy.45.w1l
  118.6 24.4 %shard_map.184 = (f32[16,192,256]{2,1,0:T(8,128)}, f32[16,192,256]{2,1,0:T(8,128)}, f32[16,192,256]{2,1,0:T(8,128)}, f32[16,192,256]{2,1,0:T(8,128)}) custom-call(f32[1,1]{1,0:T(1,128)} %bitcast.15.doubling_ref, f32[64,2,48,128]{3,2,1,0:T(8,128)} %copy-done.2, f32[64,2,128]{2,1,0:T(2,128)} %constant.77.clone.twiddle_ref, ...), custom_call_target="tpu_custom_call" | custom-call | flops 8000000000 | bytes 16000000 | tf_op jit(solution)/shard_map/pallas_call | solution.py:373
  143.0 33.8 %all-to-all-done.src_ref = f32[64,2,48,128]{3,2,1,0:T(8,128)S(1)} async-done(((f32[64,2,48,128]{3,2,1,0:T(8,128)}), f32[64,2,48,128]{3,2,1,0:T(8,128)S(1)}, u32[]{:S(2)}, u32[]{:S(2)}) %all-to-all-start) | async-done | bytes 3145760 | tf_op jit(solution)/shard_map/all_to_all | solution.py:355
  176.7 1.7 copy-done.1
  178.4 31.1 %shard_map.185 = (f32[16,192,256]{2,1,0:T(8,128)}, f32[16,192,256]{2,1,0:T(8,128)}, f32[64,2,48,128]{3,2,1,0:T(8,128)}) custom-call(f32[64,2,48,128]{3,2,1,0:T(8,128)} %copy-done.1, f32[64,2,128]{2,1,0:T(2,128)} %constant.77.clone.twiddle_ref, bf16[512,512]{1,0:T(8,128)(2,1)} %constant.78.clone.th_ref, bf16[512,512]{1,0:T(8,128)(2,1)} %constant.79.clone.tl_ref, ...), custom_call_target="tpu_custom_call" | custom-call | flops 10000000000 | bytes 20000000 | tf_op jit(solution)/shard_map/pallas_call | solution.py:313
  209.5 12.3 %shard_map.187 = (f32[192,192]{1,0:T(8,128)}, f32[192,1]{1,0:T(8,128)}, f32[192,192]{1,0:T(8,128)}, f32[192,1]{1,0:T(8,128)}) custom-call(f32[16,192,256]{2,1,0:T(8,128)} %get-tuple-element.19.spec_ref, f32[16,192,256]{2,1,0:T(8,128)} %get-tuple-element.20.outer_ref, f32[16,192,256]{2,1,0:T(8,128)} %get-tuple-element.21.one_ref, ...), custom_call_target="tpu_custom_call" | custom-call | flops 4000000000 | bytes 13000000 | tf_op jit(solution)/shard_map/pallas_call | solution.py:313
  221.8 1.1 add_bitcast_fusion.1
  223.0 1.0 reduce.2
  224.0 1.0 reduce.3
  225.0 1.1 add_bitcast_fusion
  226.4 22.5 %all_to_all.40 = f32[64,5,128]{2,1,0:T(8,128)S(1)} all-to-all(f32[64,5,128]{2,1,0:T(8,128)S(1)} %reshape.85), channel_id=1, replica_groups=mesh['dp'=4,'px'=8,'py'=8] {'px','py'}, dimensions={0} | all-to-all | bytes 327680 | tf_op jit(solution)/shard_map/all_to_all | solution.py:355
  249.0 9.1 %all_to_all.41 = f32[4,5,128]{2,1,0:T(8,128)S(1)} all-to-all(f32[4,5,128]{2,1,0:T(8,128)S(1)} %bitcast_reduce_fusion), channel_id=1, replica_groups=mesh['dp'=4,'px'=8,'py'=8] {'dp'}, dimensions={0} | all-to-all | bytes 20480 | tf_op jit(solution)/shard_map/all_to_all | solution.py:414
  258.1 9.2 %all_to_all.42 = f32[8,5,128]{2,1,0:T(8,128)S(1)} all-to-all(f32[8,5,128]{2,1,0:T(8,128)S(1)} %broadcast_in_dim.19), channel_id=1, replica_groups=mesh['dp'=4,'px'=8,'py'=8] {'py'}, dimensions={0} | all-to-all | bytes 40960 | tf_op jit(solution)/shard_map/all_to_all | solution.py:417
  267.3 9.7 %all_to_all.43 = f32[8,40,128]{2,1,0:T(8,128)S(1)} all-to-all(f32[8,40,128]{2,1,0:T(8,128)S(1)} %broadcast_in_dim.21), channel_id=1, replica_groups=mesh['dp'=4,'px'=8,'py'=8] {'px'}, dimensions={0} | all-to-all | bytes 327680 | tf_op jit(solution)/shard_map/all_to_all | solution.py:417
  277.0 15.6 %all_to_all.44 = f32[4,320,128]{2,1,0:T(8,128)} all-to-all(f32[4,320,128]{2,1,0:T(8,128)S(1)} %broadcast_in_dim.23), channel_id=1, replica_groups=mesh['dp'=4,'px'=8,'py'=8] {'dp'}, dimensions={0} | all-to-all | bytes 1310720 | tf_op jit(solution)/shard_map/all_to_all | solution.py:417
  292.7 4.9 %all-to-all-start.2 = ((f32[64,2,48,128]{3,2,1,0:T(8,128)}), f32[64,2,48,128]{3,2,1,0:T(8,128)S(1)}, u32[]{:S(2)}, u32[]{:S(2)}) async-start(f32[64,2,48,128]{3,2,1,0:T(8,128)} %get-tuple-element.18), calls=%async_computation.2 | async-start | bytes 6291456 | tf_op jit(solution)/shard_map/all_to_all | solution.py:355
  297.6 1.5 copy.58
  301.2 1.9 fusion.8
  303.1 1.2 reshape.90
  305.1 1.2 reshape.88
  307.0 60.5 %all-to-all-done.2.src_ref = f32[64,2,48,128]{3,2,1,0:T(8,128)S(1)} async-done(((f32[64,2,48,128]{3,2,1,0:T(8,128)}), f32[64,2,48,128]{3,2,1,0:T(8,128)S(1)}, u32[]{:S(2)}, u32[]{:S(2)}) %all-to-all-start.2) | async-done | bytes 3145760 | tf_op jit(solution)/shard_map/all_to_all | solution.py:355
  367.5 1.6 copy-done
  369.2 8.6 %shard_map.186 = bf16[2048,384]{1,0:T(8,128)(2,1)} custom-call(f32[64,2,48,128]{3,2,1,0:T(8,128)} %copy-done, bf16[2048,384]{1,0:T(8,128)(2,1)} %bitcast.54, bf16[256,256]{1,0:T(8,128)(2,1)} %constant.82.clone.high_ref, bf16[256,256]{1,0:T(8,128)(2,1)} %constant.83.clone.low_ref), custom_call_target="tpu_custom_call" | custom-call | flops 1200000000 | bytes 7000000 | tf_op jit(solution)/shard_map/pallas_call | solution.py:313
  (35 shorter events, 11.1 us)
Async XLA Ops:
  8.7 85.5 %all-to-all-start.1 = ((f32[64,2,48,128]{3,2,1,0:T(8,128)}), f32[64,2,48,128]{3,2,1,0:T(8,128)S(1)}, u32[]{:S(2)}, u32[]{:S(2)}) async-start(f32[64,2,48,128]{3,2,1,0:T(8,128)} %shard_map.183), calls=%async_computation.1 | async-start | bytes 6291456 | tf_op jit(solution)/shard_map/all_to_all | solution.py:355
  94.1 1.7 copy-start.2
  95.8 80.9 %all-to-all-start = ((f32[64,2,48,128]{3,2,1,0:T(8,128)}), f32[64,2,48,128]{3,2,1,0:T(8,128)S(1)}, u32[]{:S(2)}, u32[]{:S(2)}) async-start(f32[64,2,48,128]{3,2,1,0:T(8,128)} %shard_map.182), calls=%async_computation | async-start | bytes 6291456 | tf_op jit(solution)/shard_map/all_to_all | solution.py:355
  176.7 1.7 copy-start.1
  292.7 74.9 %all-to-all-start.2 = ((f32[64,2,48,128]{3,2,1,0:T(8,128)}), f32[64,2,48,128]{3,2,1,0:T(8,128)S(1)}, u32[]{:S(2)}, u32[]{:S(2)}) async-start(f32[64,2,48,128]{3,2,1,0:T(8,128)} %get-tuple-element.18), calls=%async_computation.2 | async-start | bytes 6291456 | tf_op jit(solution)/shard_map/all_to_all | solution.py:355
  299.1 0.8 copy-start.3
  367.5 1.7 copy-start

commit v2 on v1

--- a/solution.py
+++ b/solution.py
@@ -18,13 +18,14 @@
 C = 384
 HALF = BS // 2
 CELLS = 64
-GROUPS = 16
-WIDE = 256
-PIECE = 640
+STEP = 8
+GROUPS = 64 // STEP
+WIDE = STEP * 64
+ROWS = 512
 SHRINK = 0.25
 f32 = jnp.float32
 bf16 = jnp.bfloat16
-BIG = pltpu.CompilerParams(vmem_limit_bytes=56 * 1024 * 1024)
+BIG = pltpu.CompilerParams(vmem_limit_bytes=26 * 1024 * 1024)
 SPECTRAL = jax.ShapeDtypeStruct((64, 2, HALF, 128), f32)
 GROUPED = jax.ShapeDtypeStruct((GROUPS, 2 * BS, WIDE), f32)
 
@@ -55,8 +56,7 @@
     real[0, :, 1] = both.imag
     real[1, :, 0] = -both.imag
     real[1, :, 1] = both.real
-    eye = np.eye(2)
-    forward = np.einsum("qxpf,kl,cd->kqcxpdlf", real, eye, eye).reshape(512, 512)
+    forward = np.einsum("qxpf,cd->qcxpdf", real, np.eye(2)).reshape(256, 256)
     return np_split(forward), np_split(forward.T.copy())
 
 
@@ -80,9 +80,24 @@
 
 
 def dot3(left, right, dims=((1,), (0,))):
-    return (
-        dot(left[0], right[0], dims) + dot(left[0], right[1], dims) + dot(left[1], right[0], dims)
-    )
+    high, low = left
+    rows = high.shape[0]
+    both = dot(jnp.concatenate([high, low], axis=0), right[0], dims)
+    return both[:rows] + both[rows:] + dot(high, right[1], dims)
+
+
+def product(weight_ref, value):
+    rows = weight_ref.shape[0] // 2
+    high, low = split(value)
+    both = dot(weight_ref[...], high)
+    return both[:rows] + both[rows:] + dot(weight_ref[:rows], low)
+
+
+def swap(upper, lower):
+    lane = lax.broadcasted_iota(jnp.int32, upper.shape, 1)
+    first = jnp.where(lane < 64, upper, pltpu.roll(lower, 64, 1))
+    second = jnp.where(lane < 64, pltpu.roll(upper, 64, 1), lower)
+    return first, second
 
 
 def fft(re, im, sign):
@@ -166,59 +181,56 @@
 
 
 def load_group(work_ref, group, high_ref, low_ref):
-    rows = []
-    for pair in range(2):
-        rows.append(
-            jnp.concatenate(
-                [work_ref[group * 4 + pair * 2 + n // 2, n % 2] for n in range(4)], axis=1
-            )
-        )
+    rows = [
+        jnp.concatenate([work_ref[group * STEP + n, 0], work_ref[group * STEP + n, 1]], axis=1)
+        for n in range(STEP)
+    ]
     values = dot3(split(jnp.concatenate(rows, axis=0)), (high_ref[...], low_ref[...]))
-    halves = []
-    for pair in range(2):
-        part = values[pair * HALF : (pair + 1) * HALF]
-        halves.append(
-            jnp.concatenate([part[:, n * 128 : (n + 1) * 128] for n in range(4)], axis=0)
-        )
-    return jnp.concatenate(halves, axis=1)
+    pairs = []
+    for pair in range(STEP // 2):
+        part = []
+        for q in range(2):
+            lanes = slice(q * 128, (q + 1) * 128)
+            upper = values[2 * pair * HALF : (2 * pair + 1) * HALF, lanes]
+            lower = values[(2 * pair + 1) * HALF : (2 * pair + 2) * HALF, lanes]
+            part.extend(swap(upper, lower))
+        pairs.append(jnp.concatenate(part, axis=0))
+    return jnp.concatenate(pairs, axis=1)
 
 
 def store_group(work_ref, group, spectral, high_ref, low_ref):
     rows = []
-    for pair in range(2):
+    for pair in range(STEP // 2):
         part = spectral[:, pair * 128 : (pair + 1) * 128]
-        rows.append(
-            jnp.concatenate([part[n * HALF : (n + 1) * HALF] for n in range(4)], axis=1)
-        )
+        parts = [
+            swap(part[q * BS : q * BS + HALF], part[q * BS + HALF : (q + 1) * BS])
+            for q in range(2)
+        ]
+        for n in range(2):
+            rows.append(jnp.concatenate([parts[0][n], parts[1][n]], axis=1))
     values = dot3(split(jnp.concatenate(rows, axis=0)), (high_ref[...], low_ref[...]))
-    for pair in range(2):
-        for n in range(4):
-            work_ref[group * 4 + pair * 2 + n // 2, n % 2] = values[
-                pair * HALF : (pair + 1) * HALF, n * 128 : (n + 1) * 128
+    for n in range(STEP):
+        for q in range(2):
+            work_ref[group * STEP + n, q] = values[
+                n * HALF : (n + 1) * HALF, q * 128 : (q + 1) * 128
             ]
 
 
-def depth_kernel(field_ref, high_ref, low_ref, out_ref, work_ref):
+def depth_kernel(field_ref, both_ref, out_ref, work_ref):
     for g in range(8):
-        rows = field_ref[g * 256 : (g + 1) * 256, :]
-        values = dot(high_ref[...], rows) + dot(low_ref[...], rows)
+        values = dot(both_ref[...], field_ref[g * 256 : (g + 1) * 256, :])
+        values = values[:256] + values[256:]
         work_ref[:, g * 8 : (g + 1) * 8, :] = values.reshape(2 * KZ, 8, C)
-
-    def body(k, carry):
-        values = work_ref[pl.ds(2 * k, 2)].reshape(2 * CELLS, C).T
-        lane = lax.broadcasted_iota(jnp.int32, (HALF, 128), 1)
+    for k in range(KZ):
+        values = work_ref[2 * k : 2 * k + 2].reshape(2 * CELLS, C).T
         for b in range(NB):
             upper = values[b * BS : b * BS + HALF]
             lower = values[b * BS + HALF : (b + 1) * BS]
-            out_ref[b * KZ + k, 0] = jnp.where(lane < 64, upper, pltpu.roll(lower, 64, 1))
-            out_ref[b * KZ + k, 1] = jnp.where(lane < 64, pltpu.roll(upper, 64, 1), lower)
-        return carry
-
-    lax.fori_loop(0, KZ, body, 0)
+            out_ref[b * KZ + k, 0], out_ref[b * KZ + k, 1] = swap(upper, lower)
 
 
 def forward_kernel(
-    doubling_ref, src_ref, twiddle_ref, th_ref, tl_ref, w1h, w1l, b1, w2h, w2l, b2,
+    doubling_ref, src_ref, twiddle_ref, th_ref, tl_ref, w1, b1, w2, b2,
     spec_ref, outer_ref, slope_ref, square_ref, work_ref,
 ):
     plane_forward(src_ref, work_ref, twiddle_ref)
@@ -227,7 +239,7 @@
     def body(g, carry):
         spectral = load_group(work_ref, g, th_ref, tl_ref)
         spec_ref[g] = spectral
-        pre = dot3((w1h[...], w1l[...]), split(spectral)) + b1[...]
+        pre = product(w1, spectral) + b1[...]
         pre_sq = pre * pre
         t = jnp.tanh(root * (pre + 0.044715 * (pre * pre_sq)))
         outer = 0.5 * pre * (1.0 + t)
@@ -235,7 +247,7 @@
         slope_ref[g] = 0.5 * (1.0 + t) + 0.5 * pre * (1.0 - t * t) * (
             root * (1.0 + 3.0 * 0.044715 * pre_sq)
         )
-        pre_two = dot3((w2h[...], w2l[...]), split(outer)) + b2[...]
+        pre_two = product(w2, outer) + b2[...]
         t2 = jnp.tanh(pre_two * (1.0 / SHRINK))
         square_ref[g] = t2 * t2 * doubling_ref[0, 0]
         return carry
@@ -244,7 +256,7 @@
 
 
 def backward_kernel(
-    src_ref, twiddle_ref, th_ref, tl_ref, bh_ref, bl_ref, w1h, w1l, w2h, w2l, slope_ref, square_ref,
+    src_ref, twiddle_ref, th_ref, tl_ref, bh_ref, bl_ref, w1, w2, slope_ref, square_ref,
     two_ref, one_ref, out_ref, work_ref,
 ):
     plane_forward(src_ref, work_ref, twiddle_ref)
@@ -252,9 +264,9 @@
     def body(g, carry):
         grad_two = load_group(work_ref, g, th_ref, tl_ref) * square_ref[g]
         two_ref[g] = grad_two
-        grad_one = dot3((w2h[...], w2l[...]), split(grad_two)) * slope_ref[g]
+        grad_one = product(w2, grad_two) * slope_ref[g]
         one_ref[g] = grad_one
-        grad_spec = dot3((w1h[...], w1l[...]), split(grad_one))
+        grad_spec = product(w1, grad_one)
         store_group(work_ref, g, grad_spec, bh_ref, bl_ref)
         return carry
 
@@ -262,44 +274,54 @@
     plane_backward(work_ref, out_ref, twiddle_ref)
 
 
-def table_kernel(spec_ref, outer_ref, one_ref, two_ref, t1_ref, b1_ref, t2_ref, b2_ref):
+def spread(value):
+    gap = jnp.zeros((128 - BS, value.shape[1]), value.dtype)
+    return jnp.concatenate([value[:BS], gap, value[BS:], gap], axis=0)
+
+
+def table_kernel(spec_ref, outer_ref, one_ref, two_ref, out_ref):
     lanes = ((1,), (1,))
-    shape = (2 * BS, 2 * BS)
 
     def body(g, carry):
         t1, s1, t2, s2 = carry
-        one = one_ref[g]
-        two = two_ref[g]
+        one = spread(one_ref[g])
+        two = spread(two_ref[g])
         t1 = t1 + dot3(split(spec_ref[g]), split(one), lanes)
         t2 = t2 + dot3(split(outer_ref[g]), split(two), lanes)
         return t1, s1 + one, t2, s2 + two
 
-    zero = jnp.zeros(shape, f32)
-    wide = jnp.zeros((2 * BS, WIDE), f32)
+    zero = jnp.zeros((2 * BS, 256), f32)
+    wide = jnp.zeros((256, WIDE), f32)
     t1, s1, t2, s2 = lax.fori_loop(0, GROUPS, body, (zero, wide, zero, wide))
-    t1_ref[...] = t1
-    t2_ref[...] = t2
-    b1_ref[...] = jnp.sum(s1, axis=1, keepdims=True)
-    b2_ref[...] = jnp.sum(s2, axis=1, keepdims=True)
+    norm = 1.0 / math.sqrt(4 * NX * NY * KZ)
+    ones = jnp.ones((8, WIDE), bf16)
+    row = lax.broadcasted_iota(jnp.int32, (8, 128), 0)
+    out_ref[4 * BS :] = jnp.zeros((ROWS - 4 * BS, 128), f32)
+    biases = jnp.zeros((8, 128), f32)
+    for n, (table, total) in enumerate(((t1, s1), (t2, s2))):
+        real = table[:BS, :128] + table[BS:, 128:]
+        imag = table[:BS, 128:] - table[BS:, :128]
+        out_ref[2 * n * BS : (2 * n + 1) * BS] = real * norm
+        out_ref[(2 * n + 1) * BS : (2 * n + 2) * BS] = imag * norm
+        high, low = split(total)
+        sums = dot(ones, high, lanes) + dot(ones, low, lanes)
+        for q in range(2):
+            biases = jnp.where(row == 2 * n + q, sums[:, q * 128 : (q + 1) * 128], biases)
+    out_ref[4 * BS : 4 * BS + 8] = biases * norm
 
 
 def field_kernel(src_ref, cotangent_ref, high_ref, low_ref, out_ref, work_ref):
-    def body(k, carry):
-        lane = lax.broadcasted_iota(jnp.int32, (HALF, 128), 1)
+    for k in range(KZ):
         parts = []
         for b in range(NB):
-            re = src_ref[b * KZ + k, 0]
-            im = src_ref[b * KZ + k, 1]
-            parts.append(jnp.where(lane < 64, re, pltpu.roll(im, 64, 1)))
-            parts.append(jnp.where(lane < 64, pltpu.roll(re, 64, 1), im))
+            parts.extend(swap(src_ref[b * KZ + k, 0], src_ref[b * KZ + k, 1]))
         values = jnp.concatenate(parts, axis=0).T
-        work_ref[pl.ds(2 * k, 2)] = values.reshape(2, CELLS, C)
-        return carry
-
-    lax.fori_loop(0, KZ, body, 0)
+        work_ref[2 * k : 2 * k + 2] = values.reshape(2, CELLS, C)
+    both = jnp.concatenate([high_ref[...], low_ref[...]], axis=0)
     for g in range(8):
-        rows = work_ref[:, g * 8 : (g + 1) * 8, :].reshape(256, C)
-        values = dot3((high_ref[...], low_ref[...]), split(rows))
+        high, low = split(work_ref[:, g * 8 : (g + 1) * 8, :].reshape(256, C))
+        values = dot(both, high)
+        values = values[:256] + values[256:] + dot(high_ref[...], low)
         span = slice(g * 256, (g + 1) * 256)
         out_ref[span, :] = (cotangent_ref[span, :].astype(f32) + values).astype(bf16)
 
@@ -325,7 +347,7 @@
     return call(
         depth_kernel,
         SPECTRAL,
-        (field.reshape(2048, C), *tables),
+        (field.reshape(2048, C), np.concatenate(tables, axis=0)),
         [pltpu.VMEM((2 * KZ, CELLS, C), f32)],
         800_000_000,
         5_000_000,
@@ -340,15 +362,45 @@
     )
 
 
-def jax_split(value):
+def stacked(value):
     high = lax.reduce_precision(value, 8, 7)
-    return high.astype(bf16), (value - high).astype(bf16)
-
-
-def fold(table):
-    return jnp.stack(
-        [table[:BS, :BS] + table[BS:, BS:], table[:BS, BS:] - table[BS:, :BS]]
-    )
+    return jnp.concatenate([high.astype(bf16), (value - high).astype(bf16)], axis=0)
+
+
+def keep_half(value, axis, flip, bit):
+    half = value.shape[0] // 2
+    size = lax.axis_size(axis)
+    mine = lax.dynamic_slice_in_dim(value, bit * half, half, 0)
+    other = lax.dynamic_slice_in_dim(value, (1 - bit) * half, half, 0)
+    return mine + lax.ppermute(other, axis, [(n, n ^ flip) for n in range(size)])
+
+
+def join_half(value, axis, flip, bit):
+    size = lax.axis_size(axis)
+    other = lax.ppermute(value, axis, [(n, n ^ flip) for n in range(size)])
+    return jnp.where(bit == 0, jnp.stack([value, other]), jnp.stack([other, value]))
+
+
+def total_rows(rows, grad_cells):
+    dp = lax.axis_index("dp")
+    px = lax.axis_index("px")
+    py = lax.axis_index("py")
+    core = dp % 2
+    low = dp // 2
+    rows = keep_half(rows, "dp", 1, core)
+    rows = keep_half(rows, "dp", 2, low)
+    rows = keep_half(rows, "px", 1, px % 2)
+    pieces = rows.reshape(8, -1, 128)
+    total = lax.dynamic_index_in_dim(pieces, py, 0, keepdims=False)
+    for offset in range(1, 8):
+        piece = lax.dynamic_index_in_dim(pieces, (py + offset) % 8, 0, keepdims=False)
+        total = total + lax.ppermute(piece, "py", [(n, (n + offset) % 8) for n in range(8)])
+    total, grad_cells = lax.optimization_barrier((total, grad_cells))
+    total = exchange(jnp.broadcast_to(total[None], (64, *total.shape)))
+    total = join_half(total, "dp", 2, low)
+    total = join_half(total, "dp", 1, core)
+    total = total.reshape(2, 2, NB, 2, 8, ROWS // 64, 128)
+    return total.transpose(2, 0, 1, 3, 4, 5, 6).reshape(NB, ROWS, 128), grad_cells
 
 
 def exchange(value):
@@ -373,52 +425,37 @@
     spec, outer, slope, square = pl.pallas_call(
         forward_kernel,
         out_shape=(GROUPED,) * 4,
-        in_specs=[pl.BlockSpec(memory_space=pltpu.SMEM)] + vmem(10),
+        in_specs=[pl.BlockSpec(memory_space=pltpu.SMEM)] + vmem(8),
         out_specs=tuple(vmem(4)),
         scratch_shapes=[pltpu.VMEM((64, 2, HALF, 128), f32)],
         compiler_params=BIG,
         cost_estimate=pl.CostEstimate(
             flops=8_000_000_000, bytes_accessed=16_000_000, transcendentals=1_500_000
         ),
-    )(doubling, state_spec, twiddle, *plane_fwd, *jax_split(first), bias_one, *jax_split(second), bias_two)
+    )(doubling, state_spec, twiddle, *plane_fwd, stacked(first), bias_one, stacked(second), bias_two)
 
     grad_two, grad_one, grad_plane = call(
         backward_kernel,
         (GROUPED, GROUPED, SPECTRAL),
-        (cot_spec, twiddle, *plane_fwd, *plane_bwd, *jax_split(first.T), *jax_split(second.T), slope, square),
+        (cot_spec, twiddle, *plane_fwd, *plane_bwd, stacked(first.T), stacked(second.T), slope, square),
         [pltpu.VMEM((64, 2, HALF, 128), f32)],
         10_000_000_000,
         20_000_000,
     )
     grad_cells = exchange(grad_plane)
 
-    t1, s1, t2, s2 = call(
+    rows = call(
         table_kernel,
-        (
-            jax.ShapeDtypeStruct((2 * BS, 2 * BS), f32),
-            jax.ShapeDtypeStruct((2 * BS, 1), f32),
-        )
-        * 2,
+        jax.ShapeDtypeStruct((ROWS, 128), f32),
         (spec, outer, grad_one, grad_two),
         [],
         4_000_000_000,
         13_000_000,
     )
-    norm = 1.0 / math.sqrt(4 * NX * NY * KZ)
-    wide = 2 * BS * BS
-    flat = jnp.concatenate(
-        [fold(t1).reshape(-1), fold(t2).reshape(-1), s1.reshape(-1), s2.reshape(-1)]
-    )
-    flat = jnp.pad(flat * norm, (0, 64 * PIECE - flat.shape[0])).reshape(64, 5, 128)
-    flat = exchange(flat).reshape(NB, KZ, 5, 128).sum(axis=1)
-    flat = lax.all_to_all(flat, "dp", split_axis=0, concat_axis=0, tiled=True).sum(axis=0)
-    for axis, size in (("py", 8), ("px", 8), ("dp", 4)):
-        flat = jnp.broadcast_to(flat.reshape(1, -1, 128), (size, flat.size // 128, 128))
-        flat = lax.all_to_all(flat, axis, split_axis=0, concat_axis=0, tiled=True)
-    flat = flat.reshape(NB, 64 * PIECE)
-    grads_one = flat[:, :wide].reshape(NB, 2, BS, BS).transpose(1, 0, 2, 3)
-    grads_two = flat[:, wide : 2 * wide].reshape(NB, 2, BS, BS).transpose(1, 0, 2, 3)
-    biases = flat[:, 2 * wide : 2 * wide + 4 * BS].reshape(NB, 2, 2, BS)
+    rows, grad_cells = total_rows(rows, grad_cells)
+    grads_one = rows[:, : 2 * BS, :BS].reshape(NB, 2, BS, BS).transpose(1, 0, 2, 3)
+    grads_two = rows[:, 2 * BS : 4 * BS, :BS].reshape(NB, 2, BS, BS).transpose(1, 0, 2, 3)
+    biases = rows[:, 4 * BS : 4 * BS + 4, :BS].reshape(NB, 2, 2, BS)
 
     state_grad = call(
         field_kernel,

time: 383 us -> 338 us (0.88); the launches traced: 378 us -> 337 us
  Pallas kernels: 92.4 us -> 50.7 us
  blocking collectives: 66.1 us -> 24.4 us
  starting transfers between devices: 30.8 us -> 60.5 us
  local copies, waits for them, and re-layouts: 22.7 us -> 47.5 us
  waiting for transfers between devices: 157 us -> 145 us
    all_to_all x3, waiting for transfers between devices: 157 us -> 102 us  [exchange(): lax.all_to_all(value, ('px', 'py'), split_axis=0, concat_axis=0, tiled=True)]
    all_to_all x4 -> x0, blocking collectives: 43.6 us -> none  [the longest x3 34.5 us: shards(): flat = lax.all_to_all(flat, axis, split_axis=0, concat_axis=0, tiled=True)]
    ppermute x0 -> x12, waiting for transfers between devices: none -> 43.4 us  [the longest x7 31.4 us: total_rows(): lax.ppermute(piece, 'py', [(n, (n + offset) % 8) for n in range(8)])]
    unnamed x13 -> x70, local copies, waits for them, and re-layouts: 10.1 us -> 41.8 us
    pallas_call x5, Pallas kernels: 68 us -> 36.5 us  [call(): pl.pallas_call(kernel, out_shape=out_shape, in_specs=vmem(len(args)), out...]
    ppermute x0 -> x12, starting transfers between devices: none -> 23.7 us  [the longest x7 12 us: total_rows(): lax.ppermute(piece, 'py', [(n, (n + offset) % 8) for n in range(8)])]
    pallas_call x1, Pallas kernels: 24.4 us -> 14.1 us  [shards(): pl.pallas_call(forward_kernel, out_shape=(GROUPED,) * 4, in_specs=[pl.Blo...]
    all_to_all x3, starting transfers between devices: 30.8 us -> 36.9 us  [exchange(): lax.all_to_all(value, ('px', 'py'), split_axis=0, concat_axis=0, tiled=True)]
  transfers between devices with their start and end apart: 3 -> 15, of which waited for: 3 -> 9; matrix products, arithmetic and copies ran while one was open for 5% -> 3% of each run, Pallas kernels for 9% -> 9%
where the time goes in v2:
time: 338 us; the launch traced here: 337 us
  waiting for transfers between devices  145 us (43%)
  starting transfers between devices  60.5 us (18%)
  Pallas kernels  50.7 us (15%)
  local copies, waits for them, and re-layouts  47.5 us (14%)
  blocking collectives  24.4 us (7%)
  other arithmetic  7.69 us (2%)
    all_to_all x3, waiting for transfers between devices, exchange(): lax.all_to_all(value, ('px', 'py'), split_axis=0, concat_axis=0, tiled=True)  102 us
    unnamed x70, local copies, waits for them, and re-layouts  41.8 us
    all_to_all x3, starting transfers between devices, exchange(): lax.all_to_all(value, ('px', 'py'), split_axis=0, concat_axis=0, tiled=True)  36.9 us
    pallas_call x5, Pallas kernels, call(): pl.pallas_call(kernel, out_shape=out_shape, in_specs=vmem(len(args)), out...  36.5 us
    ppermute x7, waiting for transfers between devices, total_rows(): lax.ppermute(piece, 'py', [(n, (n + offset) % 8) for n in range(8)])  31.4 us
    all_to_all x1, blocking collectives, exchange(): lax.all_to_all(value, ('px', 'py'), split_axis=0, concat_axis=0, tiled=True)  24.4 us
    pallas_call x1, Pallas kernels, shards(): pl.pallas_call(forward_kernel, out_shape=(GROUPED,) * 4, in_specs=[pl.Blo...  14.1 us
    ppermute x7, starting transfers between devices, total_rows(): lax.ppermute(piece, 'py', [(n, (n + offset) % 8) for n in range(8)])  12 us
  transfers between devices with their start and end apart: 15, of which 9 were waited for; matrix products, arithmetic and copies ran while one was open for 3% of the time, Pallas kernels for 9%

profile of v2, /device:TPU:1, one launch (start us, length us, event | category | flops | bytes accessed | tf_op | source)
XLA Modules:
  0.0 336.8 jit_solution(18049680182103809799)
XLA Ops:
  3.0 4.7 %shard_map.182 = f32[64,2,48,128]{3,2,1,0:T(8,128)} custom-call(bf16[2048,384]{1,0:T(8,128)(2,1)S(1)} %bitcast.87, bf16[512,256]{1,0:T(8,128)(2,1)S(1)} %copy-done.4), custom_call_target="tpu_custom_call" | custom-call | flops 800000000 | bytes 5000000 | tf_op jit(solution)/shard_map/pallas_call | solution.py:335
  7.7 15.5 %all-to-all-start = ((f32[64,2,48,128]{3,2,1,0:T(8,128)}), f32[64,2,48,128]{3,2,1,0:T(8,128)}, u32[]{:S(2)}, u32[]{:S(2)}) async-start(f32[64,2,48,128]{3,2,1,0:T(8,128)} %shard_map.182), calls=%async_computation | async-start | bytes 6291456 | tf_op jit(solution)/shard_map/all_to_all | solution.py:407
  23.2 4.9 %shard_map.184 = f32[64,2,48,128]{3,2,1,0:T(8,128)} custom-call(bf16[2048,384]{1,0:T(8,128)(2,1)S(1)} %bitcast.85, bf16[512,256]{1,0:T(8,128)(2,1)S(1)} %copy-done.5), custom_call_target="tpu_custom_call" | custom-call | flops 800000000 | bytes 5000000 | tf_op jit(solution)/shard_map/pallas_call | solution.py:335
  28.1 65.4 %all-to-all-done.src_ref = f32[64,2,48,128]{3,2,1,0:T(8,128)} async-done(((f32[64,2,48,128]{3,2,1,0:T(8,128)}), f32[64,2,48,128]{3,2,1,0:T(8,128)}, u32[]{:S(2)}, u32[]{:S(2)}) %all-to-all-start) | async-done | bytes 3145760 | tf_op jit(solution)/shard_map/all_to_all | solution.py:407
  93.5 11.0 %all-to-all-start.1 = ((f32[64,2,48,128]{3,2,1,0:T(8,128)}), f32[64,2,48,128]{3,2,1,0:T(8,128)}, u32[]{:S(2)}, u32[]{:S(2)}) async-start(f32[64,2,48,128]{3,2,1,0:T(8,128)} %shard_map.184), calls=%async_computation.1 | async-start | bytes 6291456 | tf_op jit(solution)/shard_map/all_to_all | solution.py:407
  117.3 14.1 %shard_map.183 = (f32[8,192,512]{2,1,0:T(8,128)S(1)}, f32[8,192,512]{2,1,0:T(8,128)S(1)}, f32[8,192,512]{2,1,0:T(8,128)S(1)}, f32[8,192,512]{2,1,0:T(8,128)S(1)}) custom-call(f32[1,1]{1,0:T(1,128)} %bitcast.doubling_ref, f32[64,2,48,128]{3,2,1,0:T(8,128)} %all-to-all-done.src_ref, f32[64,2,128]{2,1,0:T(2,128)S(1)} %copy-done.18, ...), custom_call_target="tpu_custom_call" | custom-call | flops 8000000000 | bytes 16000000 | tf_op jit(solution)/shard_map/pallas_call | solution.py:425
  138.1 36.4 %all-to-all-done.1.src_ref = f32[64,2,48,128]{3,2,1,0:T(8,128)} async-done(((f32[64,2,48,128]{3,2,1,0:T(8,128)}), f32[64,2,48,128]{3,2,1,0:T(8,128)}, u32[]{:S(2)}, u32[]{:S(2)}) %all-to-all-start.1) | async-done | bytes 3145760 | tf_op jit(solution)/shard_map/all_to_all | solution.py:407
  179.0 1.9 copy-done.29
  180.8 1.9 copy-done.31
  182.7 16.7 %shard_map.185 = (f32[8,192,512]{2,1,0:T(8,128)S(1)}, f32[8,192,512]{2,1,0:T(8,128)S(1)}, f32[64,2,48,128]{3,2,1,0:T(8,128)S(1)}) custom-call(f32[64,2,48,128]{3,2,1,0:T(8,128)} %all-to-all-done.1.src_ref, f32[64,2,128]{2,1,0:T(2,128)S(1)} %copy-done.19, bf16[256,256]{1,0:T(8,128)(2,1)S(1)} %copy-done.13, bf16[256,256]{1,0:T(8,128)(2,1)S(1)} %copy-done.15, ...), custom_call_target="tpu_custom_call" | custom-call | flops 10000000000 | bytes 20000000 | tf_op jit(solution)/shard_map/pallas_call | solution.py:335
  202.7 1.7 copy-done.26
  204.4 10.3 %all-to-all-start.2 = ((f32[64,2,48,128]{3,2,1,0:T(8,128)}), f32[64,2,48,128]{3,2,1,0:T(8,128)S(1)}, u32[]{:S(2)}, u32[]{:S(2)}) async-start(f32[64,2,48,128]{3,2,1,0:T(8,128)} %copy-done.2), calls=%async_computation.2 | async-start | bytes 6291456 | tf_op jit(solution)/shard_map/all_to_all | solution.py:407
  214.8 1.9 copy-done.21
  216.7 1.9 copy-done.23
  218.6 1.9 copy-done.25
  220.5 1.9 copy-done.27
  222.4 5.7 %shard_map.186 = f32[512,128]{1,0:T(8,128)S(1)} custom-call(f32[8,192,512]{2,1,0:T(8,128)S(1)} %copy-done.21, f32[8,192,512]{2,1,0:T(8,128)S(1)} %copy-done.23, f32[8,192,512]{2,1,0:T(8,128)S(1)} %copy-done.27, f32[8,192,512]{2,1,0:T(8,128)S(1)} %copy-done.25), custom_call_target="tpu_custom_call" | custom-call | flops 4000000000 | bytes 13000000 | tf_op jit(solution)/shard_map/pallas_call | solution.py:335
  228.7 2.1 collective-permute-start
  234.1 3.2 collective-permute-done.1
  238.2 2.5 collective-permute-start.2
  240.8 2.5 collective-permute-done.2
  243.3 2.2 collective-permute-start.9
  245.5 4.0 %collective-permute-start.8 = (f32[8,128]{1,0:T(8,128)S(1)}, f32[8,128]{1,0:T(8,128)S(1)}, u32[]{:S(2)}, u32[]{:S(2)}) collective-permute-start(f32[8,128]{1,0:T(8,128)S(1)} %get-tuple-element.49), channel_id=1, source_target_pairs={{0,6},{1,7},{2,0},{3,1},{4,2},{5,3},{6,4},{7,5},{8,14},{9,15},{10,... | collective-permute-start | bytes 12296 | tf_op jit(solution)/shard_map/ppermute | solution.py:397
  250.2 2.5 collective-permute-start.6
  253.3 28.5 %collective-permute-done.9 = f32[8,128]{1,0:T(8,128)S(1)} collective-permute-done((f32[8,128]{1,0:T(8,128)S(1)}, f32[8,128]{1,0:T(8,128)S(1)}, u32[]{:S(2)}, u32[]{:S(2)}) %collective-permute-start.9) | collective-permute-done | bytes 4128 | tf_op jit(solution)/shard_map/ppermute | solution.py:397
  281.8 2.0 collective-permute-start.3
  284.4 2.3 collective-permute-done.4
  286.7 24.4 %all_to_all.20 = f32[64,8,128]{2,1,0:T(8,128)S(1)} all-to-all(f32[64,8,128]{2,1,0:T(8,128)S(1)} %broadcast_in_dim.2), channel_id=1, replica_groups=mesh['dp'=4,'px'=8,'py'=8] {'px','py'}, dimensions={0} | all-to-all | bytes 524288 | tf_op jit(solution)/shard_map/all_to_all | solution.py:407
  311.5 4.9 %collective-permute-done.10 = f32[64,8,128]{2,1,0:T(8,128)} collective-permute-done((f32[64,8,128]{2,1,0:T(8,128)S(1)}, f32[64,8,128]{2,1,0:T(8,128)}, u32[]{:S(2)}, u32[]{:S(2)}) %collective-permute-start.10) | collective-permute-done | bytes 262176 | tf_op jit(solution)/shard_map/ppermute | solution.py:380
  316.4 1.9 maximum_select_fusion.2
  318.3 6.2 %collective-permute-start.11 = (f32[2,64,8,128]{3,2,1,0:T(8,128)}, f32[2,64,8,128]{3,2,1,0:T(8,128)}, u32[]{:S(2)}, u32[]{:S(2)}) collective-permute-start(f32[2,64,8,128]{3,2,1,0:T(8,128)} %maximum_select_fusion.2), channel_id=1, source_target_pairs={{0,64},{64,0},{128,192},{192,128},{1,65},{65,1},{129,193},{193,129... | collective-permute-start | bytes 1572872 | tf_op jit(solution)/shard_map/ppermute | solution.py:380
  326.9 4.6 %shard_map.187 = bf16[2048,384]{1,0:T(8,128)(2,1)} custom-call(f32[64,2,48,128]{3,2,1,0:T(8,128)S(1)} %all-to-all-done.2.src_ref, bf16[2048,384]{1,0:T(8,128)(2,1)S(1)} %bitcast.86, bf16[256,256]{1,0:T(8,128)(2,1)S(1)} %copy-done.8, bf16[256,256]{1,0:T(8,128)(2,1)S(1)} %copy-done.9), custom_call_target="tpu_custom_call" | custom-call | flops 1200000000 | bytes 7000000 | tf_op jit(solution)/shard_map/pallas_call | solution.py:335
  (106 shorter events, 44.3 us)
Async XLA Ops:
  0.6 1.4 copy-start.3
  7.7 15.5 %copy-start = (bf16[1,8,8,32,384]{4,3,2,1,0:T(8,128)(2,1)S(1)}, bf16[1,8,8,32,384]{4,3,2,1,0:T(8,128)(2,1)}, u32[]{:S(2)}) copy-start(bf16[1,8,8,32,384]{4,3,2,1,0:T(8,128)(2,1)} %param.16) | copy-start | bytes 4718596
  7.7 15.5 %copy-start.5 = (bf16[512,256]{1,0:T(8,128)(2,1)S(1)}, bf16[512,256]{1,0:T(8,128)(2,1)}, u32[]{:S(2)}) copy-start(bf16[512,256]{1,0:T(8,128)(2,1)} %constant.161.clone.both_ref) | copy-start | bytes 786436
  7.7 85.7 %all-to-all-start = ((f32[64,2,48,128]{3,2,1,0:T(8,128)}), f32[64,2,48,128]{3,2,1,0:T(8,128)}, u32[]{:S(2)}, u32[]{:S(2)}) async-start(f32[64,2,48,128]{3,2,1,0:T(8,128)} %shard_map.182), calls=%async_computation | async-start | bytes 6291456 | tf_op jit(solution)/shard_map/all_to_all | solution.py:407
  93.5 81.0 %all-to-all-start.1 = ((f32[64,2,48,128]{3,2,1,0:T(8,128)}), f32[64,2,48,128]{3,2,1,0:T(8,128)}, u32[]{:S(2)}, u32[]{:S(2)}) async-start(f32[64,2,48,128]{3,2,1,0:T(8,128)} %shard_map.184), calls=%async_computation.1 | async-start | bytes 6291456 | tf_op jit(solution)/shard_map/all_to_all | solution.py:407
  131.4 1.7 copy-start.20
  133.1 1.7 copy-start.22
  134.8 1.6 copy-start.28
  136.5 1.7 copy-start.30
  179.0 1.9 copy-start.29
  180.8 1.9 copy-start.31
  199.4 1.6 copy-start.2
  201.0 1.6 copy-start.24
  202.7 1.7 copy-start.26
  204.4 82.3 %all-to-all-start.2 = ((f32[64,2,48,128]{3,2,1,0:T(8,128)}), f32[64,2,48,128]{3,2,1,0:T(8,128)S(1)}, u32[]{:S(2)}, u32[]{:S(2)}) async-start(f32[64,2,48,128]{3,2,1,0:T(8,128)} %copy-done.2), calls=%async_computation.2 | async-start | bytes 6291456 | tf_op jit(solution)/shard_map/all_to_all | solution.py:407
  214.8 1.9 copy-start.21
  216.7 1.9 copy-start.23
  218.6 1.9 copy-start.25
  220.5 1.9 copy-start.27
  228.0 96.5 %copy-start.8 = (bf16[256,256]{1,0:T(8,128)(2,1)S(1)}, bf16[256,256]{1,0:T(8,128)(2,1)}, u32[]{:S(2)}) copy-start(bf16[256,256]{1,0:T(8,128)(2,1)} %constant.167.clone.high_ref) | copy-start | bytes 393220
  228.7 3.5 %collective-permute-start = (f32[256,128]{1,0:T(8,128)}, f32[256,128]{1,0:T(8,128)}, u32[]{:S(2)}, u32[]{:S(2)}) collective-permute-start(f32[256,128]{1,0:T(8,128)} %constant_dynamic-slice_fusion.10), channel_id=1, source_target_pairs={{0,64},{64,0},{128,192},{192,128},{1,65},{65,1},{129,193},{193,129... | collective-permute-start | bytes 393224 | tf_op jit(solution)/shard_map/ppermute | solution.py:375
  233.7 3.6 %collective-permute-start.1 = (f32[128,128]{1,0:T(8,128)S(1)}, f32[128,128]{1,0:T(8,128)S(1)}, u32[]{:S(2)}, u32[]{:S(2)}) collective-permute-start(f32[128,128]{1,0:T(8,128)S(1)} %constant_dynamic-slice_fusion.9), channel_id=1, source_target_pairs={{0,128},{64,192},{128,0},{192,64},{1,129},{65,193},{129,1},{193,65... | collective-permute-start | bytes 196616 | tf_op jit(solution)/shard_map/ppermute | solution.py:375
  238.2 5.0 %collective-permute-start.2 = (f32[64,128]{1,0:T(8,128)S(1)}, f32[64,128]{1,0:T(8,128)S(1)}, u32[]{:S(2)}, u32[]{:S(2)}) collective-permute-start(f32[64,128]{1,0:T(8,128)S(1)} %constant_dynamic-slice_fusion.8), channel_id=1, source_target_pairs={{0,8},{8,0},{16,24},{24,16},{32,40},{40,32},{48,56},{56,48},{1,9},... | collective-permute-start | bytes 98312 | tf_op jit(solution)/shard_map/ppermute | solution.py:375
  243.3 38.5 %collective-permute-start.9 = (f32[8,128]{1,0:T(8,128)S(1)}, f32[8,128]{1,0:T(8,128)S(1)}, u32[]{:S(2)}, u32[]{:S(2)}) collective-permute-start(f32[8,128]{1,0:T(8,128)S(1)} %get-tuple-element.48), channel_id=1, source_target_pairs={{0,7},{1,0},{2,1},{3,2},{4,3},{5,4},{6,5},{7,6},{8,15},{9,8},{10,9... | collective-permute-start | bytes 12296 | tf_op jit(solution)/shard_map/ppermute | solution.py:397
  245.5 36.3 %collective-permute-start.8 = (f32[8,128]{1,0:T(8,128)S(1)}, f32[8,128]{1,0:T(8,128)S(1)}, u32[]{:S(2)}, u32[]{:S(2)}) collective-permute-start(f32[8,128]{1,0:T(8,128)S(1)} %get-tuple-element.49), channel_id=1, source_target_pairs={{0,6},{1,7},{2,0},{3,1},{4,2},{5,3},{6,4},{7,5},{8,14},{9,15},{10,... | collective-permute-start | bytes 12296 | tf_op jit(solution)/shard_map/ppermute | solution.py:397
  249.5 34.2 %collective-permute-start.7 = (f32[8,128]{1,0:T(8,128)S(1)}, f32[8,128]{1,0:T(8,128)S(1)}, u32[]{:S(2)}, u32[]{:S(2)}) collective-permute-start(f32[8,128]{1,0:T(8,128)S(1)} %get-tuple-element.50), channel_id=1, source_target_pairs={{0,5},{1,6},{2,7},{3,0},{4,1},{5,2},{6,3},{7,4},{8,13},{9,14},{10,... | collective-permute-start | bytes 12296 | tf_op jit(solution)/shard_map/ppermute | solution.py:397
  250.2 34.1 %collective-permute-start.6 = (f32[8,128]{1,0:T(8,128)S(1)}, f32[8,128]{1,0:T(8,128)S(1)}, u32[]{:S(2)}, u32[]{:S(2)}) collective-permute-start(f32[8,128]{1,0:T(8,128)S(1)} %get-tuple-element.51), channel_id=1, source_target_pairs={{0,4},{1,5},{2,6},{3,7},{4,0},{5,1},{6,2},{7,3},{8,12},{9,13},{10,... | collective-permute-start | bytes 12296 | tf_op jit(solution)/shard_map/ppermute | solution.py:397
  252.7 31.6 %collective-permute-start.5 = (f32[8,128]{1,0:T(8,128)S(1)}, f32[8,128]{1,0:T(8,128)S(1)}, u32[]{:S(2)}, u32[]{:S(2)}) collective-permute-start(f32[8,128]{1,0:T(8,128)S(1)} %get-tuple-element.52), channel_id=1, source_target_pairs={{0,3},{1,4},{2,5},{3,6},{4,7},{5,0},{6,1},{7,2},{8,11},{9,12},{10,... | collective-permute-start | bytes 12296 | tf_op jit(solution)/shard_map/ppermute | solution.py:397
  281.8 4.9 %collective-permute-start.4 = (f32[8,128]{1,0:T(8,128)S(1)}, f32[8,128]{1,0:T(8,128)S(1)}, u32[]{:S(2)}, u32[]{:S(2)}) collective-permute-start(f32[8,128]{1,0:T(8,128)S(1)} %get-tuple-element.53), channel_id=1, source_target_pairs={{0,2},{1,3},{2,4},{3,5},{4,6},{5,7},{6,0},{7,1},{8,10},{9,11},{10,... | collective-permute-start | bytes 12296 | tf_op jit(solution)/shard_map/ppermute | solution.py:397
  281.8 4.9 %collective-permute-start.3 = (f32[8,128]{1,0:T(8,128)S(1)}, f32[8,128]{1,0:T(8,128)S(1)}, u32[]{:S(2)}, u32[]{:S(2)}) collective-permute-start(f32[8,128]{1,0:T(8,128)S(1)} %get-tuple-element.47), channel_id=1, source_target_pairs={{0,1},{1,2},{2,3},{3,4},{4,5},{5,6},{6,7},{7,0},{8,9},{9,10},{10,1... | collective-permute-start | bytes 12296 | tf_op jit(solution)/shard_map/ppermute | solution.py:397
  311.1 5.3 %collective-permute-start.10 = (f32[64,8,128]{2,1,0:T(8,128)S(1)}, f32[64,8,128]{2,1,0:T(8,128)}, u32[]{:S(2)}, u32[]{:S(2)}) collective-permute-start(f32[64,8,128]{2,1,0:T(8,128)S(1)} %all_to_all.20), channel_id=1, source_target_pairs={{0,128},{64,192},{128,0},{192,64},{1,129},{65,193},{129,1},{193,65... | collective-permute-start | bytes 786440 | tf_op jit(solution)/shard_map/ppermute | solution.py:380
  318.3 14.2 %collective-permute-start.11 = (f32[2,64,8,128]{3,2,1,0:T(8,128)}, f32[2,64,8,128]{3,2,1,0:T(8,128)}, u32[]{:S(2)}, u32[]{:S(2)}) collective-permute-start(f32[2,64,8,128]{3,2,1,0:T(8,128)} %maximum_select_fusion.2), channel_id=1, source_target_pairs={{0,64},{64,0},{128,192},{192,128},{1,65},{65,1},{129,193},{193,129... | collective-permute-start | bytes 1572872 | tf_op jit(solution)/shard_map/ppermute | solution.py:380
  (16 other events, 14.7 us)

commit v3 on v2

--- a/solution.py
+++ b/solution.py
@@ -17,6 +17,7 @@
 KZ = 16
 C = 384
 HALF = BS // 2
+PART = HALF // 2
 CELLS = 64
 STEP = 8
 GROUPS = 64 // STEP
@@ -25,8 +26,9 @@
 SHRINK = 0.25
 f32 = jnp.float32
 bf16 = jnp.bfloat16
-BIG = pltpu.CompilerParams(vmem_limit_bytes=26 * 1024 * 1024)
-SPECTRAL = jax.ShapeDtypeStruct((64, 2, HALF, 128), f32)
+BIG = pltpu.CompilerParams(vmem_limit_bytes=62 * 1024 * 1024)
+SPECTRAL = (64, 2 * HALF, 128)
+PARTIAL = (64, 2 * PART, 128)
 GROUPED = jax.ShapeDtypeStruct((GROUPS, 2 * BS, WIDE), f32)
 
 
@@ -123,66 +125,73 @@
     return out_re, out_im
 
 
-def plane_stage_one(src_ref, dst_ref, sign):
+def read(ref, index, tile):
+    half = ref.shape[1] // 2
+    rows = slice(tile * 8, tile * 8 + 8), slice(half + tile * 8, half + tile * 8 + 8)
+    return ref[index, rows[0], :], ref[index, rows[1], :]
+
+
+def write(ref, index, tile, re, im):
+    half = ref.shape[1] // 2
+    ref[index, tile * 8 : tile * 8 + 8, :] = re
+    ref[index, half + tile * 8 : half + tile * 8 + 8, :] = im
+
+
+def senders(src_ref, dst_ref, sign, before, after):
+    def body(p, carry):
+        before(p)
+        for tile in range(src_ref.shape[1] // 16):
+            re, im = zip(*[read(src_ref, p * 8 + n, tile) for n in range(8)])
+            re, im = fft(re, im, sign)
+            for n in range(8):
+                write(dst_ref, p * 8 + n, tile, re[n], im[n])
+        after(p)
+        return carry
+
+    lax.fori_loop(0, 8, body, 0)
+
+
+def turned(a, b, twiddle_ref, index, sign):
+    c = twiddle_ref[index, 0:1, :]
+    s = twiddle_ref[index, 1:2, :] * sign
+    return a * c - b * s, a * s + b * c
+
+
+def plane_forward(src_ref, work_ref, twiddle_ref, before):
+    senders(src_ref, work_ref, -1.0, before, lambda p: None)
+
     def body(p, carry):
         for tile in range(HALF // 8):
-            rows = slice(tile * 8, tile * 8 + 8)
-            re = [src_ref[p * 8 + n, 0, rows, :] for n in range(8)]
-            im = [src_ref[p * 8 + n, 1, rows, :] for n in range(8)]
-            re, im = fft(re, im, sign)
-            for n in range(8):
-                dst_ref[p * 8 + n, 0, rows, :] = re[n]
-                dst_ref[p * 8 + n, 1, rows, :] = im[n]
-        return carry
-
-    lax.fori_loop(0, 8, body, 0)
-
-
-def plane_forward(src_ref, work_ref, twiddle_ref):
-    plane_stage_one(src_ref, work_ref, -1.0)
-
-    def body(p, carry):
-        for tile in range(HALF // 8):
-            rows = slice(tile * 8, tile * 8 + 8)
-            re = [work_ref[n * 8 + p, 0, rows, :] for n in range(8)]
-            im = [work_ref[n * 8 + p, 1, rows, :] for n in range(8)]
+            re, im = zip(*[read(work_ref, n * 8 + p, tile) for n in range(8)])
             re, im = fft(re, im, -1.0)
             for n in range(8):
-                c = twiddle_ref[n * 8 + p, 0:1, :]
-                s = twiddle_ref[n * 8 + p, 1:2, :]
-                work_ref[n * 8 + p, 0, rows, :] = re[n] * c - im[n] * s
-                work_ref[n * 8 + p, 1, rows, :] = re[n] * s + im[n] * c
+                write(work_ref, n * 8 + p, tile, *turned(re[n], im[n], twiddle_ref, n * 8 + p, 1.0))
         return carry
 
     lax.fori_loop(0, 8, body, 0)
 
 
-def plane_backward(work_ref, out_ref, twiddle_ref):
+def plane_backward(work_ref, out_ref, twiddle_ref, after):
     def body(p, carry):
-        for tile in range(HALF // 8):
-            rows = slice(tile * 8, tile * 8 + 8)
-            re = []
-            im = []
+        for tile in range(PART // 8):
+            pairs = [
+                turned(*read(work_ref, n * 8 + p, tile), twiddle_ref, n * 8 + p, -1.0)
+                for n in range(8)
+            ]
+            re, im = fft(*zip(*pairs), 1.0)
             for n in range(8):
-                c = twiddle_ref[n * 8 + p, 0:1, :]
-                s = twiddle_ref[n * 8 + p, 1:2, :]
-                a = work_ref[n * 8 + p, 0, rows, :]
-                b = work_ref[n * 8 + p, 1, rows, :]
-                re.append(a * c + b * s)
-                im.append(b * c - a * s)
-            re, im = fft(re, im, 1.0)
-            for n in range(8):
-                work_ref[n * 8 + p, 0, rows, :] = re[n]
-                work_ref[n * 8 + p, 1, rows, :] = im[n]
+                write(work_ref, n * 8 + p, tile, re[n], im[n])
         return carry
 
     lax.fori_loop(0, 8, body, 0)
-    plane_stage_one(work_ref, out_ref, 1.0)
+    senders(work_ref, out_ref, 1.0, lambda p: None, after)
 
 
 def load_group(work_ref, group, high_ref, low_ref):
     rows = [
-        jnp.concatenate([work_ref[group * STEP + n, 0], work_ref[group * STEP + n, 1]], axis=1)
+        jnp.concatenate(
+            [work_ref[group * STEP + n, :HALF], work_ref[group * STEP + n, HALF:]], axis=1
+        )
         for n in range(STEP)
     ]
     values = dot3(split(jnp.concatenate(rows, axis=0)), (high_ref[...], low_ref[...]))
@@ -203,7 +212,10 @@
     for pair in range(STEP // 2):
         part = spectral[:, pair * 128 : (pair + 1) * 128]
         parts = [
-            swap(part[q * BS : q * BS + HALF], part[q * BS + HALF : (q + 1) * BS])
+            swap(
+                part[2 * q * PART : (2 * q + 1) * PART],
+                part[(2 * q + 1) * PART : (2 * q + 2) * PART],
+            )
             for q in range(2)
         ]
         for n in range(2):
@@ -211,29 +223,43 @@
     values = dot3(split(jnp.concatenate(rows, axis=0)), (high_ref[...], low_ref[...]))
     for n in range(STEP):
         for q in range(2):
-            work_ref[group * STEP + n, q] = values[
-                n * HALF : (n + 1) * HALF, q * 128 : (q + 1) * 128
+            work_ref[group * STEP + n, q * PART : (q + 1) * PART] = values[
+                n * PART : (n + 1) * PART, q * 128 : (q + 1) * 128
             ]
 
 
-def depth_kernel(field_ref, both_ref, out_ref, work_ref):
+def depth_kernel(field_hbm, both_hbm, out_hbm, field_ref, both_ref, out_ref, work_ref, sems, out_sems):
+    table = pltpu.make_async_copy(both_hbm, both_ref, sems.at[8])
+    table.start()
+    copies = []
     for g in range(8):
+        span = pl.ds(g * 256, 256)
+        copies.append(pltpu.make_async_copy(field_hbm.at[span], field_ref.at[span], sems.at[g]))
+        copies[-1].start()
+    table.wait()
+    for g in range(8):
+        copies[g].wait()
         values = dot(both_ref[...], field_ref[g * 256 : (g + 1) * 256, :])
         values = values[:256] + values[256:]
         work_ref[:, g * 8 : (g + 1) * 8, :] = values.reshape(2 * KZ, 8, C)
+    sends = []
     for k in range(KZ):
         values = work_ref[2 * k : 2 * k + 2].reshape(2 * CELLS, C).T
         for b in range(NB):
             upper = values[b * BS : b * BS + HALF]
             lower = values[b * BS + HALF : (b + 1) * BS]
-            out_ref[b * KZ + k, 0], out_ref[b * KZ + k, 1] = swap(upper, lower)
+            out_ref[b, k, :HALF], out_ref[b, k, HALF:] = swap(upper, lower)
+        sends.append(pltpu.make_async_copy(out_ref.at[:, k], out_hbm.at[:, k], out_sems.at[k]))
+        sends[-1].start()
+    for send in sends:
+        send.wait()
 
 
 def forward_kernel(
     doubling_ref, src_ref, twiddle_ref, th_ref, tl_ref, w1, b1, w2, b2,
     spec_ref, outer_ref, slope_ref, square_ref, work_ref,
 ):
-    plane_forward(src_ref, work_ref, twiddle_ref)
+    plane_forward(src_ref, work_ref, twiddle_ref, lambda p: None)
     root = math.sqrt(2.0 / math.pi)
 
     def body(g, carry):
@@ -255,23 +281,63 @@
     lax.fori_loop(0, GROUPS, body, 0)
 
 
+def block_of(hbm, ref, sems, p):
+    span = pl.ds(p * 8, 8)
+    return pltpu.make_async_copy(hbm.at[span], ref.at[span], sems.at[p])
+
+
 def backward_kernel(
+    src_hbm, twiddle_hbm, th_hbm, tl_hbm, bh_hbm, bl_hbm, w1_hbm, w2_hbm, slope_hbm, square_hbm,
+    two_hbm, one_hbm, out_hbm,
     src_ref, twiddle_ref, th_ref, tl_ref, bh_ref, bl_ref, w1, w2, slope_ref, square_ref,
-    two_ref, one_ref, out_ref, work_ref,
+    two_ref, one_ref, out_ref, work_ref, part_ref, src_sems, sems, two_sems, one_sems, out_sems,
 ):
-    plane_forward(src_ref, work_ref, twiddle_ref)
+    for p in range(8):
+        block_of(src_hbm, src_ref, src_sems, p).start()
+    pairs = (
+        (twiddle_hbm, twiddle_ref), (th_hbm, th_ref), (tl_hbm, tl_ref), (square_hbm, square_ref),
+        (w2_hbm, w2), (slope_hbm, slope_ref), (w1_hbm, w1), (bh_hbm, bh_ref), (bl_hbm, bl_ref),
+    )
+    loads = [pltpu.make_async_copy(a, b, sems.at[n]) for n, (a, b) in enumerate(pairs)]
+    for load in loads:
+        load.start()
+    loads[0].wait()
+    plane_forward(
+        src_ref, work_ref, twiddle_ref, lambda p: block_of(src_hbm, src_ref, src_sems, p).wait()
+    )
+    for load in loads[1:]:
+        load.wait()
 
     def body(g, carry):
         grad_two = load_group(work_ref, g, th_ref, tl_ref) * square_ref[g]
         two_ref[g] = grad_two
+        pltpu.make_async_copy(two_ref.at[g], two_hbm.at[g], two_sems.at[g]).start()
         grad_one = product(w2, grad_two) * slope_ref[g]
         one_ref[g] = grad_one
-        grad_spec = product(w1, grad_one)
-        store_group(work_ref, g, grad_spec, bh_ref, bl_ref)
+        pltpu.make_async_copy(one_ref.at[g], one_hbm.at[g], one_sems.at[g]).start()
+        store_group(part_ref, g, product(w1, grad_one), bh_ref, bl_ref)
         return carry
 
     lax.fori_loop(0, GROUPS, body, 0)
-    plane_backward(work_ref, out_ref, twiddle_ref)
+    plane_backward(
+        part_ref, out_ref, twiddle_ref, lambda p: block_of(out_ref, out_hbm, out_sems, p).start()
+    )
+    for g in range(GROUPS):
+        pltpu.make_async_copy(two_ref.at[g], two_hbm.at[g], two_sems.at[g]).wait()
+        pltpu.make_async_copy(one_ref.at[g], one_hbm.at[g], one_sems.at[g]).wait()
+    for p in range(8):
+        block_of(out_ref, out_hbm, out_sems, p).wait()
+
+
+def rest_kernel(one_ref, twiddle_ref, bh_ref, bl_ref, w1, out_ref, part_ref, plane_ref):
+    def body(g, carry):
+        store_group(part_ref, g, product(w1, one_ref[g]), bh_ref, bl_ref)
+        return carry
+
+    lax.fori_loop(0, GROUPS, body, 0)
+    plane_backward(part_ref, plane_ref, twiddle_ref, lambda p: None)
+    out_ref[:, : 2 * PART, :] = plane_ref[...]
+    out_ref[:, 2 * PART :, :] = jnp.zeros((64, 8, 128), f32)
 
 
 def spread(value):
@@ -310,33 +376,79 @@
     out_ref[4 * BS : 4 * BS + 8] = biases * norm
 
 
-def field_kernel(src_ref, cotangent_ref, high_ref, low_ref, out_ref, work_ref):
+def field_kernel(
+    first_hbm, second_hbm, cotangent_hbm, high_hbm, low_hbm, out_hbm,
+    first_ref, second_ref, cotangent_ref, high_ref, low_ref, out_ref, work_ref,
+    first_sems, second_sems, sems, out_sems,
+):
+    loads = []
     for k in range(KZ):
+        span = pl.ds(0, 2 * PART)
+        loads.append(
+            (
+                pltpu.make_async_copy(first_hbm.at[:, k], first_ref.at[:, k], first_sems.at[k]),
+                pltpu.make_async_copy(
+                    second_hbm.at[:, k, span], second_ref.at[:, k], second_sems.at[k]
+                ),
+            )
+        )
+    pairs = ((high_hbm, high_ref), (low_hbm, low_ref), (cotangent_hbm, cotangent_ref))
+    others = [pltpu.make_async_copy(a, b, sems.at[n]) for n, (a, b) in enumerate(pairs)]
+    for load in loads:
+        load[0].start()
+        load[1].start()
+    for load in others:
+        load.start()
+    for k in range(KZ):
+        loads[k][0].wait()
+        loads[k][1].wait()
         parts = []
         for b in range(NB):
-            parts.extend(swap(src_ref[b * KZ + k, 0], src_ref[b * KZ + k, 1]))
+            left = swap(first_ref[b, k, :PART], first_ref[b, k, PART:])
+            right = swap(second_ref[b, k, :PART], second_ref[b, k, PART:])
+            parts.extend([left[0], right[0], left[1], right[1]])
         values = jnp.concatenate(parts, axis=0).T
         work_ref[2 * k : 2 * k + 2] = values.reshape(2, CELLS, C)
+    for load in others:
+        load.wait()
     both = jnp.concatenate([high_ref[...], low_ref[...]], axis=0)
+    sends = []
     for g in range(8):
         high, low = split(work_ref[:, g * 8 : (g + 1) * 8, :].reshape(256, C))
         values = dot(both, high)
         values = values[:256] + values[256:] + dot(high_ref[...], low)
         span = slice(g * 256, (g + 1) * 256)
         out_ref[span, :] = (cotangent_ref[span, :].astype(f32) + values).astype(bf16)
+        rows = pl.ds(g * 256, 256)
+        sends.append(pltpu.make_async_copy(out_ref.at[rows], out_hbm.at[rows], out_sems.at[g]))
+        sends[-1].start()
+    for send in sends:
+        send.wait()
 
 
 def vmem(n):
     return [pl.BlockSpec(memory_space=pltpu.VMEM)] * n
 
 
-def call(kernel, out_shape, args, scratch, flops, moved):
+def free(n):
+    return [pl.BlockSpec(memory_space=pl.ANY)] * n
+
+
+def held(*values):
+    return [pltpu.VMEM(v.shape, v.dtype) for v in values]
+
+
+def sems(*counts):
+    return [pltpu.SemaphoreType.DMA((n,)) for n in counts]
+
+
+def call(kernel, out_shape, args, scratch, flops, moved, place=vmem):
     outs = len(out_shape) if isinstance(out_shape, tuple) else 1
     return pl.pallas_call(
         kernel,
         out_shape=out_shape,
-        in_specs=vmem(len(args)),
-        out_specs=tuple(vmem(outs)) if isinstance(out_shape, tuple) else vmem(1)[0],
+        in_specs=place(len(args)),
+        out_specs=tuple(place(outs)) if isinstance(out_shape, tuple) else place(1)[0],
         scratch_shapes=scratch,
         compiler_params=BIG,
         cost_estimate=pl.CostEstimate(flops=flops, bytes_accessed=moved, transcendentals=0),
@@ -344,14 +456,53 @@
 
 
 def depth_forward(field, tables):
+    args = (field.reshape(2048, C), np.concatenate(tables, axis=0))
+    out = jax.ShapeDtypeStruct((NB, KZ, 2 * HALF, 128), f32)
+    scratch = [*held(*args, out), pltpu.VMEM((2 * KZ, CELLS, C), f32), *sems(9, KZ)]
+    return call(depth_kernel, out, args, scratch, 800_000_000, 5_000_000, free).reshape(SPECTRAL)
+
+
+def backward(cot_spec, twiddle, plane_fwd, plane_bwd, first, second, slope, square):
+    args = (cot_spec, twiddle, *plane_fwd, *plane_bwd, first, second, slope, square)
+    outs = (GROUPED, GROUPED, jax.ShapeDtypeStruct(PARTIAL, f32))
+    scratch = [
+        *held(*args, *outs),
+        pltpu.VMEM(SPECTRAL, f32),
+        pltpu.VMEM(PARTIAL, f32),
+        *sems(8, 9, GROUPS, GROUPS, 8),
+    ]
+    return call(backward_kernel, outs, args, scratch, 10_000_000_000, 20_000_000, free)
+
+
+def rest(grad_one, twiddle, plane_bwd, first):
     return call(
-        depth_kernel,
-        SPECTRAL,
-        (field.reshape(2048, C), np.concatenate(tables, axis=0)),
-        [pltpu.VMEM((2 * KZ, CELLS, C), f32)],
-        800_000_000,
+        rest_kernel,
+        jax.ShapeDtypeStruct((64, 2 * PART + 8, 128), f32),
+        (grad_one, twiddle, *plane_bwd, first),
+        [pltpu.VMEM(PARTIAL, f32), pltpu.VMEM(PARTIAL, f32)],
+        3_000_000_000,
         5_000_000,
     )
+
+
+def field(first, second, cotangent, tables):
+    args = (
+        first.reshape(NB, KZ, 2 * PART, 128),
+        second.reshape(NB, KZ, 2 * PART + 8, 128),
+        cotangent.reshape(2048, C),
+        *tables,
+    )
+    out = jax.ShapeDtypeStruct((2048, C), bf16)
+    scratch = [
+        *held(args[0], args[0], *args[2:], out),
+        pltpu.VMEM((2 * KZ, CELLS, C), f32),
+        *sems(KZ, KZ, 3, 8),
+    ]
+    return call(field_kernel, out, args, scratch, 1_200_000_000, 7_000_000, free)
+
+
+def rows_of(weight, part):
+    return weight.reshape(4, 2, PART, 2 * BS)[:, part].reshape(BS, 2 * BS)
 
 
 def mixing(weight):
@@ -381,26 +532,27 @@
     return jnp.where(bit == 0, jnp.stack([value, other]), jnp.stack([other, value]))
 
 
-def total_rows(rows, grad_cells):
+def owned_rows(rows):
     dp = lax.axis_index("dp")
     px = lax.axis_index("px")
     py = lax.axis_index("py")
-    core = dp % 2
-    low = dp // 2
-    rows = keep_half(rows, "dp", 1, core)
-    rows = keep_half(rows, "dp", 2, low)
+    rows = keep_half(rows, "dp", 1, dp % 2)
+    rows = keep_half(rows, "dp", 2, dp // 2)
     rows = keep_half(rows, "px", 1, px % 2)
     pieces = rows.reshape(8, -1, 128)
     total = lax.dynamic_index_in_dim(pieces, py, 0, keepdims=False)
     for offset in range(1, 8):
         piece = lax.dynamic_index_in_dim(pieces, (py + offset) % 8, 0, keepdims=False)
         total = total + lax.ppermute(piece, "py", [(n, (n + offset) % 8) for n in range(8)])
-    total, grad_cells = lax.optimization_barrier((total, grad_cells))
-    total = exchange(jnp.broadcast_to(total[None], (64, *total.shape)))
-    total = join_half(total, "dp", 2, low)
-    total = join_half(total, "dp", 1, core)
+    return total
+
+
+def every_row(total):
+    dp = lax.axis_index("dp")
+    total = join_half(total, "dp", 2, dp // 2)
+    total = join_half(total, "dp", 1, dp % 2)
     total = total.reshape(2, 2, NB, 2, 8, ROWS // 64, 128)
-    return total.transpose(2, 0, 1, 3, 4, 5, 6).reshape(NB, ROWS, 128), grad_cells
+    return total.transpose(2, 0, 1, 3, 4, 5, 6).reshape(NB, ROWS, 128)
 
 
 def exchange(value):
@@ -427,23 +579,24 @@
         out_shape=(GROUPED,) * 4,
         in_specs=[pl.BlockSpec(memory_space=pltpu.SMEM)] + vmem(8),
         out_specs=tuple(vmem(4)),
-        scratch_shapes=[pltpu.VMEM((64, 2, HALF, 128), f32)],
+        scratch_shapes=[pltpu.VMEM(SPECTRAL, f32)],
         compiler_params=BIG,
         cost_estimate=pl.CostEstimate(
             flops=8_000_000_000, bytes_accessed=16_000_000, transcendentals=1_500_000
         ),
     )(doubling, state_spec, twiddle, *plane_fwd, stacked(first), bias_one, stacked(second), bias_two)
 
-    grad_two, grad_one, grad_plane = call(
-        backward_kernel,
-        (GROUPED, GROUPED, SPECTRAL),
-        (cot_spec, twiddle, *plane_fwd, *plane_bwd, stacked(first.T), stacked(second.T), slope, square),
-        [pltpu.VMEM((64, 2, HALF, 128), f32)],
-        10_000_000_000,
-        20_000_000,
-    )
-    grad_cells = exchange(grad_plane)
-
+    grad_two, grad_one, plane = backward(
+        cot_spec,
+        twiddle,
+        plane_fwd,
+        plane_bwd,
+        stacked(rows_of(first.T, 0)),
+        stacked(second.T),
+        slope,
+        square,
+    )
+    first_part = exchange(plane)
     rows = call(
         table_kernel,
         jax.ShapeDtypeStruct((ROWS, 128), f32),
@@ -452,19 +605,19 @@
         4_000_000_000,
         13_000_000,
     )
-    rows, grad_cells = total_rows(rows, grad_cells)
+    rows = owned_rows(rows)
+    plane = rest(grad_one, twiddle, plane_bwd, stacked(rows_of(first.T, 1)))
+    plane = lax.dynamic_update_slice(
+        plane, jnp.broadcast_to(rows[None], (64, *rows.shape)), (0, 2 * PART, 0)
+    )
+    first_part, plane = lax.optimization_barrier((first_part, plane))
+    second_part = exchange(plane)
+    rows = every_row(second_part[:, 2 * PART :])
     grads_one = rows[:, : 2 * BS, :BS].reshape(NB, 2, BS, BS).transpose(1, 0, 2, 3)
     grads_two = rows[:, 2 * BS : 4 * BS, :BS].reshape(NB, 2, BS, BS).transpose(1, 0, 2, 3)
     biases = rows[:, 4 * BS : 4 * BS + 4, :BS].reshape(NB, 2, 2, BS)
 
-    state_grad = call(
-        field_kernel,
-        jax.ShapeDtypeStruct((2048, C), bf16),
-        (grad_cells, cotangent.reshape(2048, C), *depth_bwd),
-        [pltpu.VMEM((2 * KZ, CELLS, C), f32)],
-        1_200_000_000,
-        7_000_000,
-    ).reshape(1, 8, 8, NZ, C)
+    state_grad = field(first_part, second_part, cotangent, depth_bwd).reshape(1, 8, 8, NZ, C)
     return (
         state_grad,
         grads_one,

time: 338 us -> 330 us (0.976)
  local copies, waits for them, and re-layouts: 47.5 us -> 10.4 us
  waiting for transfers between devices: 145 us -> 119 us
  Pallas kernels: 50.7 us -> 75.1 us
  blocking collectives: 24.4 us -> 47 us
  starting transfers between devices: 60.5 us -> 67.8 us
    unnamed x70 -> x12, local copies, waits for them, and re-layouts: 41.8 us -> 3.68 us
    ppermute x7, waiting for transfers between devices: 31.4 us -> 0.02 us  [owned_rows(): lax.ppermute(piece, 'py', [(n, (n + offset) % 8) for n in range(8)])]
    all_to_all x1, blocking collectives: 24.4 us -> 47 us  [exchange(): lax.all_to_all(value, ('px', 'py'), split_axis=0, concat_axis=0, tiled=True)]
    pallas_call x5 -> x6, Pallas kernels: 36.5 us -> 56.9 us  [call(): pl.pallas_call(kernel, out_shape=out_shape, in_specs=place(len(args)), ou...]
    all_to_all x3, waiting for transfers between devices: 102 us -> 107 us  [exchange(): lax.all_to_all(value, ('px', 'py'), split_axis=0, concat_axis=0, tiled=True)]
    pallas_call x1, Pallas kernels: 14.1 us -> 18.1 us  [shards(): pl.pallas_call(forward_kernel, out_shape=(GROUPED,) * 4, in_specs=[pl.Blo...]
  transfers between devices with their start and end apart: 15 -> 15, of which waited for: 9 -> 6; matrix products, arithmetic and copies ran while one was open for 3% -> 4% of each run, Pallas kernels for 9% -> 15%
where the time goes in v3:
time: 330 us; the launch traced here: 329 us
  waiting for transfers between devices  119 us (36%)
  Pallas kernels  75.1 us (23%)
  starting transfers between devices  67.8 us (21%)
  blocking collectives  47 us (14%)
  local copies, waits for them, and re-layouts  10.4 us (3%)
  other arithmetic  8.44 us (3%)
    all_to_all x3, waiting for transfers between devices, exchange(): lax.all_to_all(value, ('px', 'py'), split_axis=0, concat_axis=0, tiled=True)  107 us
    pallas_call x6, Pallas kernels, call(): pl.pallas_call(kernel, out_shape=out_shape, in_specs=place(len(args)), ou...  56.9 us
    all_to_all x1, blocking collectives, exchange(): lax.all_to_all(value, ('px', 'py'), split_axis=0, concat_axis=0, tiled=True)  47 us
    all_to_all x3, starting transfers between devices, exchange(): lax.all_to_all(value, ('px', 'py'), split_axis=0, concat_axis=0, tiled=True)  37.1 us
    pallas_call x1, Pallas kernels, shards(): pl.pallas_call(forward_kernel, out_shape=(GROUPED,) * 4, in_specs=[pl.Blo...  18.1 us
    ppermute x7, starting transfers between devices, owned_rows(): lax.ppermute(piece, 'py', [(n, (n + offset) % 8) for n in range(8)])  15 us
    ppermute x2, starting transfers between devices, join_half(): other = lax.ppermute(value, axis, [(n, n ^ flip) for n in range(size)])  9.36 us
    ppermute x3, waiting for transfers between devices, keep_half(): lax.ppermute(other, axis, [(n, n ^ flip) for n in range(size)])  6.64 us
  transfers between devices with their start and end apart: 15, of which 6 were waited for; matrix products, arithmetic and copies ran while one was open for 4% of the time, Pallas kernels for 15%

profile of v3, /device:TPU:1, one launch (start us, length us, event | category | flops | bytes accessed | tf_op | source)
XLA Modules:
  0.0 328.9 jit_solution(9482893974093350738)
XLA Ops:
  0.6 6.4 %shard_map.183 = f32[4,16,96,128]{3,2,1,0:T(8,128)} custom-call(bf16[2048,384]{1,0:T(8,128)(2,1)} %bitcast.105, bf16[512,256]{1,0:T(8,128)(2,1)} %constant.167.clone.both_hbm), custom_call_target="tpu_custom_call" | custom-call | flops 800000000 | bytes 5000000 | tf_op jit(solution)/shard_map/pallas_call | solution.py:447
  7.0 15.4 %all-to-all-start.1 = ((f32[64,96,128]{2,1,0:T(8,128)}), f32[64,96,128]{2,1,0:T(8,128)}, u32[]{:S(2)}, u32[]{:S(2)}) async-start(f32[64,96,128]{2,1,0:T(8,128)} %bitcast.99), calls=%async_computation.1 | async-start | bytes 6291456 | tf_op jit(solution)/shard_map/all_to_all | solution.py:559
  22.4 6.4 %shard_map.182 = f32[4,16,96,128]{3,2,1,0:T(8,128)} custom-call(bf16[2048,384]{1,0:T(8,128)(2,1)} %bitcast.101, bf16[512,256]{1,0:T(8,128)(2,1)} %constant.167.clone.both_hbm), custom_call_target="tpu_custom_call" | custom-call | flops 800000000 | bytes 5000000 | tf_op jit(solution)/shard_map/pallas_call | solution.py:447
  28.8 63.8 %all-to-all-done.1.src_ref = f32[64,96,128]{2,1,0:T(8,128)} async-done(((f32[64,96,128]{2,1,0:T(8,128)}), f32[64,96,128]{2,1,0:T(8,128)}, u32[]{:S(2)}, u32[]{:S(2)}) %all-to-all-start.1) | async-done | bytes 3145760 | tf_op jit(solution)/shard_map/all_to_all | solution.py:559
  92.6 11.1 %all-to-all-start = ((f32[64,96,128]{2,1,0:T(8,128)}), f32[64,96,128]{2,1,0:T(8,128)}, u32[]{:S(2)}, u32[]{:S(2)}) async-start(f32[64,96,128]{2,1,0:T(8,128)} %bitcast.98), calls=%async_computation | async-start | bytes 6291456 | tf_op jit(solution)/shard_map/all_to_all | solution.py:559
  112.2 18.1 %shard_map.184 = (f32[8,192,512]{2,1,0:T(8,128)}, f32[8,192,512]{2,1,0:T(8,128)}, f32[8,192,512]{2,1,0:T(8,128)}, f32[8,192,512]{2,1,0:T(8,128)}) custom-call(f32[1,1]{1,0:T(1,128)} %bitcast.18.doubling_ref, f32[64,96,128]{2,1,0:T(8,128)} %all-to-all-done.1.src_ref, f32[64,2,128]{2,1,0:T(2,128)} %constant.168.clone.twiddle_ref.twiddle_hbm, ...), custom_call_target="tpu_custom_call" | custom-call | flops 8000000000 | bytes 16000000 | tf_op jit(solution)/shard_map/pallas_call | solution.py:577
  130.4 43.3 %all-to-all-done.src_hbm = f32[64,96,128]{2,1,0:T(8,128)} async-done(((f32[64,96,128]{2,1,0:T(8,128)}), f32[64,96,128]{2,1,0:T(8,128)}, u32[]{:S(2)}, u32[]{:S(2)}) %all-to-all-start) | async-done | bytes 3145760 | tf_op jit(solution)/shard_map/all_to_all | solution.py:559
  173.7 17.8 %shard_map.185 = (f32[8,192,512]{2,1,0:T(8,128)}, f32[8,192,512]{2,1,0:T(8,128)}, f32[64,48,128]{2,1,0:T(8,128)}) custom-call(f32[64,96,128]{2,1,0:T(8,128)} %all-to-all-done.src_hbm, f32[64,2,128]{2,1,0:T(2,128)} %constant.168.clone.twiddle_ref.twiddle_hbm, bf16[256,256]{1,0:T(8,128)(2,1)} %constant.169.clone.th_ref.th_hbm, ...), custom_call_target="tpu_custom_call" | custom-call | flops 10000000000 | bytes 20000000 | tf_op jit(solution)/shard_map/pallas_call | solution.py:447
  191.5 10.6 %all-to-all-start.2 = ((f32[64,48,128]{2,1,0:T(8,128)}), f32[64,48,128]{2,1,0:T(8,128)}, u32[]{:S(2)}, u32[]{:S(2)}) async-start(f32[64,48,128]{2,1,0:T(8,128)} %get-tuple-element.16), calls=%async_computation.2 | async-start | bytes 3145728 | tf_op jit(solution)/shard_map/all_to_all | solution.py:559
  202.1 11.1 %shard_map.187 = f32[512,128]{1,0:T(8,128)} custom-call(f32[8,192,512]{2,1,0:T(8,128)} %get-tuple-element.18.spec_ref, f32[8,192,512]{2,1,0:T(8,128)} %get-tuple-element.19.outer_ref, f32[8,192,512]{2,1,0:T(8,128)} %get-tuple-element.17.one_ref, f32[8,192,512]{2,1,0:T(8,128)} %get-tuple-element.20.two_ref), custom_call_target="tpu_custom_call" | custom-call | flops 4000000000 | bytes 13000000 | tf_op jit(solution)/shard_map/pallas_call | solution.py:447
  213.2 0.9 constant_dynamic-slice_fusion.11
  214.1 2.2 collective-permute-start
  216.3 1.0 collective-permute-done
  217.3 0.9 dynamic-slice_add_fusion
  218.7 3.6 %collective-permute-done.1 = f32[128,128]{1,0:T(8,128)S(1)} collective-permute-done((f32[128,128]{1,0:T(8,128)S(1)}, f32[128,128]{1,0:T(8,128)S(1)}, u32[]{:S(2)}, u32[]{:S(2)}) %collective-permute-start.1) | collective-permute-done | bytes 65568 | tf_op jit(solution)/shard_map/ppermute | solution.py:526
  222.4 3.8 %collective-permute-start.2 = (f32[64,128]{1,0:T(8,128)S(1)}, f32[64,128]{1,0:T(8,128)S(1)}, u32[]{:S(2)}, u32[]{:S(2)}) collective-permute-start(f32[64,128]{1,0:T(8,128)S(1)} %constant_dynamic-slice_fusion.9), channel_id=1, source_target_pairs={{0,8},{8,0},{16,24},{24,16},{32,40},{40,32},{48,56},{56,48},{1,9},... | collective-permute-start | bytes 98312 | tf_op jit(solution)/shard_map/ppermute | solution.py:526
  226.2 2.0 collective-permute-done.2
  228.2 1.3 collective-permute-start.3
  229.4 1.4 collective-permute-start.4
  231.5 3.0 collective-permute-start.5
  234.6 1.0 collective-permute-start.6
  235.6 3.5 %collective-permute-start.7 = (f32[8,128]{1,0:T(8,128)S(1)}, f32[8,128]{1,0:T(8,128)S(1)}, u32[]{:S(2)}, u32[]{:S(2)}) collective-permute-start(f32[8,128]{1,0:T(8,128)S(1)} %get-tuple-element.52), channel_id=1, source_target_pairs={{0,5},{1,6},{2,7},{3,0},{4,1},{5,2},{6,3},{7,4},{8,13},{9,14},{10,... | collective-permute-start | bytes 12296 | tf_op jit(solution)/shard_map/ppermute | solution.py:546
  239.0 3.4 %collective-permute-start.8 = (f32[8,128]{1,0:T(8,128)S(1)}, f32[8,128]{1,0:T(8,128)S(1)}, u32[]{:S(2)}, u32[]{:S(2)}) collective-permute-start(f32[8,128]{1,0:T(8,128)S(1)} %get-tuple-element.51), channel_id=1, source_target_pairs={{0,6},{1,7},{2,0},{3,1},{4,2},{5,3},{6,4},{7,5},{8,14},{9,15},{10,... | collective-permute-start | bytes 12296 | tf_op jit(solution)/shard_map/ppermute | solution.py:546
  242.4 1.4 collective-permute-start.9
  243.8 8.2 %shard_map.186 = f32[64,56,128]{2,1,0:T(8,128)} custom-call(f32[8,192,512]{2,1,0:T(8,128)} %get-tuple-element.17.one_ref, f32[64,2,128]{2,1,0:T(2,128)} %constant.168.clone.twiddle_ref.twiddle_hbm, bf16[256,256]{1,0:T(8,128)(2,1)} %constant.171.clone.bh_hbm.bh_ref, bf16[256,256]{1,0:T(8,128)(2,1)} %constant.172.clone.bl_hbm.bl_ref, ...), custom_call_target="tpu_custom_call" | custom-call | flops 3000000000 | bytes 5000000 | tf_op jit(solution)/shard_map/pallas_call | solution.py:447
  252.8 47.0 %all_to_all.20 = f32[64,56,128]{2,1,0:T(8,128)S(1)} all-to-all(f32[64,56,128]{2,1,0:T(8,128)} %broadcast_dynamic-update-slice_fusion), channel_id=1, replica_groups=mesh['dp'=4,'px'=8,'py'=8] {'px','py'}, dimensions={0} | all-to-all | bytes 3670016 | tf_op jit(solution)/shard_map/all_to_all | solution.py:559
  301.2 5.6 %collective-permute-done.10 = f32[64,8,128]{2,1,0:T(8,128)S(1)} collective-permute-done((f32[64,8,128]{2,1,0:T(8,128)S(1)}, f32[64,8,128]{2,1,0:T(8,128)S(1)}, u32[]{:S(2)}, u32[]{:S(2)}) %collective-permute-start.10) | collective-permute-done | bytes 262176 | tf_op jit(solution)/shard_map/ppermute | solution.py:531
  306.8 0.9 maximum_select_fusion.2
  307.6 8.8 %collective-permute-start.11 = (f32[2,64,8,128]{3,2,1,0:T(8,128)}, f32[2,64,8,128]{3,2,1,0:T(8,128)}, u32[]{:S(2)}, u32[]{:S(2)}) collective-permute-start(f32[2,64,8,128]{3,2,1,0:T(8,128)} %maximum_select_fusion.2), channel_id=1, source_target_pairs={{0,64},{64,0},{128,192},{192,128},{1,65},{65,1},{129,193},{193,129... | collective-permute-start | bytes 1572872 | tf_op jit(solution)/shard_map/ppermute | solution.py:531
  316.4 7.1 %shard_map.188 = bf16[2048,384]{1,0:T(8,128)(2,1)} custom-call(f32[4,16,48,128]{3,2,1,0:T(8,128)} %bitcast.31.first_hbm, f32[4,16,56,128]{3,2,1,0:T(8,128)} %bitcast.100, bf16[2048,384]{1,0:T(8,128)(2,1)} %bitcast.102, bf16[256,256]{1,0:T(8,128)(2,1)} %constant.173.clone.high_hbm, bf16[256,256]{1,0:T(8,128)(2,1)} %constant.174.clone.low_hbm), custom_call_target="tpu_custom_call" | custom-call | flops 1200000000 | bytes 7000000 | tf_op jit(solution)/shard_map/pallas_call | solution.py:447
  323.5 1.3 maximum_select_fusion.1
  324.8 1.3 maximum_select_fusion
  (53 shorter events, 14.6 us)
Async XLA Ops:
  7.0 85.6 %all-to-all-start.1 = ((f32[64,96,128]{2,1,0:T(8,128)}), f32[64,96,128]{2,1,0:T(8,128)}, u32[]{:S(2)}, u32[]{:S(2)}) async-start(f32[64,96,128]{2,1,0:T(8,128)} %bitcast.99), calls=%async_computation.1 | async-start | bytes 6291456 | tf_op jit(solution)/shard_map/all_to_all | solution.py:559
  92.6 81.1 %all-to-all-start = ((f32[64,96,128]{2,1,0:T(8,128)}), f32[64,96,128]{2,1,0:T(8,128)}, u32[]{:S(2)}, u32[]{:S(2)}) async-start(f32[64,96,128]{2,1,0:T(8,128)} %bitcast.98), calls=%async_computation | async-start | bytes 6291456 | tf_op jit(solution)/shard_map/all_to_all | solution.py:559
  191.5 61.3 %all-to-all-start.2 = ((f32[64,48,128]{2,1,0:T(8,128)}), f32[64,48,128]{2,1,0:T(8,128)}, u32[]{:S(2)}, u32[]{:S(2)}) async-start(f32[64,48,128]{2,1,0:T(8,128)} %get-tuple-element.16), calls=%async_computation.2 | async-start | bytes 3145728 | tf_op jit(solution)/shard_map/all_to_all | solution.py:559
  214.1 3.2 collective-permute-start
  218.2 4.1 %collective-permute-start.1 = (f32[128,128]{1,0:T(8,128)S(1)}, f32[128,128]{1,0:T(8,128)S(1)}, u32[]{:S(2)}, u32[]{:S(2)}) collective-permute-start(f32[128,128]{1,0:T(8,128)S(1)} %constant_dynamic-slice_fusion.10), channel_id=1, source_target_pairs={{0,128},{64,192},{128,0},{192,64},{1,129},{65,193},{129,1},{193,65... | collective-permute-start | bytes 196616 | tf_op jit(solution)/shard_map/ppermute | solution.py:526
  222.4 5.8 %collective-permute-start.2 = (f32[64,128]{1,0:T(8,128)S(1)}, f32[64,128]{1,0:T(8,128)S(1)}, u32[]{:S(2)}, u32[]{:S(2)}) collective-permute-start(f32[64,128]{1,0:T(8,128)S(1)} %constant_dynamic-slice_fusion.9), channel_id=1, source_target_pairs={{0,8},{8,0},{16,24},{24,16},{32,40},{40,32},{48,56},{56,48},{1,9},... | collective-permute-start | bytes 98312 | tf_op jit(solution)/shard_map/ppermute | solution.py:526
  228.2 10.9 %collective-permute-start.3 = (f32[8,128]{1,0:T(8,128)S(1)}, f32[8,128]{1,0:T(8,128)S(1)}, u32[]{:S(2)}, u32[]{:S(2)}) collective-permute-start(f32[8,128]{1,0:T(8,128)S(1)} %get-tuple-element.49), channel_id=1, source_target_pairs={{0,1},{1,2},{2,3},{3,4},{4,5},{5,6},{6,7},{7,0},{8,9},{9,10},{10,1... | collective-permute-start | bytes 12296 | tf_op jit(solution)/shard_map/ppermute | solution.py:546
  229.4 13.0 %collective-permute-start.4 = (f32[8,128]{1,0:T(8,128)S(1)}, f32[8,128]{1,0:T(8,128)S(1)}, u32[]{:S(2)}, u32[]{:S(2)}) collective-permute-start(f32[8,128]{1,0:T(8,128)S(1)} %get-tuple-element.55), channel_id=1, source_target_pairs={{0,2},{1,3},{2,4},{3,5},{4,6},{5,7},{6,0},{7,1},{8,10},{9,11},{10,... | collective-permute-start | bytes 12296 | tf_op jit(solution)/shard_map/ppermute | solution.py:546
  231.5 20.5 %collective-permute-start.5 = (f32[8,128]{1,0:T(8,128)S(1)}, f32[8,128]{1,0:T(8,128)S(1)}, u32[]{:S(2)}, u32[]{:S(2)}) collective-permute-start(f32[8,128]{1,0:T(8,128)S(1)} %get-tuple-element.54), channel_id=1, source_target_pairs={{0,3},{1,4},{2,5},{3,6},{4,7},{5,0},{6,1},{7,2},{8,11},{9,12},{10,... | collective-permute-start | bytes 12296 | tf_op jit(solution)/shard_map/ppermute | solution.py:546
  234.6 17.4 %collective-permute-start.6 = (f32[8,128]{1,0:T(8,128)S(1)}, f32[8,128]{1,0:T(8,128)S(1)}, u32[]{:S(2)}, u32[]{:S(2)}) collective-permute-start(f32[8,128]{1,0:T(8,128)S(1)} %get-tuple-element.53), channel_id=1, source_target_pairs={{0,4},{1,5},{2,6},{3,7},{4,0},{5,1},{6,2},{7,3},{8,12},{9,13},{10,... | collective-permute-start | bytes 12296 | tf_op jit(solution)/shard_map/ppermute | solution.py:546
  235.6 16.4 %collective-permute-start.7 = (f32[8,128]{1,0:T(8,128)S(1)}, f32[8,128]{1,0:T(8,128)S(1)}, u32[]{:S(2)}, u32[]{:S(2)}) collective-permute-start(f32[8,128]{1,0:T(8,128)S(1)} %get-tuple-element.52), channel_id=1, source_target_pairs={{0,5},{1,6},{2,7},{3,0},{4,1},{5,2},{6,3},{7,4},{8,13},{9,14},{10,... | collective-permute-start | bytes 12296 | tf_op jit(solution)/shard_map/ppermute | solution.py:546
  239.0 13.0 %collective-permute-start.8 = (f32[8,128]{1,0:T(8,128)S(1)}, f32[8,128]{1,0:T(8,128)S(1)}, u32[]{:S(2)}, u32[]{:S(2)}) collective-permute-start(f32[8,128]{1,0:T(8,128)S(1)} %get-tuple-element.51), channel_id=1, source_target_pairs={{0,6},{1,7},{2,0},{3,1},{4,2},{5,3},{6,4},{7,5},{8,14},{9,15},{10,... | collective-permute-start | bytes 12296 | tf_op jit(solution)/shard_map/ppermute | solution.py:546
  242.4 9.6 %collective-permute-start.9 = (f32[8,128]{1,0:T(8,128)S(1)}, f32[8,128]{1,0:T(8,128)S(1)}, u32[]{:S(2)}, u32[]{:S(2)}) collective-permute-start(f32[8,128]{1,0:T(8,128)S(1)} %get-tuple-element.50), channel_id=1, source_target_pairs={{0,7},{1,0},{2,1},{3,2},{4,3},{5,4},{6,5},{7,6},{8,15},{9,8},{10,9... | collective-permute-start | bytes 12296 | tf_op jit(solution)/shard_map/ppermute | solution.py:546
  299.8 16.6 %copy-start = (f32[64,56,128]{2,1,0:T(8,128)}, f32[64,56,128]{2,1,0:T(8,128)S(1)}, u32[]{:S(2)}) copy-start(f32[64,56,128]{2,1,0:T(8,128)S(1)} %all_to_all.20) | copy-start | bytes 5505028
  299.8 0.8 copy-start.1
  300.6 6.1 %collective-permute-start.10 = (f32[64,8,128]{2,1,0:T(8,128)S(1)}, f32[64,8,128]{2,1,0:T(8,128)S(1)}, u32[]{:S(2)}, u32[]{:S(2)}) collective-permute-start(f32[64,8,128]{2,1,0:T(8,128)S(1)} %get-tuple-element.31), channel_id=1, source_target_pairs={{0,128},{64,192},{128,0},{192,64},{1,129},{65,193},{129,1},{193,65... | collective-permute-start | bytes 786440 | tf_op jit(solution)/shard_map/ppermute | solution.py:531
  306.8 0.9 copy-start.2
  307.6 17.2 %collective-permute-start.11 = (f32[2,64,8,128]{3,2,1,0:T(8,128)}, f32[2,64,8,128]{3,2,1,0:T(8,128)}, u32[]{:S(2)}, u32[]{:S(2)}) collective-permute-start(f32[2,64,8,128]{3,2,1,0:T(8,128)} %maximum_select_fusion.2), channel_id=1, source_target_pairs={{0,64},{64,0},{128,192},{192,128},{1,65},{65,1},{129,193},{193,129... | collective-permute-start | bytes 1572872 | tf_op jit(solution)/shard_map/ppermute | solution.py:531

commit v4 on v3

--- a/solution.py
+++ b/solution.py
@@ -288,56 +288,51 @@
 
 def backward_kernel(
     src_hbm, twiddle_hbm, th_hbm, tl_hbm, bh_hbm, bl_hbm, w1_hbm, w2_hbm, slope_hbm, square_hbm,
-    two_hbm, one_hbm, out_hbm,
+    two_hbm, out_hbm,
     src_ref, twiddle_ref, th_ref, tl_ref, bh_ref, bl_ref, w1, w2, slope_ref, square_ref,
-    two_ref, one_ref, out_ref, work_ref, part_ref, src_sems, sems, two_sems, one_sems, out_sems,
+    two_ref, out_ref, work_ref, part_ref, src_sems, sems, square_sems, slope_sems,
+    two_sems, out_sems,
 ):
     for p in range(8):
         block_of(src_hbm, src_ref, src_sems, p).start()
     pairs = (
-        (twiddle_hbm, twiddle_ref), (th_hbm, th_ref), (tl_hbm, tl_ref), (square_hbm, square_ref),
-        (w2_hbm, w2), (slope_hbm, slope_ref), (w1_hbm, w1), (bh_hbm, bh_ref), (bl_hbm, bl_ref),
+        (twiddle_hbm, twiddle_ref), (th_hbm, th_ref), (tl_hbm, tl_ref), (w2_hbm, w2),
+        (w1_hbm, w1), (bh_hbm, bh_ref), (bl_hbm, bl_ref),
     )
     loads = [pltpu.make_async_copy(a, b, sems.at[n]) for n, (a, b) in enumerate(pairs)]
     for load in loads:
         load.start()
     loads[0].wait()
-    plane_forward(
-        src_ref, work_ref, twiddle_ref, lambda p: block_of(src_hbm, src_ref, src_sems, p).wait()
-    )
+
+    def before(p):
+        block_of(src_hbm, src_ref, src_sems, p).wait()
+        pltpu.make_async_copy(square_hbm.at[p], square_ref.at[p], square_sems.at[p]).start()
+        pltpu.make_async_copy(slope_hbm.at[p], slope_ref.at[p], slope_sems.at[p]).start()
+
+    plane_forward(src_ref, work_ref, twiddle_ref, before)
     for load in loads[1:]:
         load.wait()
 
-    def body(g, carry):
-        grad_two = load_group(work_ref, g, th_ref, tl_ref) * square_ref[g]
+    sends = []
+    spectral = load_group(work_ref, 0, th_ref, tl_ref)
+    for g in range(GROUPS):
+        following = load_group(work_ref, g + 1, th_ref, tl_ref) if g + 1 < GROUPS else None
+        pltpu.make_async_copy(square_hbm.at[g], square_ref.at[g], square_sems.at[g]).wait()
+        grad_two = spectral * square_ref[g]
         two_ref[g] = grad_two
-        pltpu.make_async_copy(two_ref.at[g], two_hbm.at[g], two_sems.at[g]).start()
+        sends.append(pltpu.make_async_copy(two_ref.at[g], two_hbm.at[g], two_sems.at[g]))
+        sends[-1].start()
+        pltpu.make_async_copy(slope_hbm.at[g], slope_ref.at[g], slope_sems.at[g]).wait()
         grad_one = product(w2, grad_two) * slope_ref[g]
-        one_ref[g] = grad_one
-        pltpu.make_async_copy(one_ref.at[g], one_hbm.at[g], one_sems.at[g]).start()
         store_group(part_ref, g, product(w1, grad_one), bh_ref, bl_ref)
-        return carry
-
-    lax.fori_loop(0, GROUPS, body, 0)
+        spectral = following
     plane_backward(
         part_ref, out_ref, twiddle_ref, lambda p: block_of(out_ref, out_hbm, out_sems, p).start()
     )
-    for g in range(GROUPS):
-        pltpu.make_async_copy(two_ref.at[g], two_hbm.at[g], two_sems.at[g]).wait()
-        pltpu.make_async_copy(one_ref.at[g], one_hbm.at[g], one_sems.at[g]).wait()
+    for send in sends:
+        send.wait()
     for p in range(8):
         block_of(out_ref, out_hbm, out_sems, p).wait()
-
-
-def rest_kernel(one_ref, twiddle_ref, bh_ref, bl_ref, w1, out_ref, part_ref, plane_ref):
-    def body(g, carry):
-        store_group(part_ref, g, product(w1, one_ref[g]), bh_ref, bl_ref)
-        return carry
-
-    lax.fori_loop(0, GROUPS, body, 0)
-    plane_backward(part_ref, plane_ref, twiddle_ref, lambda p: None)
-    out_ref[:, : 2 * PART, :] = plane_ref[...]
-    out_ref[:, 2 * PART :, :] = jnp.zeros((64, 8, 128), f32)
 
 
 def spread(value):
@@ -345,35 +340,55 @@
     return jnp.concatenate([value[:BS], gap, value[BS:], gap], axis=0)
 
 
-def table_kernel(spec_ref, outer_ref, one_ref, two_ref, out_ref):
+def rest_kernel(
+    spec_ref, outer_ref, two_ref, slope_ref, w2, w1, twiddle_ref, bh_ref, bl_ref,
+    out_ref, plane_hbm,
+    t1_ref, s1_ref, t2_ref, s2_ref, part_ref, plane_ref, sends,
+):
     lanes = ((1,), (1,))
-
-    def body(g, carry):
-        t1, s1, t2, s2 = carry
-        one = spread(one_ref[g])
-        two = spread(two_ref[g])
-        t1 = t1 + dot3(split(spec_ref[g]), split(one), lanes)
-        t2 = t2 + dot3(split(outer_ref[g]), split(two), lanes)
-        return t1, s1 + one, t2, s2 + two
-
-    zero = jnp.zeros((2 * BS, 256), f32)
-    wide = jnp.zeros((256, WIDE), f32)
-    t1, s1, t2, s2 = lax.fori_loop(0, GROUPS, body, (zero, wide, zero, wide))
-    norm = 1.0 / math.sqrt(4 * NX * NY * KZ)
-    ones = jnp.ones((8, WIDE), bf16)
-    row = lax.broadcasted_iota(jnp.int32, (8, 128), 0)
-    out_ref[4 * BS :] = jnp.zeros((ROWS - 4 * BS, 128), f32)
-    biases = jnp.zeros((8, 128), f32)
-    for n, (table, total) in enumerate(((t1, s1), (t2, s2))):
-        real = table[:BS, :128] + table[BS:, 128:]
-        imag = table[:BS, 128:] - table[BS:, :128]
-        out_ref[2 * n * BS : (2 * n + 1) * BS] = real * norm
-        out_ref[(2 * n + 1) * BS : (2 * n + 2) * BS] = imag * norm
-        high, low = split(total)
-        sums = dot(ones, high, lanes) + dot(ones, low, lanes)
-        for q in range(2):
-            biases = jnp.where(row == 2 * n + q, sums[:, q * 128 : (q + 1) * 128], biases)
-    out_ref[4 * BS : 4 * BS + 8] = biases * norm
+    g = pl.program_id(0)
+
+    @pl.when(g == 0)
+    def _():
+        for ref in (t1_ref, s1_ref, t2_ref, s2_ref):
+            ref[...] = jnp.zeros(ref.shape, f32)
+
+    grad_two = two_ref[0]
+    two = spread(grad_two)
+    t2_ref[...] += dot3(split(outer_ref[0]), split(two), lanes)
+    s2_ref[...] += two
+    grad_one = product(w2, grad_two) * slope_ref[0]
+    one = spread(grad_one)
+    t1_ref[...] += dot3(split(spec_ref[0]), split(one), lanes)
+    s1_ref[...] += one
+    store_group(part_ref, g, product(w1, grad_one), bh_ref, bl_ref)
+
+    def send(p):
+        span = pl.ds(p * 8, 8)
+        rows = pl.ds(0, 2 * PART)
+        return pltpu.make_async_copy(plane_ref.at[span], plane_hbm.at[span, rows], sends.at[p])
+
+    @pl.when(g == GROUPS - 1)
+    def _():
+        plane_backward(part_ref, plane_ref, twiddle_ref, lambda p: send(p).start())
+        norm = 1.0 / math.sqrt(4 * NX * NY * KZ)
+        ones = jnp.ones((8, WIDE), bf16)
+        row = lax.broadcasted_iota(jnp.int32, (8, 128), 0)
+        out_ref[4 * BS :] = jnp.zeros((ROWS - 4 * BS, 128), f32)
+        biases = jnp.zeros((8, 128), f32)
+        for n, (table_ref, total_ref) in enumerate(((t1_ref, s1_ref), (t2_ref, s2_ref))):
+            table = table_ref[...]
+            real = table[:BS, :128] + table[BS:, 128:]
+            imag = table[:BS, 128:] - table[BS:, :128]
+            out_ref[2 * n * BS : (2 * n + 1) * BS] = real * norm
+            out_ref[(2 * n + 1) * BS : (2 * n + 2) * BS] = imag * norm
+            high, low = split(total_ref[...])
+            sums = dot(ones, high, lanes) + dot(ones, low, lanes)
+            for q in range(2):
+                biases = jnp.where(row == 2 * n + q, sums[:, q * 128 : (q + 1) * 128], biases)
+        out_ref[4 * BS : 4 * BS + 8] = biases * norm
+        for p in range(8):
+            send(p).wait()
 
 
 def field_kernel(
@@ -464,25 +479,40 @@
 
 def backward(cot_spec, twiddle, plane_fwd, plane_bwd, first, second, slope, square):
     args = (cot_spec, twiddle, *plane_fwd, *plane_bwd, first, second, slope, square)
-    outs = (GROUPED, GROUPED, jax.ShapeDtypeStruct(PARTIAL, f32))
+    outs = (GROUPED, jax.ShapeDtypeStruct(PARTIAL, f32))
     scratch = [
         *held(*args, *outs),
         pltpu.VMEM(SPECTRAL, f32),
         pltpu.VMEM(PARTIAL, f32),
-        *sems(8, 9, GROUPS, GROUPS, 8),
+        *sems(8, 7, *[GROUPS] * 3, 8),
     ]
     return call(backward_kernel, outs, args, scratch, 10_000_000_000, 20_000_000, free)
 
 
-def rest(grad_one, twiddle, plane_bwd, first):
-    return call(
+def by_group(n):
+    return [pl.BlockSpec((1, 2 * BS, WIDE), lambda g: (g, 0, 0))] * n
+
+
+def rest(spec, outer, grad_two, slope, second, first, twiddle, plane_bwd):
+    return pl.pallas_call(
         rest_kernel,
-        jax.ShapeDtypeStruct((64, 2 * PART + 8, 128), f32),
-        (grad_one, twiddle, *plane_bwd, first),
-        [pltpu.VMEM(PARTIAL, f32), pltpu.VMEM(PARTIAL, f32)],
-        3_000_000_000,
-        5_000_000,
-    )
+        grid=(GROUPS,),
+        out_shape=(
+            jax.ShapeDtypeStruct((ROWS, 128), f32),
+            jax.ShapeDtypeStruct((64, 2 * PART + 8, 128), f32),
+        ),
+        in_specs=by_group(4) + vmem(5),
+        out_specs=(pl.BlockSpec((ROWS, 128), lambda g: (0, 0)), *free(1)),
+        scratch_shapes=[
+            *[pltpu.VMEM((2 * BS, 256), f32), pltpu.VMEM((256, WIDE), f32)] * 2,
+            *[pltpu.VMEM(PARTIAL, f32)] * 2,
+            *sems(8),
+        ],
+        compiler_params=BIG,
+        cost_estimate=pl.CostEstimate(
+            flops=8_000_000_000, bytes_accessed=16_000_000, transcendentals=0
+        ),
+    )(spec, outer, grad_two, slope, second, first, twiddle, *plane_bwd)
 
 
 def field(first, second, cotangent, tables):
@@ -548,9 +578,7 @@
 
 
 def every_row(total):
-    dp = lax.axis_index("dp")
-    total = join_half(total, "dp", 2, dp // 2)
-    total = join_half(total, "dp", 1, dp % 2)
+    total = join_half(total, "dp", 1, lax.axis_index("dp") % 2)
     total = total.reshape(2, 2, NB, 2, 8, ROWS // 64, 128)
     return total.transpose(2, 0, 1, 3, 4, 5, 6).reshape(NB, ROWS, 128)
 
@@ -586,38 +614,35 @@
         ),
     )(doubling, state_spec, twiddle, *plane_fwd, stacked(first), bias_one, stacked(second), bias_two)
 
-    grad_two, grad_one, plane = backward(
+    second_back = stacked(second.T)
+    grad_two, plane = backward(
         cot_spec,
         twiddle,
         plane_fwd,
         plane_bwd,
         stacked(rows_of(first.T, 0)),
-        stacked(second.T),
+        second_back,
         slope,
         square,
     )
     first_part = exchange(plane)
-    rows = call(
-        table_kernel,
-        jax.ShapeDtypeStruct((ROWS, 128), f32),
-        (spec, outer, grad_one, grad_two),
-        [],
-        4_000_000_000,
-        13_000_000,
+    rows, plane = rest(
+        spec, outer, grad_two, slope, second_back, stacked(rows_of(first.T, 1)), twiddle, plane_bwd
     )
     rows = owned_rows(rows)
-    plane = rest(grad_one, twiddle, plane_bwd, stacked(rows_of(first.T, 1)))
     plane = lax.dynamic_update_slice(
         plane, jnp.broadcast_to(rows[None], (64, *rows.shape)), (0, 2 * PART, 0)
     )
     first_part, plane = lax.optimization_barrier((first_part, plane))
     second_part = exchange(plane)
-    rows = every_row(second_part[:, 2 * PART :])
+    rows = join_half(second_part[:, 2 * PART :], "dp", 2, lax.axis_index("dp") // 2)
+    state_grad = field(first_part, second_part, cotangent, depth_bwd).reshape(1, 8, 8, NZ, C)
+    state_grad, rows = lax.optimization_barrier((state_grad, rows))
+    rows = every_row(rows)
     grads_one = rows[:, : 2 * BS, :BS].reshape(NB, 2, BS, BS).transpose(1, 0, 2, 3)
     grads_two = rows[:, 2 * BS : 4 * BS, :BS].reshape(NB, 2, BS, BS).transpose(1, 0, 2, 3)
     biases = rows[:, 4 * BS : 4 * BS + 4, :BS].reshape(NB, 2, 2, BS)
 
-    state_grad = field(first_part, second_part, cotangent, depth_bwd).reshape(1, 8, 8, NZ, C)
     return (
         state_grad,
         grads_one,

time: 330 us -> 319 us (0.967)
  Pallas kernels: 75.1 us -> 66.7 us
    pallas_call x6 -> x4, Pallas kernels: 56.9 us -> 33.8 us  [call(): pl.pallas_call(kernel, out_shape=out_shape, in_specs=place(len(args)), ou...]
    pallas_call x0 -> x1, Pallas kernels: none -> 14.5 us  [rest(): pl.pallas_call(rest_kernel, grid=(GROUPS,), out_shape=(jax.ShapeDtypeStru...]
    ppermute x2, waiting for transfers between devices: 5.57 us -> 1.54 us  [join_half(): other = lax.ppermute(value, axis, [(n, n ^ flip) for n in range(size)])]
  transfers between devices with their start and end apart: 15 -> 15, of which waited for: 6 -> 8; matrix products, arithmetic and copies ran while one was open for 4% -> 4% of each run, Pallas kernels for 15% -> 15%
where the time goes in v4:
time: 319 us; the launch traced here: 318 us
  waiting for transfers between devices  119 us (37%)
  Pallas kernels  66.7 us (21%)
  starting transfers between devices  65.6 us (21%)
  blocking collectives  48.2 us (15%)
  local copies, waits for them, and re-layouts  10.8 us (3%)
  other arithmetic  6.61 us (2%)
    all_to_all x3, waiting for transfers between devices, exchange(): lax.all_to_all(value, ('px', 'py'), split_axis=0, concat_axis=0, tiled=True)  107 us
    all_to_all x1, blocking collectives, exchange(): lax.all_to_all(value, ('px', 'py'), split_axis=0, concat_axis=0, tiled=True)  48.2 us
    all_to_all x3, starting transfers between devices, exchange(): lax.all_to_all(value, ('px', 'py'), split_axis=0, concat_axis=0, tiled=True)  37.1 us
    pallas_call x4, Pallas kernels, call(): pl.pallas_call(kernel, out_shape=out_shape, in_specs=place(len(args)), ou...  33.8 us
    pallas_call x1, Pallas kernels, shards(): pl.pallas_call(forward_kernel, out_shape=(GROUPED,) * 4, in_specs=[pl.Blo...  18.3 us
    pallas_call x1, Pallas kernels, rest(): pl.pallas_call(rest_kernel, grid=(GROUPS,), out_shape=(jax.ShapeDtypeStru...  14.5 us
    ppermute x7, starting transfers between devices, owned_rows(): lax.ppermute(piece, 'py', [(n, (n + offset) % 8) for n in range(8)])  14.4 us
    ppermute x2, starting transfers between devices, join_half(): other = lax.ppermute(value, axis, [(n, n ^ flip) for n in range(size)])  8.85 us
  transfers between devices with their start and end apart: 15, of which 8 were waited for; matrix products, arithmetic and copies ran while one was open for 4% of the time, Pallas kernels for 15%

profile of v4, /device:TPU:1, one launch (start us, length us, event | category | flops | bytes accessed | tf_op | source)
XLA Modules:
  0.0 318.3 jit_solution(879629325339665358)
XLA Ops:
  0.6 6.4 %shard_map.183 = f32[4,16,96,128]{3,2,1,0:T(8,128)} custom-call(bf16[2048,384]{1,0:T(8,128)(2,1)} %bitcast.101, bf16[512,256]{1,0:T(8,128)(2,1)} %constant.167.clone.both_hbm), custom_call_target="tpu_custom_call" | custom-call | flops 800000000 | bytes 5000000 | tf_op jit(solution)/shard_map/pallas_call | solution.py:462
  7.0 15.4 %all-to-all-start.1 = ((f32[64,96,128]{2,1,0:T(8,128)}), f32[64,96,128]{2,1,0:T(8,128)}, u32[]{:S(2)}, u32[]{:S(2)}) async-start(f32[64,96,128]{2,1,0:T(8,128)} %bitcast.94), calls=%async_computation.1 | async-start | bytes 6291456 | tf_op jit(solution)/shard_map/all_to_all | solution.py:587
  22.4 6.4 %shard_map.182 = f32[4,16,96,128]{3,2,1,0:T(8,128)} custom-call(bf16[2048,384]{1,0:T(8,128)(2,1)} %bitcast.96, bf16[512,256]{1,0:T(8,128)(2,1)} %constant.167.clone.both_hbm), custom_call_target="tpu_custom_call" | custom-call | flops 800000000 | bytes 5000000 | tf_op jit(solution)/shard_map/pallas_call | solution.py:462
  28.8 63.8 %all-to-all-done.1.src_ref = f32[64,96,128]{2,1,0:T(8,128)} async-done(((f32[64,96,128]{2,1,0:T(8,128)}), f32[64,96,128]{2,1,0:T(8,128)}, u32[]{:S(2)}, u32[]{:S(2)}) %all-to-all-start.1) | async-done | bytes 3145760 | tf_op jit(solution)/shard_map/all_to_all | solution.py:587
  92.6 11.3 %all-to-all-start = ((f32[64,96,128]{2,1,0:T(8,128)}), f32[64,96,128]{2,1,0:T(8,128)}, u32[]{:S(2)}, u32[]{:S(2)}) async-start(f32[64,96,128]{2,1,0:T(8,128)} %bitcast.93), calls=%async_computation | async-start | bytes 6291456 | tf_op jit(solution)/shard_map/all_to_all | solution.py:587
  103.9 0.8 constant_dynamic-slice_fusion.14
  106.7 0.8 copy.27.w2
  112.4 18.3 %shard_map.184 = (f32[8,192,512]{2,1,0:T(8,128)}, f32[8,192,512]{2,1,0:T(8,128)}, f32[8,192,512]{2,1,0:T(8,128)}, f32[8,192,512]{2,1,0:T(8,128)}) custom-call(f32[1,1]{1,0:T(1,128)} %bitcast.18.doubling_ref, f32[64,96,128]{2,1,0:T(8,128)} %all-to-all-done.1.src_ref, f32[64,2,128]{2,1,0:T(2,128)} %constant.168.clone.twiddle_ref.twiddle_hbm, ...), custom_call_target="tpu_custom_call" | custom-call | flops 8000000000 | bytes 16000000 | tf_op jit(solution)/shard_map/pallas_call | solution.py:605
  130.8 42.9 %all-to-all-done.src_hbm = f32[64,96,128]{2,1,0:T(8,128)} async-done(((f32[64,96,128]{2,1,0:T(8,128)}), f32[64,96,128]{2,1,0:T(8,128)}, u32[]{:S(2)}, u32[]{:S(2)}) %all-to-all-start) | async-done | bytes 3145760 | tf_op jit(solution)/shard_map/all_to_all | solution.py:587
  173.7 14.0 %shard_map.185 = (f32[8,192,512]{2,1,0:T(8,128)}, f32[64,48,128]{2,1,0:T(8,128)}) custom-call(f32[64,96,128]{2,1,0:T(8,128)} %all-to-all-done.src_hbm, f32[64,2,128]{2,1,0:T(2,128)} %constant.168.clone.twiddle_ref.twiddle_hbm, bf16[256,256]{1,0:T(8,128)(2,1)} %constant.169.clone.th_ref.th_hbm, bf16[256,256]{1,0:T(8,128)(2,1)} %constant.170.clone.tl_ref.tl_hbm, ...), custom_call_target="tpu_custom_call" | custom-call | flops 10000000000 | bytes 20000000 | tf_op jit(solution)/shard_map/pallas_call | solution.py:462
  187.7 10.4 %all-to-all-start.2 = ((f32[64,48,128]{2,1,0:T(8,128)}), f32[64,48,128]{2,1,0:T(8,128)}, u32[]{:S(2)}, u32[]{:S(2)}) async-start(f32[64,48,128]{2,1,0:T(8,128)} %get-tuple-element.19), calls=%async_computation.2 | async-start | bytes 3145728 | tf_op jit(solution)/shard_map/all_to_all | solution.py:587
  198.8 14.5 %shard_map.186 = (f32[512,128]{1,0:T(8,128)}, f32[64,56,128]{2,1,0:T(8,128)}) custom-call(f32[8,192,512]{2,1,0:T(8,128)} %get-tuple-element.20.spec_ref, f32[8,192,512]{2,1,0:T(8,128)} %get-tuple-element.21.outer_ref, f32[8,192,512]{2,1,0:T(8,128)} %get-tuple-element.22.two_ref, f32[8,192,512]{2,1,0:T(8,128)} %get-tuple-element.17.slope_hbm.slope_ref, ...), custom_call_target="tpu_custom_call" | custom-call | flops 8000000000 | bytes 16000000 | tf_op jit(solution)/shard_map/pallas_call | solution.py:497
  213.3 0.9 constant_dynamic-slice_fusion.11
  214.2 2.2 collective-permute-start
  216.4 1.0 collective-permute-done
  217.4 0.9 dynamic-slice_add_fusion
  219.0 4.1 %collective-permute-done.1 = f32[128,128]{1,0:T(8,128)S(1)} collective-permute-done((f32[128,128]{1,0:T(8,128)S(1)}, f32[128,128]{1,0:T(8,128)S(1)}, u32[]{:S(2)}, u32[]{:S(2)}) %collective-permute-start.1) | collective-permute-done | bytes 65568 | tf_op jit(solution)/shard_map/ppermute | solution.py:556
  223.2 2.3 collective-permute-start.2
  225.5 3.3 %collective-permute-done.2 = f32[64,128]{1,0:T(8,128)S(1)} collective-permute-done((f32[64,128]{1,0:T(8,128)S(1)}, f32[64,128]{1,0:T(8,128)S(1)}, u32[]{:S(2)}, u32[]{:S(2)}) %collective-permute-start.2) | collective-permute-done | bytes 32800 | tf_op jit(solution)/shard_map/ppermute | solution.py:556
  228.9 1.4 collective-permute-start.3
  230.3 2.3 collective-permute-start.4
  232.6 2.7 collective-permute-start.5
  235.4 2.8 collective-permute-start.6
  238.2 1.5 collective-permute-start.7
  239.7 3.6 %collective-permute-start.8 = (f32[8,128]{1,0:T(8,128)S(1)}, f32[8,128]{1,0:T(8,128)S(1)}, u32[]{:S(2)}, u32[]{:S(2)}) collective-permute-start(f32[8,128]{1,0:T(8,128)S(1)} %get-tuple-element.59), channel_id=1, source_target_pairs={{0,6},{1,7},{2,0},{3,1},{4,2},{5,3},{6,4},{7,5},{8,14},{9,15},{10,... | collective-permute-start | bytes 12296 | tf_op jit(solution)/shard_map/ppermute | solution.py:576
  244.1 2.0 collective-permute-done.9
  246.9 48.2 %all_to_all.20 = f32[64,56,128]{2,1,0:T(8,128)S(1)} all-to-all(f32[64,56,128]{2,1,0:T(8,128)} %broadcast_dynamic-update-slice_fusion), channel_id=1, replica_groups=mesh['dp'=4,'px'=8,'py'=8] {'px','py'}, dimensions={0} | all-to-all | bytes 3670016 | tf_op jit(solution)/shard_map/all_to_all | solution.py:587
  295.1 0.9 slice_bitcast_fusion
  296.5 7.1 %shard_map.187 = bf16[2048,384]{1,0:T(8,128)(2,1)} custom-call(f32[4,16,48,128]{3,2,1,0:T(8,128)} %bitcast.31.first_hbm, f32[4,16,56,128]{3,2,1,0:T(8,128)} %bitcast.95, bf16[2048,384]{1,0:T(8,128)(2,1)} %bitcast.97, bf16[256,256]{1,0:T(8,128)(2,1)} %constant.173.clone.high_hbm, bf16[256,256]{1,0:T(8,128)(2,1)} %constant.174.clone.low_hbm), custom_call_target="tpu_custom_call" | custom-call | flops 1200000000 | bytes 7000000 | tf_op jit(solution)/shard_map/pallas_call | solution.py:462
  303.6 1.2 maximum_select_fusion
  304.8 8.6 %collective-permute-start.11 = (f32[2,64,8,128]{3,2,1,0:T(8,128)S(1)}, f32[2,64,8,128]{3,2,1,0:T(8,128)S(1)}, u32[]{:S(2)}, u32[]{:S(2)}) collective-permute-start(f32[2,64,8,128]{3,2,1,0:T(8,128)S(1)} %maximum_select_fusion), channel_id=1, source_target_pairs={{0,64},{64,0},{128,192},{192,128},{1,65},{65,1},{129,193},{193,129... | collective-permute-start | bytes 1572872 | tf_op jit(solution)/shard_map/ppermute | solution.py:561
  313.5 1.5 collective-permute-done.11
  (48 shorter events, 13.5 us)
Async XLA Ops:
  7.0 85.6 %all-to-all-start.1 = ((f32[64,96,128]{2,1,0:T(8,128)}), f32[64,96,128]{2,1,0:T(8,128)}, u32[]{:S(2)}, u32[]{:S(2)}) async-start(f32[64,96,128]{2,1,0:T(8,128)} %bitcast.94), calls=%async_computation.1 | async-start | bytes 6291456 | tf_op jit(solution)/shard_map/all_to_all | solution.py:587
  92.6 81.1 %all-to-all-start = ((f32[64,96,128]{2,1,0:T(8,128)}), f32[64,96,128]{2,1,0:T(8,128)}, u32[]{:S(2)}, u32[]{:S(2)}) async-start(f32[64,96,128]{2,1,0:T(8,128)} %bitcast.93), calls=%async_computation | async-start | bytes 6291456 | tf_op jit(solution)/shard_map/all_to_all | solution.py:587
  187.7 59.2 %all-to-all-start.2 = ((f32[64,48,128]{2,1,0:T(8,128)}), f32[64,48,128]{2,1,0:T(8,128)}, u32[]{:S(2)}, u32[]{:S(2)}) async-start(f32[64,48,128]{2,1,0:T(8,128)} %get-tuple-element.19), calls=%async_computation.2 | async-start | bytes 3145728 | tf_op jit(solution)/shard_map/all_to_all | solution.py:587
  214.2 3.2 collective-permute-start
  218.3 4.8 %collective-permute-start.1 = (f32[128,128]{1,0:T(8,128)S(1)}, f32[128,128]{1,0:T(8,128)S(1)}, u32[]{:S(2)}, u32[]{:S(2)}) collective-permute-start(f32[128,128]{1,0:T(8,128)S(1)} %constant_dynamic-slice_fusion.10), channel_id=1, source_target_pairs={{0,128},{64,192},{128,0},{192,64},{1,129},{65,193},{129,1},{193,65... | collective-permute-start | bytes 196616 | tf_op jit(solution)/shard_map/ppermute | solution.py:556
  223.2 5.7 %collective-permute-start.2 = (f32[64,128]{1,0:T(8,128)S(1)}, f32[64,128]{1,0:T(8,128)S(1)}, u32[]{:S(2)}, u32[]{:S(2)}) collective-permute-start(f32[64,128]{1,0:T(8,128)S(1)} %constant_dynamic-slice_fusion.9), channel_id=1, source_target_pairs={{0,8},{8,0},{16,24},{24,16},{32,40},{40,32},{48,56},{56,48},{1,9},... | collective-permute-start | bytes 98312 | tf_op jit(solution)/shard_map/ppermute | solution.py:556
  228.9 10.9 %collective-permute-start.3 = (f32[8,128]{1,0:T(8,128)S(1)}, f32[8,128]{1,0:T(8,128)S(1)}, u32[]{:S(2)}, u32[]{:S(2)}) collective-permute-start(f32[8,128]{1,0:T(8,128)S(1)} %get-tuple-element.57), channel_id=1, source_target_pairs={{0,1},{1,2},{2,3},{3,4},{4,5},{5,6},{6,7},{7,0},{8,9},{9,10},{10,1... | collective-permute-start | bytes 12296 | tf_op jit(solution)/shard_map/ppermute | solution.py:576
  230.3 13.0 %collective-permute-start.4 = (f32[8,128]{1,0:T(8,128)S(1)}, f32[8,128]{1,0:T(8,128)S(1)}, u32[]{:S(2)}, u32[]{:S(2)}) collective-permute-start(f32[8,128]{1,0:T(8,128)S(1)} %get-tuple-element.63), channel_id=1, source_target_pairs={{0,2},{1,3},{2,4},{3,5},{4,6},{5,7},{6,0},{7,1},{8,10},{9,11},{10,... | collective-permute-start | bytes 12296 | tf_op jit(solution)/shard_map/ppermute | solution.py:576
  232.6 10.7 %collective-permute-start.5 = (f32[8,128]{1,0:T(8,128)S(1)}, f32[8,128]{1,0:T(8,128)S(1)}, u32[]{:S(2)}, u32[]{:S(2)}) collective-permute-start(f32[8,128]{1,0:T(8,128)S(1)} %get-tuple-element.62), channel_id=1, source_target_pairs={{0,3},{1,4},{2,5},{3,6},{4,7},{5,0},{6,1},{7,2},{8,11},{9,12},{10,... | collective-permute-start | bytes 12296 | tf_op jit(solution)/shard_map/ppermute | solution.py:576
  235.4 8.0 %collective-permute-start.6 = (f32[8,128]{1,0:T(8,128)S(1)}, f32[8,128]{1,0:T(8,128)S(1)}, u32[]{:S(2)}, u32[]{:S(2)}) collective-permute-start(f32[8,128]{1,0:T(8,128)S(1)} %get-tuple-element.61), channel_id=1, source_target_pairs={{0,4},{1,5},{2,6},{3,7},{4,0},{5,1},{6,2},{7,3},{8,12},{9,13},{10,... | collective-permute-start | bytes 12296 | tf_op jit(solution)/shard_map/ppermute | solution.py:576
  238.2 5.2 %collective-permute-start.7 = (f32[8,128]{1,0:T(8,128)S(1)}, f32[8,128]{1,0:T(8,128)S(1)}, u32[]{:S(2)}, u32[]{:S(2)}) collective-permute-start(f32[8,128]{1,0:T(8,128)S(1)} %get-tuple-element.60), channel_id=1, source_target_pairs={{0,5},{1,6},{2,7},{3,0},{4,1},{5,2},{6,3},{7,4},{8,13},{9,14},{10,... | collective-permute-start | bytes 12296 | tf_op jit(solution)/shard_map/ppermute | solution.py:576
  239.7 4.3 %collective-permute-start.8 = (f32[8,128]{1,0:T(8,128)S(1)}, f32[8,128]{1,0:T(8,128)S(1)}, u32[]{:S(2)}, u32[]{:S(2)}) collective-permute-start(f32[8,128]{1,0:T(8,128)S(1)} %get-tuple-element.59), channel_id=1, source_target_pairs={{0,6},{1,7},{2,0},{3,1},{4,2},{5,3},{6,4},{7,5},{8,14},{9,15},{10,... | collective-permute-start | bytes 12296 | tf_op jit(solution)/shard_map/ppermute | solution.py:576
  243.3 2.8 collective-permute-start.9
  295.1 1.4 copy-start
  296.0 7.6 %collective-permute-start.10 = (f32[64,8,128]{2,1,0:T(8,128)}, f32[64,8,128]{2,1,0:T(8,128)}, u32[]{:S(2)}, u32[]{:S(2)}) collective-permute-start(f32[64,8,128]{2,1,0:T(8,128)} %get-tuple-element.37), channel_id=1, source_target_pairs={{0,128},{64,192},{128,0},{192,64},{1,129},{65,193},{129,1},{193,65... | collective-permute-start | bytes 786440 | tf_op jit(solution)/shard_map/ppermute | solution.py:561
  304.8 10.2 %collective-permute-start.11 = (f32[2,64,8,128]{3,2,1,0:T(8,128)S(1)}, f32[2,64,8,128]{3,2,1,0:T(8,128)S(1)}, u32[]{:S(2)}, u32[]{:S(2)}) collective-permute-start(f32[2,64,8,128]{3,2,1,0:T(8,128)S(1)} %maximum_select_fusion), channel_id=1, source_target_pairs={{0,64},{64,0},{128,192},{192,128},{1,65},{65,1},{129,193},{193,129... | collective-permute-start | bytes 1572872 | tf_op jit(solution)/shard_map/ppermute | solution.py:561

commit v5 on v4

--- a/solution.py
+++ b/solution.py
@@ -17,7 +17,8 @@
 KZ = 16
 C = 384
 HALF = BS // 2
-PART = HALF // 2
+FIRST = 32
+SECOND = HALF - FIRST
 CELLS = 64
 STEP = 8
 GROUPS = 64 // STEP
@@ -28,7 +29,6 @@
 bf16 = jnp.bfloat16
 BIG = pltpu.CompilerParams(vmem_limit_bytes=62 * 1024 * 1024)
 SPECTRAL = (64, 2 * HALF, 128)
-PARTIAL = (64, 2 * PART, 128)
 GROUPED = jax.ShapeDtypeStruct((GROUPS, 2 * BS, WIDE), f32)
 
 
@@ -46,7 +46,11 @@
     pair = np.stack([np.cos(angle), -np.sin(angle)], axis=1) * scale
     eye = np.eye(8)
     forward = np.einsum("kqz,ab->kqabz", pair, eye).reshape(256, 256)
-    return np_split(forward), np_split(forward.T.copy())
+    scheme = ((0, 1), (0, 1, 0))
+    return [
+        np.concatenate([np_split(table)[n] for n in order], axis=1)
+        for table, order in zip((forward, forward.T.copy()), scheme)
+    ]
 
 
 def plane_tables():
@@ -59,7 +63,8 @@
     real[1, :, 0] = -both.imag
     real[1, :, 1] = both.real
     forward = np.einsum("qxpf,cd->qcxpdf", real, np.eye(2)).reshape(256, 256)
-    return np_split(forward), np_split(forward.T.copy())
+    tables = np_split(forward), np_split(forward.T.copy())
+    return [np.concatenate([high, high, low], axis=0) for high, low in tables]
 
 
 def twiddle_table():
@@ -81,18 +86,22 @@
     return lax.dot_general(left, right, (dims, ((), ())), preferred_element_type=f32)
 
 
+def thrice(pair, axis):
+    high, low = pair
+    return jnp.concatenate([high, low, high], axis=axis)
+
+
+def paired(pair, axis):
+    high, low = pair
+    return jnp.concatenate([high, high, low], axis=axis)
+
+
 def dot3(left, right, dims=((1,), (0,))):
-    high, low = left
-    rows = high.shape[0]
-    both = dot(jnp.concatenate([high, low], axis=0), right[0], dims)
-    return both[:rows] + both[rows:] + dot(high, right[1], dims)
+    return dot(thrice(left, 1), paired(right, dims[1][0]), dims)
 
 
 def product(weight_ref, value):
-    rows = weight_ref.shape[0] // 2
-    high, low = split(value)
-    both = dot(weight_ref[...], high)
-    return both[:rows] + both[rows:] + dot(weight_ref[:rows], low)
+    return dot(weight_ref[...], paired(split(value), 0))
 
 
 def swap(upper, lower):
@@ -173,7 +182,7 @@
 
 def plane_backward(work_ref, out_ref, twiddle_ref, after):
     def body(p, carry):
-        for tile in range(PART // 8):
+        for tile in range(work_ref.shape[1] // 16):
             pairs = [
                 turned(*read(work_ref, n * 8 + p, tile), twiddle_ref, n * 8 + p, -1.0)
                 for n in range(8)
@@ -187,14 +196,14 @@
     senders(work_ref, out_ref, 1.0, lambda p: None, after)
 
 
-def load_group(work_ref, group, high_ref, low_ref):
+def load_group(work_ref, group, table_ref):
     rows = [
         jnp.concatenate(
             [work_ref[group * STEP + n, :HALF], work_ref[group * STEP + n, HALF:]], axis=1
         )
         for n in range(STEP)
     ]
-    values = dot3(split(jnp.concatenate(rows, axis=0)), (high_ref[...], low_ref[...]))
+    values = dot(thrice(split(jnp.concatenate(rows, axis=0)), 1), table_ref[...])
     pairs = []
     for pair in range(STEP // 2):
         part = []
@@ -207,24 +216,25 @@
     return jnp.concatenate(pairs, axis=1)
 
 
-def store_group(work_ref, group, spectral, high_ref, low_ref):
+def store_group(work_ref, group, spectral, table_ref):
+    count = spectral.shape[0] // 4
     rows = []
     for pair in range(STEP // 2):
         part = spectral[:, pair * 128 : (pair + 1) * 128]
         parts = [
             swap(
-                part[2 * q * PART : (2 * q + 1) * PART],
-                part[(2 * q + 1) * PART : (2 * q + 2) * PART],
+                part[2 * q * count : (2 * q + 1) * count],
+                part[(2 * q + 1) * count : (2 * q + 2) * count],
             )
             for q in range(2)
         ]
         for n in range(2):
             rows.append(jnp.concatenate([parts[0][n], parts[1][n]], axis=1))
-    values = dot3(split(jnp.concatenate(rows, axis=0)), (high_ref[...], low_ref[...]))
+    values = dot(thrice(split(jnp.concatenate(rows, axis=0)), 1), table_ref[...])
     for n in range(STEP):
         for q in range(2):
-            work_ref[group * STEP + n, q * PART : (q + 1) * PART] = values[
-                n * PART : (n + 1) * PART, q * 128 : (q + 1) * 128
+            work_ref[group * STEP + n, q * count : (q + 1) * count] = values[
+                n * count : (n + 1) * count, q * 128 : (q + 1) * 128
             ]
 
 
@@ -239,8 +249,8 @@
     table.wait()
     for g in range(8):
         copies[g].wait()
-        values = dot(both_ref[...], field_ref[g * 256 : (g + 1) * 256, :])
-        values = values[:256] + values[256:]
+        rows = field_ref[g * 256 : (g + 1) * 256, :]
+        values = dot(both_ref[...], jnp.concatenate([rows, rows], axis=0))
         work_ref[:, g * 8 : (g + 1) * 8, :] = values.reshape(2 * KZ, 8, C)
     sends = []
     for k in range(KZ):
@@ -256,14 +266,14 @@
 
 
 def forward_kernel(
-    doubling_ref, src_ref, twiddle_ref, th_ref, tl_ref, w1, b1, w2, b2,
+    doubling_ref, src_ref, twiddle_ref, t_ref, w1, b1, w2, b2,
     spec_ref, outer_ref, slope_ref, square_ref, work_ref,
 ):
     plane_forward(src_ref, work_ref, twiddle_ref, lambda p: None)
     root = math.sqrt(2.0 / math.pi)
 
     def body(g, carry):
-        spectral = load_group(work_ref, g, th_ref, tl_ref)
+        spectral = load_group(work_ref, g, t_ref)
         spec_ref[g] = spectral
         pre = product(w1, spectral) + b1[...]
         pre_sq = pre * pre
@@ -287,17 +297,17 @@
 
 
 def backward_kernel(
-    src_hbm, twiddle_hbm, th_hbm, tl_hbm, bh_hbm, bl_hbm, w1_hbm, w2_hbm, slope_hbm, square_hbm,
+    src_hbm, twiddle_hbm, t_hbm, back_hbm, w1_hbm, w2_hbm, slope_hbm, square_hbm,
     two_hbm, out_hbm,
-    src_ref, twiddle_ref, th_ref, tl_ref, bh_ref, bl_ref, w1, w2, slope_ref, square_ref,
+    src_ref, twiddle_ref, t_ref, back_ref, w1, w2, slope_ref, square_ref,
     two_ref, out_ref, work_ref, part_ref, src_sems, sems, square_sems, slope_sems,
     two_sems, out_sems,
 ):
     for p in range(8):
         block_of(src_hbm, src_ref, src_sems, p).start()
     pairs = (
-        (twiddle_hbm, twiddle_ref), (th_hbm, th_ref), (tl_hbm, tl_ref), (w2_hbm, w2),
-        (w1_hbm, w1), (bh_hbm, bh_ref), (bl_hbm, bl_ref),
+        (twiddle_hbm, twiddle_ref), (t_hbm, t_ref), (w2_hbm, w2),
+        (w1_hbm, w1), (back_hbm, back_ref),
     )
     loads = [pltpu.make_async_copy(a, b, sems.at[n]) for n, (a, b) in enumerate(pairs)]
     for load in loads:
@@ -314,9 +324,9 @@
         load.wait()
 
     sends = []
-    spectral = load_group(work_ref, 0, th_ref, tl_ref)
+    spectral = load_group(work_ref, 0, t_ref)
     for g in range(GROUPS):
-        following = load_group(work_ref, g + 1, th_ref, tl_ref) if g + 1 < GROUPS else None
+        following = load_group(work_ref, g + 1, t_ref) if g + 1 < GROUPS else None
         pltpu.make_async_copy(square_hbm.at[g], square_ref.at[g], square_sems.at[g]).wait()
         grad_two = spectral * square_ref[g]
         two_ref[g] = grad_two
@@ -324,7 +334,7 @@
         sends[-1].start()
         pltpu.make_async_copy(slope_hbm.at[g], slope_ref.at[g], slope_sems.at[g]).wait()
         grad_one = product(w2, grad_two) * slope_ref[g]
-        store_group(part_ref, g, product(w1, grad_one), bh_ref, bl_ref)
+        store_group(part_ref, g, product(w1, grad_one), back_ref)
         spectral = following
     plane_backward(
         part_ref, out_ref, twiddle_ref, lambda p: block_of(out_ref, out_hbm, out_sems, p).start()
@@ -341,7 +351,7 @@
 
 
 def rest_kernel(
-    spec_ref, outer_ref, two_ref, slope_ref, w2, w1, twiddle_ref, bh_ref, bl_ref,
+    spec_ref, outer_ref, two_ref, slope_ref, w2, w1, twiddle_ref, back_ref,
     out_ref, plane_hbm,
     t1_ref, s1_ref, t2_ref, s2_ref, part_ref, plane_ref, sends,
 ):
@@ -361,11 +371,11 @@
     one = spread(grad_one)
     t1_ref[...] += dot3(split(spec_ref[0]), split(one), lanes)
     s1_ref[...] += one
-    store_group(part_ref, g, product(w1, grad_one), bh_ref, bl_ref)
+    store_group(part_ref, g, product(w1, grad_one), back_ref)
 
     def send(p):
         span = pl.ds(p * 8, 8)
-        rows = pl.ds(0, 2 * PART)
+        rows = pl.ds(0, 2 * SECOND)
         return pltpu.make_async_copy(plane_ref.at[span], plane_hbm.at[span, rows], sends.at[p])
 
     @pl.when(g == GROUPS - 1)
@@ -392,13 +402,13 @@
 
 
 def field_kernel(
-    first_hbm, second_hbm, cotangent_hbm, high_hbm, low_hbm, out_hbm,
-    first_ref, second_ref, cotangent_ref, high_ref, low_ref, out_ref, work_ref,
+    first_hbm, second_hbm, cotangent_hbm, table_hbm, out_hbm,
+    first_ref, second_ref, cotangent_ref, table_ref, out_ref, work_ref,
     first_sems, second_sems, sems, out_sems,
 ):
     loads = []
     for k in range(KZ):
-        span = pl.ds(0, 2 * PART)
+        span = pl.ds(0, 2 * SECOND)
         loads.append(
             (
                 pltpu.make_async_copy(first_hbm.at[:, k], first_ref.at[:, k], first_sems.at[k]),
@@ -407,7 +417,7 @@
                 ),
             )
         )
-    pairs = ((high_hbm, high_ref), (low_hbm, low_ref), (cotangent_hbm, cotangent_ref))
+    pairs = ((table_hbm, table_ref), (cotangent_hbm, cotangent_ref))
     others = [pltpu.make_async_copy(a, b, sems.at[n]) for n, (a, b) in enumerate(pairs)]
     for load in loads:
         load[0].start()
@@ -419,19 +429,16 @@
         loads[k][1].wait()
         parts = []
         for b in range(NB):
-            left = swap(first_ref[b, k, :PART], first_ref[b, k, PART:])
-            right = swap(second_ref[b, k, :PART], second_ref[b, k, PART:])
+            left = swap(first_ref[b, k, :FIRST], first_ref[b, k, FIRST:])
+            right = swap(second_ref[b, k, :SECOND], second_ref[b, k, SECOND:])
             parts.extend([left[0], right[0], left[1], right[1]])
         values = jnp.concatenate(parts, axis=0).T
         work_ref[2 * k : 2 * k + 2] = values.reshape(2, CELLS, C)
     for load in others:
         load.wait()
-    both = jnp.concatenate([high_ref[...], low_ref[...]], axis=0)
     sends = []
     for g in range(8):
-        high, low = split(work_ref[:, g * 8 : (g + 1) * 8, :].reshape(256, C))
-        values = dot(both, high)
-        values = values[:256] + values[256:] + dot(high_ref[...], low)
+        values = product(table_ref, work_ref[:, g * 8 : (g + 1) * 8, :].reshape(256, C))
         span = slice(g * 256, (g + 1) * 256)
         out_ref[span, :] = (cotangent_ref[span, :].astype(f32) + values).astype(bf16)
         rows = pl.ds(g * 256, 256)
@@ -471,20 +478,20 @@
 
 
 def depth_forward(field, tables):
-    args = (field.reshape(2048, C), np.concatenate(tables, axis=0))
+    args = (field.reshape(2048, C), tables)
     out = jax.ShapeDtypeStruct((NB, KZ, 2 * HALF, 128), f32)
     scratch = [*held(*args, out), pltpu.VMEM((2 * KZ, CELLS, C), f32), *sems(9, KZ)]
     return call(depth_kernel, out, args, scratch, 800_000_000, 5_000_000, free).reshape(SPECTRAL)
 
 
 def backward(cot_spec, twiddle, plane_fwd, plane_bwd, first, second, slope, square):
-    args = (cot_spec, twiddle, *plane_fwd, *plane_bwd, first, second, slope, square)
-    outs = (GROUPED, jax.ShapeDtypeStruct(PARTIAL, f32))
+    args = (cot_spec, twiddle, plane_fwd, plane_bwd, first, second, slope, square)
+    outs = (GROUPED, jax.ShapeDtypeStruct((64, 2 * FIRST, 128), f32))
     scratch = [
         *held(*args, *outs),
         pltpu.VMEM(SPECTRAL, f32),
-        pltpu.VMEM(PARTIAL, f32),
-        *sems(8, 7, *[GROUPS] * 3, 8),
+        pltpu.VMEM((64, 2 * FIRST, 128), f32),
+        *sems(8, 5, *[GROUPS] * 3, 8),
     ]
     return call(backward_kernel, outs, args, scratch, 10_000_000_000, 20_000_000, free)
 
@@ -499,40 +506,40 @@
         grid=(GROUPS,),
         out_shape=(
             jax.ShapeDtypeStruct((ROWS, 128), f32),
-            jax.ShapeDtypeStruct((64, 2 * PART + 8, 128), f32),
+            jax.ShapeDtypeStruct((64, 2 * SECOND + 8, 128), f32),
         ),
-        in_specs=by_group(4) + vmem(5),
+        in_specs=by_group(4) + vmem(4),
         out_specs=(pl.BlockSpec((ROWS, 128), lambda g: (0, 0)), *free(1)),
         scratch_shapes=[
             *[pltpu.VMEM((2 * BS, 256), f32), pltpu.VMEM((256, WIDE), f32)] * 2,
-            *[pltpu.VMEM(PARTIAL, f32)] * 2,
+            *[pltpu.VMEM((64, 2 * SECOND, 128), f32)] * 2,
             *sems(8),
         ],
         compiler_params=BIG,
         cost_estimate=pl.CostEstimate(
             flops=8_000_000_000, bytes_accessed=16_000_000, transcendentals=0
         ),
-    )(spec, outer, grad_two, slope, second, first, twiddle, *plane_bwd)
+    )(spec, outer, grad_two, slope, second, first, twiddle, plane_bwd)
 
 
 def field(first, second, cotangent, tables):
     args = (
-        first.reshape(NB, KZ, 2 * PART, 128),
-        second.reshape(NB, KZ, 2 * PART + 8, 128),
+        first.reshape(NB, KZ, 2 * FIRST, 128),
+        second.reshape(NB, KZ, 2 * SECOND + 8, 128),
         cotangent.reshape(2048, C),
-        *tables,
+        tables,
     )
     out = jax.ShapeDtypeStruct((2048, C), bf16)
     scratch = [
-        *held(args[0], args[0], *args[2:], out),
+        *held(args[0], jax.ShapeDtypeStruct((NB, KZ, 2 * SECOND, 128), f32), *args[2:], out),
         pltpu.VMEM((2 * KZ, CELLS, C), f32),
-        *sems(KZ, KZ, 3, 8),
+        *sems(KZ, KZ, 2, 8),
     ]
     return call(field_kernel, out, args, scratch, 1_200_000_000, 7_000_000, free)
 
 
-def rows_of(weight, part):
-    return weight.reshape(4, 2, PART, 2 * BS)[:, part].reshape(BS, 2 * BS)
+def rows_of(weight, start, stop):
+    return weight.reshape(4, HALF, 2 * BS)[:, start:stop].reshape(-1, 2 * BS)
 
 
 def mixing(weight):
@@ -545,7 +552,7 @@
 
 def stacked(value):
     high = lax.reduce_precision(value, 8, 7)
-    return jnp.concatenate([high.astype(bf16), (value - high).astype(bf16)], axis=0)
+    return thrice((high.astype(bf16), (value - high).astype(bf16)), 1)
 
 
 def keep_half(value, axis, flip, bit):
@@ -605,14 +612,14 @@
     spec, outer, slope, square = pl.pallas_call(
         forward_kernel,
         out_shape=(GROUPED,) * 4,
-        in_specs=[pl.BlockSpec(memory_space=pltpu.SMEM)] + vmem(8),
+        in_specs=[pl.BlockSpec(memory_space=pltpu.SMEM)] + vmem(7),
         out_specs=tuple(vmem(4)),
         scratch_shapes=[pltpu.VMEM(SPECTRAL, f32)],
         compiler_params=BIG,
         cost_estimate=pl.CostEstimate(
             flops=8_000_000_000, bytes_accessed=16_000_000, transcendentals=1_500_000
         ),
-    )(doubling, state_spec, twiddle, *plane_fwd, stacked(first), bias_one, stacked(second), bias_two)
+    )(doubling, state_spec, twiddle, plane_fwd, stacked(first), bias_one, stacked(second), bias_two)
 
     second_back = stacked(second.T)
     grad_two, plane = backward(
@@ -620,22 +627,22 @@
         twiddle,
         plane_fwd,
         plane_bwd,
-        stacked(rows_of(first.T, 0)),
+        stacked(rows_of(first.T, 0, FIRST)),
         second_back,
         slope,
         square,
     )
     first_part = exchange(plane)
     rows, plane = rest(
-        spec, outer, grad_two, slope, second_back, stacked(rows_of(first.T, 1)), twiddle, plane_bwd
+        spec, outer, grad_two, slope, second_back, stacked(rows_of(first.T, FIRST, HALF)), twiddle, plane_bwd
     )
     rows = owned_rows(rows)
     plane = lax.dynamic_update_slice(
-        plane, jnp.broadcast_to(rows[None], (64, *rows.shape)), (0, 2 * PART, 0)
+        plane, jnp.broadcast_to(rows[None], (64, *rows.shape)), (0, 2 * SECOND, 0)
     )
     first_part, plane = lax.optimization_barrier((first_part, plane))
     second_part = exchange(plane)
-    rows = join_half(second_part[:, 2 * PART :], "dp", 2, lax.axis_index("dp") // 2)
+    rows = join_half(second_part[:, 2 * SECOND :], "dp", 2, lax.axis_index("dp") // 2)
     state_grad = field(first_part, second_part, cotangent, depth_bwd).reshape(1, 8, 8, NZ, C)
     state_grad, rows = lax.optimization_barrier((state_grad, rows))
     rows = every_row(rows)

time: 319 us -> 312 us (0.978)
  blocking collectives: 48.2 us -> 37.7 us
  waiting for transfers between devices: 119 us -> 124 us
    all_to_all x1, blocking collectives: 48.2 us -> 37.7 us  [exchange(): lax.all_to_all(value, ('px', 'py'), split_axis=0, concat_axis=0, tiled=True)]
    ppermute x7, waiting for transfers between devices: 2.74 us -> 7.86 us  [owned_rows(): lax.ppermute(piece, 'py', [(n, (n + offset) % 8) for n in range(8)])]
  transfers between devices with their start and end apart: 15 -> 15, of which waited for: 8 -> 9; matrix products, arithmetic and copies ran while one was open for 4% -> 4% of each run, Pallas kernels for 15% -> 14%
where the time goes in v5:
time: 312 us; the launch traced here: 311 us
  waiting for transfers between devices  124 us (40%)
  starting transfers between devices  66 us (21%)
  Pallas kernels  65.4 us (21%)
  blocking collectives  37.7 us (12%)
  local copies, waits for them, and re-layouts  10.2 us (3%)
  other arithmetic  6.76 us (2%)
    all_to_all x3, waiting for transfers between devices, exchange(): lax.all_to_all(value, ('px', 'py'), split_axis=0, concat_axis=0, tiled=True)  107 us
    all_to_all x1, blocking collectives, exchange(): lax.all_to_all(value, ('px', 'py'), split_axis=0, concat_axis=0, tiled=True)  37.7 us
    all_to_all x3, starting transfers between devices, exchange(): lax.all_to_all(value, ('px', 'py'), split_axis=0, concat_axis=0, tiled=True)  37 us
    pallas_call x4, Pallas kernels, call(): pl.pallas_call(kernel, out_shape=out_shape, in_specs=place(len(args)), ou...  34.4 us
    pallas_call x1, Pallas kernels, shards(): pl.pallas_call(forward_kernel, out_shape=(GROUPED,) * 4, in_specs=[pl.Blo...  17.7 us
    ppermute x7, starting transfers between devices, owned_rows(): lax.ppermute(piece, 'py', [(n, (n + offset) % 8) for n in range(8)])  15.4 us
    pallas_call x1, Pallas kernels, rest(): pl.pallas_call(rest_kernel, grid=(GROUPS,), out_shape=(jax.ShapeDtypeStru...  13.2 us
    ppermute x2, starting transfers between devices, join_half(): other = lax.ppermute(value, axis, [(n, n ^ flip) for n in range(size)])  8.2 us
  transfers between devices with their start and end apart: 15, of which 9 were waited for; matrix products, arithmetic and copies ran while one was open for 4% of the time, Pallas kernels for 14%

profile of v5, /device:TPU:1, one launch (start us, length us, event | category | flops | bytes accessed | tf_op | source)
XLA Modules:
  0.0 311.2 jit_solution(10112623188797802186)
XLA Ops:
  0.6 6.4 %shard_map.147 = f32[4,16,96,128]{3,2,1,0:T(8,128)} custom-call(bf16[2048,384]{1,0:T(8,128)(2,1)} %bitcast.101, bf16[256,512]{1,0:T(8,128)(2,1)} %constant.161.clone.both_hbm), custom_call_target="tpu_custom_call" | custom-call | flops 800000000 | bytes 5000000 | tf_op jit(solution)/shard_map/pallas_call | solution.py:469
  7.0 15.4 %all-to-all-start.1 = ((f32[64,96,128]{2,1,0:T(8,128)}), f32[64,96,128]{2,1,0:T(8,128)}, u32[]{:S(2)}, u32[]{:S(2)}) async-start(f32[64,96,128]{2,1,0:T(8,128)} %bitcast.94), calls=%async_computation.1 | async-start | bytes 6291456 | tf_op jit(solution)/shard_map/all_to_all | solution.py:594
  22.4 6.3 %shard_map.146 = f32[4,16,96,128]{3,2,1,0:T(8,128)} custom-call(bf16[2048,384]{1,0:T(8,128)(2,1)} %bitcast.96, bf16[256,512]{1,0:T(8,128)(2,1)} %constant.161.clone.both_hbm), custom_call_target="tpu_custom_call" | custom-call | flops 800000000 | bytes 5000000 | tf_op jit(solution)/shard_map/pallas_call | solution.py:469
  28.7 64.0 %all-to-all-done.1.src_ref = f32[64,96,128]{2,1,0:T(8,128)} async-done(((f32[64,96,128]{2,1,0:T(8,128)}), f32[64,96,128]{2,1,0:T(8,128)}, u32[]{:S(2)}, u32[]{:S(2)}) %all-to-all-start.1) | async-done | bytes 3145760 | tf_op jit(solution)/shard_map/all_to_all | solution.py:594
  92.6 11.2 %all-to-all-start = ((f32[64,96,128]{2,1,0:T(8,128)}), f32[64,96,128]{2,1,0:T(8,128)}, u32[]{:S(2)}, u32[]{:S(2)}) async-start(f32[64,96,128]{2,1,0:T(8,128)} %bitcast.93), calls=%async_computation | async-start | bytes 6291456 | tf_op jit(solution)/shard_map/all_to_all | solution.py:594
  112.7 17.7 %shard_map.148 = (f32[8,192,512]{2,1,0:T(8,128)}, f32[8,192,512]{2,1,0:T(8,128)}, f32[8,192,512]{2,1,0:T(8,128)}, f32[8,192,512]{2,1,0:T(8,128)}) custom-call(f32[1,1]{1,0:T(1,128)} %bitcast.18.doubling_ref, f32[64,96,128]{2,1,0:T(8,128)} %all-to-all-done.1.src_ref, f32[64,2,128]{2,1,0:T(2,128)} %constant.162.clone.twiddle_ref.twiddle_hbm, ...), custom_call_target="tpu_custom_call" | custom-call | flops 8000000000 | bytes 16000000 | tf_op jit(solution)/shard_map/pallas_call | solution.py:612
  130.4 43.3 %all-to-all-done.src_hbm = f32[64,96,128]{2,1,0:T(8,128)} async-done(((f32[64,96,128]{2,1,0:T(8,128)}), f32[64,96,128]{2,1,0:T(8,128)}, u32[]{:S(2)}, u32[]{:S(2)}) %all-to-all-start) | async-done | bytes 3145760 | tf_op jit(solution)/shard_map/all_to_all | solution.py:594
  173.7 14.7 %shard_map.149 = (f32[8,192,512]{2,1,0:T(8,128)}, f32[64,64,128]{2,1,0:T(8,128)}) custom-call(f32[64,96,128]{2,1,0:T(8,128)} %all-to-all-done.src_hbm, f32[64,2,128]{2,1,0:T(2,128)} %constant.162.clone.twiddle_ref.twiddle_hbm, bf16[768,256]{1,0:T(8,128)(2,1)} %constant.163.clone.t_ref.t_hbm, bf16[768,256]{1,0:T(8,128)(2,1)} %constant.164.clone.back_hbm.back_ref, ...), custom_call_target="tpu_custom_call" | custom-call | flops 10000000000 | bytes 20000000 | tf_op jit(solution)/shard_map/pallas_call | solution.py:469
  188.4 10.4 %all-to-all-start.2 = ((f32[64,64,128]{2,1,0:T(8,128)}), f32[64,64,128]{2,1,0:T(8,128)}, u32[]{:S(2)}, u32[]{:S(2)}) async-start(f32[64,64,128]{2,1,0:T(8,128)} %get-tuple-element.19), calls=%async_computation.2 | async-start | bytes 4194304 | tf_op jit(solution)/shard_map/all_to_all | solution.py:594
  199.6 13.2 %shard_map.150 = (f32[512,128]{1,0:T(8,128)}, f32[64,40,128]{2,1,0:T(8,128)}) custom-call(f32[8,192,512]{2,1,0:T(8,128)} %get-tuple-element.20.spec_ref, f32[8,192,512]{2,1,0:T(8,128)} %get-tuple-element.21.outer_ref, f32[8,192,512]{2,1,0:T(8,128)} %get-tuple-element.22.two_ref, f32[8,192,512]{2,1,0:T(8,128)} %get-tuple-element.17.slope_hbm.slope_ref, ...), custom_call_target="tpu_custom_call" | custom-call | flops 8000000000 | bytes 16000000 | tf_op jit(solution)/shard_map/pallas_call | solution.py:504
  212.8 0.9 constant_dynamic-slice_fusion.11
  213.7 2.4 collective-permute-start
  216.2 1.0 collective-permute-done
  217.2 0.9 dynamic-slice_add_fusion
  218.6 3.4 %collective-permute-done.1 = f32[128,128]{1,0:T(8,128)S(1)} collective-permute-done((f32[128,128]{1,0:T(8,128)S(1)}, f32[128,128]{1,0:T(8,128)S(1)}, u32[]{:S(2)}, u32[]{:S(2)}) %collective-permute-start.1) | collective-permute-done | bytes 65568 | tf_op jit(solution)/shard_map/ppermute | solution.py:563
  222.0 2.5 collective-permute-start.2
  224.6 3.1 %collective-permute-done.2 = f32[64,128]{1,0:T(8,128)S(1)} collective-permute-done((f32[64,128]{1,0:T(8,128)S(1)}, f32[64,128]{1,0:T(8,128)S(1)}, u32[]{:S(2)}, u32[]{:S(2)}) %collective-permute-start.2) | collective-permute-done | bytes 32800 | tf_op jit(solution)/shard_map/ppermute | solution.py:563
  227.7 1.4 collective-permute-start.3
  229.1 1.3 collective-permute-start.9
  230.5 2.5 collective-permute-start.8
  233.0 2.7 collective-permute-start.7
  235.7 1.6 collective-permute-start.6
  237.3 4.9 %collective-permute-done.3 = f32[8,128]{1,0:T(8,128)S(1)} collective-permute-done((f32[8,128]{1,0:T(8,128)S(1)}, f32[8,128]{1,0:T(8,128)S(1)}, u32[]{:S(2)}, u32[]{:S(2)}) %collective-permute-start.3) | collective-permute-done | bytes 4128 | tf_op jit(solution)/shard_map/ppermute | solution.py:583
  242.2 3.8 %collective-permute-start.5 = (f32[8,128]{1,0:T(8,128)S(1)}, f32[8,128]{1,0:T(8,128)S(1)}, u32[]{:S(2)}, u32[]{:S(2)}) collective-permute-start(f32[8,128]{1,0:T(8,128)S(1)} %get-tuple-element.60), channel_id=1, source_target_pairs={{0,3},{1,4},{2,5},{3,6},{4,7},{5,0},{6,1},{7,2},{8,11},{9,12},{10,... | collective-permute-start | bytes 12296 | tf_op jit(solution)/shard_map/ppermute | solution.py:583
  246.0 2.1 collective-permute-start.4
  248.1 1.0 collective-permute-done.5
  249.1 1.9 collective-permute-done.4
  251.8 37.7 %all_to_all.20 = f32[64,40,128]{2,1,0:T(8,128)S(1)} all-to-all(f32[64,40,128]{2,1,0:T(8,128)} %broadcast_dynamic-update-slice_fusion), channel_id=1, replica_groups=mesh['dp'=4,'px'=8,'py'=8] {'px','py'}, dimensions={0} | all-to-all | bytes 2621440 | tf_op jit(solution)/shard_map/all_to_all | solution.py:594
  290.6 7.1 %shard_map.151 = bf16[2048,384]{1,0:T(8,128)(2,1)} custom-call(f32[4,16,64,128]{3,2,1,0:T(8,128)} %bitcast.31.first_hbm, f32[4,16,40,128]{3,2,1,0:T(8,128)} %bitcast.95, bf16[2048,384]{1,0:T(8,128)(2,1)} %bitcast.97, bf16[256,768]{1,0:T(8,128)(2,1)} %constant.165.clone.table_hbm), custom_call_target="tpu_custom_call" | custom-call | flops 1200000000 | bytes 7000000 | tf_op jit(solution)/shard_map/pallas_call | solution.py:469
  297.7 1.1 maximum_select_fusion
  298.7 7.7 %collective-permute-start.11 = (f32[2,64,8,128]{3,2,1,0:T(8,128)S(1)}, f32[2,64,8,128]{3,2,1,0:T(8,128)S(1)}, u32[]{:S(2)}, u32[]{:S(2)}) collective-permute-start(f32[2,64,8,128]{3,2,1,0:T(8,128)S(1)} %maximum_select_fusion), channel_id=1, source_target_pairs={{0,64},{64,0},{128,192},{192,128},{1,65},{65,1},{129,193},{193,129... | collective-permute-start | bytes 1572872 | tf_op jit(solution)/shard_map/ppermute | solution.py:568
  306.5 1.5 collective-permute-done.11
  (50 shorter events, 15.0 us)
Async XLA Ops:
  7.0 85.6 %all-to-all-start.1 = ((f32[64,96,128]{2,1,0:T(8,128)}), f32[64,96,128]{2,1,0:T(8,128)}, u32[]{:S(2)}, u32[]{:S(2)}) async-start(f32[64,96,128]{2,1,0:T(8,128)} %bitcast.94), calls=%async_computation.1 | async-start | bytes 6291456 | tf_op jit(solution)/shard_map/all_to_all | solution.py:594
  92.6 81.0 %all-to-all-start = ((f32[64,96,128]{2,1,0:T(8,128)}), f32[64,96,128]{2,1,0:T(8,128)}, u32[]{:S(2)}, u32[]{:S(2)}) async-start(f32[64,96,128]{2,1,0:T(8,128)} %bitcast.93), calls=%async_computation | async-start | bytes 6291456 | tf_op jit(solution)/shard_map/all_to_all | solution.py:594
  188.4 63.4 %all-to-all-start.2 = ((f32[64,64,128]{2,1,0:T(8,128)}), f32[64,64,128]{2,1,0:T(8,128)}, u32[]{:S(2)}, u32[]{:S(2)}) async-start(f32[64,64,128]{2,1,0:T(8,128)} %get-tuple-element.19), calls=%async_computation.2 | async-start | bytes 4194304 | tf_op jit(solution)/shard_map/all_to_all | solution.py:594
  213.7 3.4 %collective-permute-start = (f32[256,128]{1,0:T(8,128)S(1)}, f32[256,128]{1,0:T(8,128)S(1)}, u32[]{:S(2)}, u32[]{:S(2)}) collective-permute-start(f32[256,128]{1,0:T(8,128)S(1)} %constant_dynamic-slice_fusion.11), channel_id=1, source_target_pairs={{0,64},{64,0},{128,192},{192,128},{1,65},{65,1},{129,193},{193,129... | collective-permute-start | bytes 393224 | tf_op jit(solution)/shard_map/ppermute | solution.py:563
  218.1 3.9 %collective-permute-start.1 = (f32[128,128]{1,0:T(8,128)S(1)}, f32[128,128]{1,0:T(8,128)S(1)}, u32[]{:S(2)}, u32[]{:S(2)}) collective-permute-start(f32[128,128]{1,0:T(8,128)S(1)} %constant_dynamic-slice_fusion.10), channel_id=1, source_target_pairs={{0,128},{64,192},{128,0},{192,64},{1,129},{65,193},{129,1},{193,65... | collective-permute-start | bytes 196616 | tf_op jit(solution)/shard_map/ppermute | solution.py:563
  222.0 5.6 %collective-permute-start.2 = (f32[64,128]{1,0:T(8,128)S(1)}, f32[64,128]{1,0:T(8,128)S(1)}, u32[]{:S(2)}, u32[]{:S(2)}) collective-permute-start(f32[64,128]{1,0:T(8,128)S(1)} %constant_dynamic-slice_fusion.9), channel_id=1, source_target_pairs={{0,8},{8,0},{16,24},{24,16},{32,40},{40,32},{48,56},{56,48},{1,9},... | collective-permute-start | bytes 98312 | tf_op jit(solution)/shard_map/ppermute | solution.py:563
  227.7 14.5 %collective-permute-start.3 = (f32[8,128]{1,0:T(8,128)S(1)}, f32[8,128]{1,0:T(8,128)S(1)}, u32[]{:S(2)}, u32[]{:S(2)}) collective-permute-start(f32[8,128]{1,0:T(8,128)S(1)} %get-tuple-element.55), channel_id=1, source_target_pairs={{0,1},{1,2},{2,3},{3,4},{4,5},{5,6},{6,7},{7,0},{8,9},{9,10},{10,1... | collective-permute-start | bytes 12296 | tf_op jit(solution)/shard_map/ppermute | solution.py:583
  229.1 16.9 %collective-permute-start.9 = (f32[8,128]{1,0:T(8,128)S(1)}, f32[8,128]{1,0:T(8,128)S(1)}, u32[]{:S(2)}, u32[]{:S(2)}) collective-permute-start(f32[8,128]{1,0:T(8,128)S(1)} %get-tuple-element.56), channel_id=1, source_target_pairs={{0,7},{1,0},{2,1},{3,2},{4,3},{5,4},{6,5},{7,6},{8,15},{9,8},{10,9... | collective-permute-start | bytes 12296 | tf_op jit(solution)/shard_map/ppermute | solution.py:583
  230.5 17.6 %collective-permute-start.8 = (f32[8,128]{1,0:T(8,128)S(1)}, f32[8,128]{1,0:T(8,128)S(1)}, u32[]{:S(2)}, u32[]{:S(2)}) collective-permute-start(f32[8,128]{1,0:T(8,128)S(1)} %get-tuple-element.57), channel_id=1, source_target_pairs={{0,6},{1,7},{2,0},{3,1},{4,2},{5,3},{6,4},{7,5},{8,14},{9,15},{10,... | collective-permute-start | bytes 12296 | tf_op jit(solution)/shard_map/ppermute | solution.py:583
  233.0 15.1 %collective-permute-start.7 = (f32[8,128]{1,0:T(8,128)S(1)}, f32[8,128]{1,0:T(8,128)S(1)}, u32[]{:S(2)}, u32[]{:S(2)}) collective-permute-start(f32[8,128]{1,0:T(8,128)S(1)} %get-tuple-element.58), channel_id=1, source_target_pairs={{0,5},{1,6},{2,7},{3,0},{4,1},{5,2},{6,3},{7,4},{8,13},{9,14},{10,... | collective-permute-start | bytes 12296 | tf_op jit(solution)/shard_map/ppermute | solution.py:583
  235.7 12.4 %collective-permute-start.6 = (f32[8,128]{1,0:T(8,128)S(1)}, f32[8,128]{1,0:T(8,128)S(1)}, u32[]{:S(2)}, u32[]{:S(2)}) collective-permute-start(f32[8,128]{1,0:T(8,128)S(1)} %get-tuple-element.59), channel_id=1, source_target_pairs={{0,4},{1,5},{2,6},{3,7},{4,0},{5,1},{6,2},{7,3},{8,12},{9,13},{10,... | collective-permute-start | bytes 12296 | tf_op jit(solution)/shard_map/ppermute | solution.py:583
  242.2 6.9 %collective-permute-start.5 = (f32[8,128]{1,0:T(8,128)S(1)}, f32[8,128]{1,0:T(8,128)S(1)}, u32[]{:S(2)}, u32[]{:S(2)}) collective-permute-start(f32[8,128]{1,0:T(8,128)S(1)} %get-tuple-element.60), channel_id=1, source_target_pairs={{0,3},{1,4},{2,5},{3,6},{4,7},{5,0},{6,1},{7,2},{8,11},{9,12},{10,... | collective-permute-start | bytes 12296 | tf_op jit(solution)/shard_map/ppermute | solution.py:583
  246.0 5.0 %collective-permute-start.4 = (f32[8,128]{1,0:T(8,128)S(1)}, f32[8,128]{1,0:T(8,128)S(1)}, u32[]{:S(2)}, u32[]{:S(2)}) collective-permute-start(f32[8,128]{1,0:T(8,128)S(1)} %get-tuple-element.61), channel_id=1, source_target_pairs={{0,2},{1,3},{2,4},{3,5},{4,6},{5,7},{6,0},{7,1},{8,10},{9,11},{10,... | collective-permute-start | bytes 12296 | tf_op jit(solution)/shard_map/ppermute | solution.py:583
  289.5 1.1 copy-start
  289.5 8.1 %collective-permute-start.10 = (f32[64,8,128]{2,1,0:T(8,128)S(1)}, f32[64,8,128]{2,1,0:T(8,128)}, u32[]{:S(2)}, u32[]{:S(2)}) collective-permute-start(f32[64,8,128]{2,1,0:T(8,128)S(1)} %get-tuple-element.37), channel_id=1, source_target_pairs={{0,128},{64,192},{128,0},{192,64},{1,129},{65,193},{129,1},{193,65... | collective-permute-start | bytes 786440 | tf_op jit(solution)/shard_map/ppermute | solution.py:568
  298.7 9.3 %collective-permute-start.11 = (f32[2,64,8,128]{3,2,1,0:T(8,128)S(1)}, f32[2,64,8,128]{3,2,1,0:T(8,128)S(1)}, u32[]{:S(2)}, u32[]{:S(2)}) collective-permute-start(f32[2,64,8,128]{3,2,1,0:T(8,128)S(1)} %maximum_select_fusion), channel_id=1, source_target_pairs={{0,64},{64,0},{128,192},{192,128},{1,65},{65,1},{129,193},{193,129... | collective-permute-start | bytes 1572872 | tf_op jit(solution)/shard_map/ppermute | solution.py:568

commit v6 on v5

--- a/solution.py
+++ b/solution.py
@@ -17,7 +17,7 @@
 KZ = 16
 C = 384
 HALF = BS // 2
-FIRST = 32
+FIRST = 40
 SECOND = HALF - FIRST
 CELLS = 64
 STEP = 8
@@ -448,6 +448,38 @@
         send.wait()
 
 
+def gather_kernel(core_ref, low_ref, *refs):
+    sources, (one_ref, bias_one_ref, two_ref, bias_two_ref, all_ref) = refs[:4], refs[4:]
+    core = core_ref[0, 0]
+    low = low_ref[0, 0]
+    for n, source in enumerate(sources):
+        place = (core + n // 2) % 2 * 2 + (low + n % 2) % 2
+        start = pl.multiple_of(place * (ROWS // 4), ROWS // 4)
+        all_ref[:, pl.ds(start, ROWS // 4), :] = source[...].reshape(NB, ROWS // 4, 128)
+    for b in range(NB):
+        for q in range(2):
+            one_ref[q, b] = all_ref[b, q * BS : (q + 1) * BS, :BS]
+            two_ref[q, b] = all_ref[b, (2 + q) * BS : (3 + q) * BS, :BS]
+            bias_one_ref[q, b : b + 1] = all_ref[b, 4 * BS + q : 4 * BS + q + 1, :BS]
+            bias_two_ref[q, b : b + 1] = all_ref[b, 4 * BS + 2 + q : 4 * BS + 3 + q, :BS]
+
+
+def gathered(sources):
+    dp = lax.axis_index("dp")
+    bits = [(dp % 2).reshape(1, 1).astype(jnp.int32), (dp // 2).reshape(1, 1).astype(jnp.int32)]
+    weight = jax.ShapeDtypeStruct((2, NB, BS, BS), f32)
+    bias = jax.ShapeDtypeStruct((2, NB, BS), f32)
+    return pl.pallas_call(
+        gather_kernel,
+        out_shape=(weight, bias, weight, bias),
+        in_specs=[pl.BlockSpec(memory_space=pltpu.SMEM)] * 2 + vmem(4),
+        out_specs=tuple(vmem(4)),
+        scratch_shapes=[pltpu.VMEM((NB, ROWS, 128), f32)],
+        compiler_params=pltpu.CompilerParams(vmem_limit_bytes=16 * 1024 * 1024),
+        cost_estimate=pl.CostEstimate(flops=0, bytes_accessed=2_000_000, transcendentals=0),
+    )(*bits, *sources)
+
+
 def vmem(n):
     return [pl.BlockSpec(memory_space=pltpu.VMEM)] * n
 
@@ -563,12 +595,6 @@
     return mine + lax.ppermute(other, axis, [(n, n ^ flip) for n in range(size)])
 
 
-def join_half(value, axis, flip, bit):
-    size = lax.axis_size(axis)
-    other = lax.ppermute(value, axis, [(n, n ^ flip) for n in range(size)])
-    return jnp.where(bit == 0, jnp.stack([value, other]), jnp.stack([other, value]))
-
-
 def owned_rows(rows):
     dp = lax.axis_index("dp")
     px = lax.axis_index("px")
@@ -584,10 +610,8 @@
     return total
 
 
-def every_row(total):
-    total = join_half(total, "dp", 1, lax.axis_index("dp") % 2)
-    total = total.reshape(2, 2, NB, 2, 8, ROWS // 64, 128)
-    return total.transpose(2, 0, 1, 3, 4, 5, 6).reshape(NB, ROWS, 128)
+def partner(value, flip):
+    return lax.ppermute(value, "dp", [(n, n ^ flip) for n in range(4)])
 
 
 def exchange(value):
@@ -642,21 +666,13 @@
     )
     first_part, plane = lax.optimization_barrier((first_part, plane))
     second_part = exchange(plane)
-    rows = join_half(second_part[:, 2 * SECOND :], "dp", 2, lax.axis_index("dp") // 2)
+    mine = second_part[:, 2 * SECOND :]
+    across = partner(mine, 1)
+    beside = partner(mine, 2)
     state_grad = field(first_part, second_part, cotangent, depth_bwd).reshape(1, 8, 8, NZ, C)
-    state_grad, rows = lax.optimization_barrier((state_grad, rows))
-    rows = every_row(rows)
-    grads_one = rows[:, : 2 * BS, :BS].reshape(NB, 2, BS, BS).transpose(1, 0, 2, 3)
-    grads_two = rows[:, 2 * BS : 4 * BS, :BS].reshape(NB, 2, BS, BS).transpose(1, 0, 2, 3)
-    biases = rows[:, 4 * BS : 4 * BS + 4, :BS].reshape(NB, 2, 2, BS)
-
-    return (
-        state_grad,
-        grads_one,
-        biases[:, 0].transpose(1, 0, 2),
-        grads_two,
-        biases[:, 1].transpose(1, 0, 2),
-    )
+    state_grad, across, beside = lax.optimization_barrier((state_grad, across, beside))
+    sums = gathered((mine, beside, across, partner(beside, 1)))
+    return (state_grad, *sums)
 
 
 def solution(mesh):

time: 312 us -> 309 us (level)
  waiting for transfers between devices: 124 us -> 136 us
  blocking collectives: 37.7 us -> 25.9 us
  local copies, waits for them, and re-layouts: 10.2 us -> 6.83 us
    ppermute x7, waiting for transfers between devices: 7.86 us -> 20 us  [owned_rows(): lax.ppermute(piece, 'py', [(n, (n + offset) % 8) for n in range(8)])]
    all_to_all x1, blocking collectives: 37.7 us -> 25.9 us  [exchange(): lax.all_to_all(value, ('px', 'py'), split_axis=0, concat_axis=0, tiled=True)]
    unnamed x8 -> x4, local copies, waits for them, and re-layouts: 3.47 us -> 0.17 us
    ppermute x2 -> x3, starting transfers between devices: 8.2 us -> 8.94 us  [partner(): return lax.ppermute(value, 'dp', [(n, n ^ flip) for n in range(4)])]
  transfers between devices with their start and end apart: 15 -> 16, of which waited for: 9 -> 9; matrix products, arithmetic and copies ran while one was open for 4% -> 4% of each run, Pallas kernels for 14% -> 14%
where the time goes in v6:
time: 309 us
  waiting for transfers between devices  136 us (44%)
  Pallas kernels  67.1 us (22%)
  starting transfers between devices  66.6 us (22%)
  blocking collectives  25.9 us (8%)
  local copies, waits for them, and re-layouts  6.83 us (2%)
  other arithmetic  5.29 us (2%)
    all_to_all x3, waiting for transfers between devices, exchange(): lax.all_to_all(value, ('px', 'py'), split_axis=0, concat_axis=0, tiled=True)  107 us
    all_to_all x3, starting transfers between devices, exchange(): lax.all_to_all(value, ('px', 'py'), split_axis=0, concat_axis=0, tiled=True)  37.1 us
    pallas_call x4, Pallas kernels, call(): pl.pallas_call(kernel, out_shape=out_shape, in_specs=place(len(args)), ou...  35 us
    all_to_all x1, blocking collectives, exchange(): lax.all_to_all(value, ('px', 'py'), split_axis=0, concat_axis=0, tiled=True)  25.9 us
    ppermute x7, waiting for transfers between devices, owned_rows(): lax.ppermute(piece, 'py', [(n, (n + offset) % 8) for n in range(8)])  20 us
    pallas_call x1, Pallas kernels, shards(): pl.pallas_call(forward_kernel, out_shape=(GROUPED,) * 4, in_specs=[pl.Blo...  17.7 us
    ppermute x7, starting transfers between devices, owned_rows(): lax.ppermute(piece, 'py', [(n, (n + offset) % 8) for n in range(8)])  15.5 us
    pallas_call x1, Pallas kernels, rest(): pl.pallas_call(rest_kernel, grid=(GROUPS,), out_shape=(jax.ShapeDtypeStru...  13.4 us
  transfers between devices with their start and end apart: 16, of which 9 were waited for; matrix products, arithmetic and copies ran while one was open for 4% of the time, Pallas kernels for 14%

profile of v6, /device:TPU:1, one launch (start us, length us, event | category | flops | bytes accessed | tf_op | source)
XLA Modules:
  0.0 308.6 jit_solution(9628212783921871936)
XLA Ops:
  0.6 6.4 %shard_map.147 = f32[4,16,96,128]{3,2,1,0:T(8,128)} custom-call(bf16[2048,384]{1,0:T(8,128)(2,1)} %bitcast.78, bf16[256,512]{1,0:T(8,128)(2,1)} %constant.159.clone.both_hbm), custom_call_target="tpu_custom_call" | custom-call | flops 800000000 | bytes 5000000 | tf_op jit(solution)/shard_map/pallas_call | solution.py:501
  7.0 15.4 %all-to-all-start.1 = ((f32[64,96,128]{2,1,0:T(8,128)}), f32[64,96,128]{2,1,0:T(8,128)}, u32[]{:S(2)}, u32[]{:S(2)}) async-start(f32[64,96,128]{2,1,0:T(8,128)} %bitcast.74), calls=%async_computation.1 | async-start | bytes 6291456 | tf_op jit(solution)/shard_map/all_to_all | solution.py:618
  22.4 6.3 %shard_map.146 = f32[4,16,96,128]{3,2,1,0:T(8,128)} custom-call(bf16[2048,384]{1,0:T(8,128)(2,1)} %bitcast.75, bf16[256,512]{1,0:T(8,128)(2,1)} %constant.159.clone.both_hbm), custom_call_target="tpu_custom_call" | custom-call | flops 800000000 | bytes 5000000 | tf_op jit(solution)/shard_map/pallas_call | solution.py:501
  28.7 63.9 %all-to-all-done.1.src_ref = f32[64,96,128]{2,1,0:T(8,128)} async-done(((f32[64,96,128]{2,1,0:T(8,128)}), f32[64,96,128]{2,1,0:T(8,128)}, u32[]{:S(2)}, u32[]{:S(2)}) %all-to-all-start.1) | async-done | bytes 3145760 | tf_op jit(solution)/shard_map/all_to_all | solution.py:618
  92.6 11.2 %all-to-all-start = ((f32[64,96,128]{2,1,0:T(8,128)}), f32[64,96,128]{2,1,0:T(8,128)}, u32[]{:S(2)}, u32[]{:S(2)}) async-start(f32[64,96,128]{2,1,0:T(8,128)} %bitcast.73), calls=%async_computation | async-start | bytes 6291456 | tf_op jit(solution)/shard_map/all_to_all | solution.py:618
  109.0 0.9 copy.23.w2
  112.7 17.7 %shard_map.148 = (f32[8,192,512]{2,1,0:T(8,128)}, f32[8,192,512]{2,1,0:T(8,128)}, f32[8,192,512]{2,1,0:T(8,128)}, f32[8,192,512]{2,1,0:T(8,128)}) custom-call(f32[1,1]{1,0:T(1,128)} %bitcast.18.doubling_ref, f32[64,96,128]{2,1,0:T(8,128)} %all-to-all-done.1.src_ref, f32[64,2,128]{2,1,0:T(2,128)} %constant.160.clone.twiddle_ref.twiddle_hbm, ...), custom_call_target="tpu_custom_call" | custom-call | flops 8000000000 | bytes 16000000 | tf_op jit(solution)/shard_map/pallas_call | solution.py:636
  130.4 43.2 %all-to-all-done.src_hbm = f32[64,96,128]{2,1,0:T(8,128)} async-done(((f32[64,96,128]{2,1,0:T(8,128)}), f32[64,96,128]{2,1,0:T(8,128)}, u32[]{:S(2)}, u32[]{:S(2)}) %all-to-all-start) | async-done | bytes 3145760 | tf_op jit(solution)/shard_map/all_to_all | solution.py:618
  173.7 15.2 %shard_map.149 = (f32[8,192,512]{2,1,0:T(8,128)}, f32[64,80,128]{2,1,0:T(8,128)}) custom-call(f32[64,96,128]{2,1,0:T(8,128)} %all-to-all-done.src_hbm, f32[64,2,128]{2,1,0:T(2,128)} %constant.160.clone.twiddle_ref.twiddle_hbm, bf16[768,256]{1,0:T(8,128)(2,1)} %constant.161.clone.t_ref.t_hbm, bf16[768,256]{1,0:T(8,128)(2,1)} %constant.162.clone.back_hbm.back_ref, ...), custom_call_target="tpu_custom_call" | custom-call | flops 10000000000 | bytes 20000000 | tf_op jit(solution)/shard_map/pallas_call | solution.py:501
  188.9 10.6 %all-to-all-start.2 = ((f32[64,80,128]{2,1,0:T(8,128)}), f32[64,80,128]{2,1,0:T(8,128)}, u32[]{:S(2)}, u32[]{:S(2)}) async-start(f32[64,80,128]{2,1,0:T(8,128)} %get-tuple-element.24), calls=%async_computation.2 | async-start | bytes 5242880 | tf_op jit(solution)/shard_map/all_to_all | solution.py:618
  200.3 13.4 %shard_map.150 = (f32[512,128]{1,0:T(8,128)}, f32[64,24,128]{2,1,0:T(8,128)}) custom-call(f32[8,192,512]{2,1,0:T(8,128)} %get-tuple-element.25.spec_ref, f32[8,192,512]{2,1,0:T(8,128)} %get-tuple-element.26.outer_ref, f32[8,192,512]{2,1,0:T(8,128)} %get-tuple-element.27.two_ref, f32[8,192,512]{2,1,0:T(8,128)} %get-tuple-element.22.slope_hbm.slope_ref, ...), custom_call_target="tpu_custom_call" | custom-call | flops 8000000000 | bytes 16000000 | tf_op jit(solution)/shard_map/pallas_call | solution.py:536
  213.6 0.9 constant_dynamic-slice_fusion.11
  214.6 2.2 collective-permute-start
  216.8 1.0 collective-permute-done
  217.8 0.9 dynamic-slice_add_fusion
  219.2 3.7 %collective-permute-done.1 = f32[128,128]{1,0:T(8,128)S(1)} collective-permute-done((f32[128,128]{1,0:T(8,128)S(1)}, f32[128,128]{1,0:T(8,128)S(1)}, u32[]{:S(2)}, u32[]{:S(2)}) %collective-permute-start.1) | collective-permute-done | bytes 65568 | tf_op jit(solution)/shard_map/ppermute | solution.py:595
  223.0 2.3 collective-permute-start.2
  225.3 2.6 collective-permute-done.2
  227.9 2.7 collective-permute-start.3
  230.7 3.9 %collective-permute-start.8 = (f32[8,128]{1,0:T(8,128)S(1)}, f32[8,128]{1,0:T(8,128)S(1)}, u32[]{:S(2)}, u32[]{:S(2)}) collective-permute-start(f32[8,128]{1,0:T(8,128)S(1)} %get-tuple-element.56), channel_id=1, source_target_pairs={{0,6},{1,7},{2,0},{3,1},{4,2},{5,3},{6,4},{7,5},{8,14},{9,15},{10,... | collective-permute-start | bytes 12296 | tf_op jit(solution)/shard_map/ppermute | solution.py:609
  234.5 1.9 collective-permute-start.7
  236.5 1.7 collective-permute-start.6
  238.2 16.0 %collective-permute-done.3 = f32[8,128]{1,0:T(8,128)S(1)} collective-permute-done((f32[8,128]{1,0:T(8,128)S(1)}, f32[8,128]{1,0:T(8,128)S(1)}, u32[]{:S(2)}, u32[]{:S(2)}) %collective-permute-start.3) | collective-permute-done | bytes 4128 | tf_op jit(solution)/shard_map/ppermute | solution.py:609
  254.2 4.4 %collective-permute-start.5 = (f32[8,128]{1,0:T(8,128)S(1)}, f32[8,128]{1,0:T(8,128)S(1)}, u32[]{:S(2)}, u32[]{:S(2)}) collective-permute-start(f32[8,128]{1,0:T(8,128)S(1)} %get-tuple-element.59), channel_id=1, source_target_pairs={{0,3},{1,4},{2,5},{3,6},{4,7},{5,0},{6,1},{7,2},{8,11},{9,12},{10,... | collective-permute-start | bytes 12296 | tf_op jit(solution)/shard_map/ppermute | solution.py:609
  258.6 0.8 collective-permute-start.4
  259.4 1.2 collective-permute-done.5
  260.7 2.8 collective-permute-done.4
  264.2 25.9 %all_to_all.20 = f32[64,24,128]{2,1,0:T(8,128)S(1)} all-to-all(f32[64,24,128]{2,1,0:T(8,128)} %broadcast_dynamic-update-slice_fusion), channel_id=1, replica_groups=mesh['dp'=4,'px'=8,'py'=8] {'px','py'}, dimensions={0} | all-to-all | bytes 1572864 | tf_op jit(solution)/shard_map/all_to_all | solution.py:618
  290.6 8.3 %collective-permute-start.10 = (f32[64,8,128]{2,1,0:T(8,128)S(1)}, f32[64,8,128]{2,1,0:T(8,128)S(1)}, u32[]{:S(2)}, u32[]{:S(2)}) collective-permute-start(f32[64,8,128]{2,1,0:T(8,128)S(1)} %slice.34.refs_0_), channel_id=1, source_target_pairs={{0,64},{64,0},{128,192},{192,128},{1,65},{65,1},{129,193},{193,129... | collective-permute-start | bytes 786440 | tf_op jit(solution)/shard_map/ppermute | solution.py:614
  298.8 7.1 %shard_map.151 = bf16[2048,384]{1,0:T(8,128)(2,1)} custom-call(f32[4,16,80,128]{3,2,1,0:T(8,128)} %bitcast.31.first_hbm, f32[4,16,24,128]{3,2,1,0:T(8,128)} %bitcast.77, bf16[2048,384]{1,0:T(8,128)(2,1)} %bitcast.76, bf16[256,768]{1,0:T(8,128)(2,1)} %constant.163.clone.table_hbm), custom_call_target="tpu_custom_call" | custom-call | flops 1200000000 | bytes 7000000 | tf_op jit(solution)/shard_map/pallas_call | solution.py:501
  306.1 1.4 collective-permute-done.12.refs_3_
  307.6 1.0 shard_map.152
  (42 shorter events, 10.6 us)
Async XLA Ops:
  7.0 85.6 %all-to-all-start.1 = ((f32[64,96,128]{2,1,0:T(8,128)}), f32[64,96,128]{2,1,0:T(8,128)}, u32[]{:S(2)}, u32[]{:S(2)}) async-start(f32[64,96,128]{2,1,0:T(8,128)} %bitcast.74), calls=%async_computation.1 | async-start | bytes 6291456 | tf_op jit(solution)/shard_map/all_to_all | solution.py:618
  92.6 81.0 %all-to-all-start = ((f32[64,96,128]{2,1,0:T(8,128)}), f32[64,96,128]{2,1,0:T(8,128)}, u32[]{:S(2)}, u32[]{:S(2)}) async-start(f32[64,96,128]{2,1,0:T(8,128)} %bitcast.73), calls=%async_computation | async-start | bytes 6291456 | tf_op jit(solution)/shard_map/all_to_all | solution.py:618
  188.9 75.3 %all-to-all-start.2 = ((f32[64,80,128]{2,1,0:T(8,128)}), f32[64,80,128]{2,1,0:T(8,128)}, u32[]{:S(2)}, u32[]{:S(2)}) async-start(f32[64,80,128]{2,1,0:T(8,128)} %get-tuple-element.24), calls=%async_computation.2 | async-start | bytes 5242880 | tf_op jit(solution)/shard_map/all_to_all | solution.py:618
  214.6 3.2 %collective-permute-start = (f32[256,128]{1,0:T(8,128)S(1)}, f32[256,128]{1,0:T(8,128)S(1)}, u32[]{:S(2)}, u32[]{:S(2)}) collective-permute-start(f32[256,128]{1,0:T(8,128)S(1)} %constant_dynamic-slice_fusion.11), channel_id=1, source_target_pairs={{0,64},{64,0},{128,192},{192,128},{1,65},{65,1},{129,193},{193,129... | collective-permute-start | bytes 393224 | tf_op jit(solution)/shard_map/ppermute | solution.py:595
  218.7 4.2 %collective-permute-start.1 = (f32[128,128]{1,0:T(8,128)S(1)}, f32[128,128]{1,0:T(8,128)S(1)}, u32[]{:S(2)}, u32[]{:S(2)}) collective-permute-start(f32[128,128]{1,0:T(8,128)S(1)} %constant_dynamic-slice_fusion.10), channel_id=1, source_target_pairs={{0,128},{64,192},{128,0},{192,64},{1,129},{65,193},{129,1},{193,65... | collective-permute-start | bytes 196616 | tf_op jit(solution)/shard_map/ppermute | solution.py:595
  223.0 4.9 %collective-permute-start.2 = (f32[64,128]{1,0:T(8,128)S(1)}, f32[64,128]{1,0:T(8,128)S(1)}, u32[]{:S(2)}, u32[]{:S(2)}) collective-permute-start(f32[64,128]{1,0:T(8,128)S(1)} %constant_dynamic-slice_fusion.9), channel_id=1, source_target_pairs={{0,8},{8,0},{16,24},{24,16},{32,40},{40,32},{48,56},{56,48},{1,9},... | collective-permute-start | bytes 98312 | tf_op jit(solution)/shard_map/ppermute | solution.py:595
  227.9 26.3 %collective-permute-start.3 = (f32[8,128]{1,0:T(8,128)S(1)}, f32[8,128]{1,0:T(8,128)S(1)}, u32[]{:S(2)}, u32[]{:S(2)}) collective-permute-start(f32[8,128]{1,0:T(8,128)S(1)} %get-tuple-element.54), channel_id=1, source_target_pairs={{0,1},{1,2},{2,3},{3,4},{4,5},{5,6},{6,7},{7,0},{8,9},{9,10},{10,1... | collective-permute-start | bytes 12296 | tf_op jit(solution)/shard_map/ppermute | solution.py:609
  230.6 28.0 %collective-permute-start.9 = (f32[8,128]{1,0:T(8,128)S(1)}, f32[8,128]{1,0:T(8,128)S(1)}, u32[]{:S(2)}, u32[]{:S(2)}) collective-permute-start(f32[8,128]{1,0:T(8,128)S(1)} %get-tuple-element.55), channel_id=1, source_target_pairs={{0,7},{1,0},{2,1},{3,2},{4,3},{5,4},{6,5},{7,6},{8,15},{9,8},{10,9... | collective-permute-start | bytes 12296 | tf_op jit(solution)/shard_map/ppermute | solution.py:609
  230.7 28.8 %collective-permute-start.8 = (f32[8,128]{1,0:T(8,128)S(1)}, f32[8,128]{1,0:T(8,128)S(1)}, u32[]{:S(2)}, u32[]{:S(2)}) collective-permute-start(f32[8,128]{1,0:T(8,128)S(1)} %get-tuple-element.56), channel_id=1, source_target_pairs={{0,6},{1,7},{2,0},{3,1},{4,2},{5,3},{6,4},{7,5},{8,14},{9,15},{10,... | collective-permute-start | bytes 12296 | tf_op jit(solution)/shard_map/ppermute | solution.py:609
  234.5 24.9 %collective-permute-start.7 = (f32[8,128]{1,0:T(8,128)S(1)}, f32[8,128]{1,0:T(8,128)S(1)}, u32[]{:S(2)}, u32[]{:S(2)}) collective-permute-start(f32[8,128]{1,0:T(8,128)S(1)} %get-tuple-element.57), channel_id=1, source_target_pairs={{0,5},{1,6},{2,7},{3,0},{4,1},{5,2},{6,3},{7,4},{8,13},{9,14},{10,... | collective-permute-start | bytes 12296 | tf_op jit(solution)/shard_map/ppermute | solution.py:609
  236.5 22.9 %collective-permute-start.6 = (f32[8,128]{1,0:T(8,128)S(1)}, f32[8,128]{1,0:T(8,128)S(1)}, u32[]{:S(2)}, u32[]{:S(2)}) collective-permute-start(f32[8,128]{1,0:T(8,128)S(1)} %get-tuple-element.58), channel_id=1, source_target_pairs={{0,4},{1,5},{2,6},{3,7},{4,0},{5,1},{6,2},{7,3},{8,12},{9,13},{10,... | collective-permute-start | bytes 12296 | tf_op jit(solution)/shard_map/ppermute | solution.py:609
  254.2 6.5 %collective-permute-start.5 = (f32[8,128]{1,0:T(8,128)S(1)}, f32[8,128]{1,0:T(8,128)S(1)}, u32[]{:S(2)}, u32[]{:S(2)}) collective-permute-start(f32[8,128]{1,0:T(8,128)S(1)} %get-tuple-element.59), channel_id=1, source_target_pairs={{0,3},{1,4},{2,5},{3,6},{4,7},{5,0},{6,1},{7,2},{8,11},{9,12},{10,... | collective-permute-start | bytes 12296 | tf_op jit(solution)/shard_map/ppermute | solution.py:609
  258.6 4.9 %collective-permute-start.4 = (f32[8,128]{1,0:T(8,128)S(1)}, f32[8,128]{1,0:T(8,128)S(1)}, u32[]{:S(2)}, u32[]{:S(2)}) collective-permute-start(f32[8,128]{1,0:T(8,128)S(1)} %get-tuple-element.60), channel_id=1, source_target_pairs={{0,2},{1,3},{2,4},{3,5},{4,6},{5,7},{6,0},{7,1},{8,10},{9,11},{10,... | collective-permute-start | bytes 12296 | tf_op jit(solution)/shard_map/ppermute | solution.py:609
  290.1 8.8 %copy-start = (f32[64,24,128]{2,1,0:T(8,128)}, f32[64,24,128]{2,1,0:T(8,128)S(1)}, u32[]{:S(2)}) copy-start(f32[64,24,128]{2,1,0:T(8,128)S(1)} %all_to_all.20) | copy-start | bytes 2359300
  290.1 15.8 %collective-permute-start.11 = (f32[64,8,128]{2,1,0:T(8,128)S(1)}, f32[64,8,128]{2,1,0:T(8,128)S(1)}, u32[]{:S(2)}, u32[]{:S(2)}) collective-permute-start(f32[64,8,128]{2,1,0:T(8,128)S(1)} %slice.34.refs_0_), channel_id=1, source_target_pairs={{0,128},{64,192},{128,0},{192,64},{1,129},{65,193},{129,1},{193,65... | collective-permute-start | bytes 786440 | tf_op jit(solution)/shard_map/ppermute | solution.py:614
  290.6 15.4 %collective-permute-start.10 = (f32[64,8,128]{2,1,0:T(8,128)S(1)}, f32[64,8,128]{2,1,0:T(8,128)S(1)}, u32[]{:S(2)}, u32[]{:S(2)}) collective-permute-start(f32[64,8,128]{2,1,0:T(8,128)S(1)} %slice.34.refs_0_), channel_id=1, source_target_pairs={{0,64},{64,0},{128,192},{192,128},{1,65},{65,1},{129,193},{193,129... | collective-permute-start | bytes 786440 | tf_op jit(solution)/shard_map/ppermute | solution.py:614
  305.9 1.6 collective-permute-start.12

commit v7 on v6

--- a/solution.py
+++ b/solution.py
@@ -18,6 +18,7 @@
 C = 384
 HALF = BS // 2
 FIRST = 40
+BATCH = 4
 SECOND = HALF - FIRST
 CELLS = 64
 STEP = 8
@@ -248,7 +249,9 @@
         copies[-1].start()
     table.wait()
     for g in range(8):
-        copies[g].wait()
+        if g % BATCH == 0:
+            for copy in copies[g : g + BATCH]:
+                copy.wait()
         rows = field_ref[g * 256 : (g + 1) * 256, :]
         values = dot(both_ref[...], jnp.concatenate([rows, rows], axis=0))
         work_ref[:, g * 8 : (g + 1) * 8, :] = values.reshape(2 * KZ, 8, C)
@@ -260,7 +263,9 @@
             lower = values[b * BS + HALF : (b + 1) * BS]
             out_ref[b, k, :HALF], out_ref[b, k, HALF:] = swap(upper, lower)
         sends.append(pltpu.make_async_copy(out_ref.at[:, k], out_hbm.at[:, k], out_sems.at[k]))
-        sends[-1].start()
+        if k % BATCH == BATCH - 1:
+            for send in sends[-BATCH:]:
+                send.start()
     for send in sends:
         send.wait()
 
@@ -327,12 +332,15 @@
     spectral = load_group(work_ref, 0, t_ref)
     for g in range(GROUPS):
         following = load_group(work_ref, g + 1, t_ref) if g + 1 < GROUPS else None
-        pltpu.make_async_copy(square_hbm.at[g], square_ref.at[g], square_sems.at[g]).wait()
+        for n in range(g, g + BATCH) if g % BATCH == 0 else ():
+            pltpu.make_async_copy(square_hbm.at[n], square_ref.at[n], square_sems.at[n]).wait()
+            pltpu.make_async_copy(slope_hbm.at[n], slope_ref.at[n], slope_sems.at[n]).wait()
         grad_two = spectral * square_ref[g]
         two_ref[g] = grad_two
         sends.append(pltpu.make_async_copy(two_ref.at[g], two_hbm.at[g], two_sems.at[g]))
-        sends[-1].start()
-        pltpu.make_async_copy(slope_hbm.at[g], slope_ref.at[g], slope_sems.at[g]).wait()
+        if g % BATCH == BATCH - 1:
+            for send in sends[-BATCH:]:
+                send.start()
         grad_one = product(w2, grad_two) * slope_ref[g]
         store_group(part_ref, g, product(w1, grad_one), back_ref)
         spectral = following
@@ -425,8 +433,9 @@
     for load in others:
         load.start()
     for k in range(KZ):
-        loads[k][0].wait()
-        loads[k][1].wait()
+        for load in loads[k : k + BATCH] if k % BATCH == 0 else ():
+            load[0].wait()
+            load[1].wait()
         parts = []
         for b in range(NB):
             left = swap(first_ref[b, k, :FIRST], first_ref[b, k, FIRST:])
@@ -443,7 +452,9 @@
         out_ref[span, :] = (cotangent_ref[span, :].astype(f32) + values).astype(bf16)
         rows = pl.ds(g * 256, 256)
         sends.append(pltpu.make_async_copy(out_ref.at[rows], out_hbm.at[rows], out_sems.at[g]))
-        sends[-1].start()
+        if g % BATCH == BATCH - 1:
+            for send in sends[-BATCH:]:
+                send.start()
     for send in sends:
         send.wait()
 

time: 309 us -> 307 us (level)
  Pallas kernels: 67.1 us -> 63.8 us
    pallas_call x4, Pallas kernels: 35 us -> 31.7 us  [call(): pl.pallas_call(kernel, out_shape=out_shape, in_specs=place(len(args)), ou...]
where the time goes in v7:
time: 307 us; the launch traced here: 306 us
  waiting for transfers between devices  136 us (44%)
  starting transfers between devices  67.3 us (22%)
  Pallas kernels  63.8 us (21%)
  blocking collectives  26.1 us (9%)
  local copies, waits for them, and re-layouts  6.83 us (2%)
  other arithmetic  5.29 us (2%)
    all_to_all x3, waiting for transfers between devices, exchange(): lax.all_to_all(value, ('px', 'py'), split_axis=0, concat_axis=0, tiled=True)  108 us
    all_to_all x3, starting transfers between devices, exchange(): lax.all_to_all(value, ('px', 'py'), split_axis=0, concat_axis=0, tiled=True)  37 us
    pallas_call x4, Pallas kernels, call(): pl.pallas_call(kernel, out_shape=out_shape, in_specs=place(len(args)), ou...  31.7 us
    all_to_all x1, blocking collectives, exchange(): lax.all_to_all(value, ('px', 'py'), split_axis=0, concat_axis=0, tiled=True)  26.1 us
    ppermute x7, waiting for transfers between devices, owned_rows(): lax.ppermute(piece, 'py', [(n, (n + offset) % 8) for n in range(8)])  19.5 us
    pallas_call x1, Pallas kernels, shards(): pl.pallas_call(forward_kernel, out_shape=(GROUPED,) * 4, in_specs=[pl.Blo...  17.7 us
    ppermute x7, starting transfers between devices, owned_rows(): lax.ppermute(piece, 'py', [(n, (n + offset) % 8) for n in range(8)])  16 us
    pallas_call x1, Pallas kernels, rest(): pl.pallas_call(rest_kernel, grid=(GROUPS,), out_shape=(jax.ShapeDtypeStru...  13.4 us
  transfers between devices with their start and end apart: 16, of which 9 were waited for; matrix products, arithmetic and copies ran while one was open for 4% of the time, Pallas kernels for 14%

profile of v7, /device:TPU:1, one launch (start us, length us, event | category | flops | bytes accessed | tf_op | source)
XLA Modules:
  0.0 305.9 jit_solution(1939836132422269543)
XLA Ops:
  0.6 5.8 %shard_map.147 = f32[4,16,96,128]{3,2,1,0:T(8,128)} custom-call(bf16[2048,384]{1,0:T(8,128)(2,1)} %bitcast.78, bf16[256,512]{1,0:T(8,128)(2,1)} %constant.159.clone.both_hbm), custom_call_target="tpu_custom_call" | custom-call | flops 800000000 | bytes 5000000 | tf_op jit(solution)/shard_map/pallas_call | solution.py:512
  6.4 15.4 %all-to-all-start.1 = ((f32[64,96,128]{2,1,0:T(8,128)}), f32[64,96,128]{2,1,0:T(8,128)}, u32[]{:S(2)}, u32[]{:S(2)}) async-start(f32[64,96,128]{2,1,0:T(8,128)} %bitcast.74), calls=%async_computation.1 | async-start | bytes 6291456 | tf_op jit(solution)/shard_map/all_to_all | solution.py:629
  21.8 5.8 %shard_map.146 = f32[4,16,96,128]{3,2,1,0:T(8,128)} custom-call(bf16[2048,384]{1,0:T(8,128)(2,1)} %bitcast.75, bf16[256,512]{1,0:T(8,128)(2,1)} %constant.159.clone.both_hbm), custom_call_target="tpu_custom_call" | custom-call | flops 800000000 | bytes 5000000 | tf_op jit(solution)/shard_map/pallas_call | solution.py:512
  27.5 64.5 %all-to-all-done.1.src_ref = f32[64,96,128]{2,1,0:T(8,128)} async-done(((f32[64,96,128]{2,1,0:T(8,128)}), f32[64,96,128]{2,1,0:T(8,128)}, u32[]{:S(2)}, u32[]{:S(2)}) %all-to-all-start.1) | async-done | bytes 3145760 | tf_op jit(solution)/shard_map/all_to_all | solution.py:629
  92.0 11.2 %all-to-all-start = ((f32[64,96,128]{2,1,0:T(8,128)}), f32[64,96,128]{2,1,0:T(8,128)}, u32[]{:S(2)}, u32[]{:S(2)}) async-start(f32[64,96,128]{2,1,0:T(8,128)} %bitcast.73), calls=%async_computation | async-start | bytes 6291456 | tf_op jit(solution)/shard_map/all_to_all | solution.py:629
  108.4 0.9 copy.23.w2
  112.1 17.7 %shard_map.148 = (f32[8,192,512]{2,1,0:T(8,128)}, f32[8,192,512]{2,1,0:T(8,128)}, f32[8,192,512]{2,1,0:T(8,128)}, f32[8,192,512]{2,1,0:T(8,128)}) custom-call(f32[1,1]{1,0:T(1,128)} %bitcast.18.doubling_ref, f32[64,96,128]{2,1,0:T(8,128)} %all-to-all-done.1.src_ref, f32[64,2,128]{2,1,0:T(2,128)} %constant.160.clone.twiddle_ref.twiddle_hbm, ...), custom_call_target="tpu_custom_call" | custom-call | flops 8000000000 | bytes 16000000 | tf_op jit(solution)/shard_map/pallas_call | solution.py:647
  129.9 43.2 %all-to-all-done.src_hbm = f32[64,96,128]{2,1,0:T(8,128)} async-done(((f32[64,96,128]{2,1,0:T(8,128)}), f32[64,96,128]{2,1,0:T(8,128)}, u32[]{:S(2)}, u32[]{:S(2)}) %all-to-all-start) | async-done | bytes 3145760 | tf_op jit(solution)/shard_map/all_to_all | solution.py:629
  173.1 13.8 %shard_map.149 = (f32[8,192,512]{2,1,0:T(8,128)}, f32[64,80,128]{2,1,0:T(8,128)}) custom-call(f32[64,96,128]{2,1,0:T(8,128)} %all-to-all-done.src_hbm, f32[64,2,128]{2,1,0:T(2,128)} %constant.160.clone.twiddle_ref.twiddle_hbm, bf16[768,256]{1,0:T(8,128)(2,1)} %constant.161.clone.t_ref.t_hbm, bf16[768,256]{1,0:T(8,128)(2,1)} %constant.162.clone.back_hbm.back_ref, ...), custom_call_target="tpu_custom_call" | custom-call | flops 10000000000 | bytes 20000000 | tf_op jit(solution)/shard_map/pallas_call | solution.py:512
  186.9 10.4 %all-to-all-start.2 = ((f32[64,80,128]{2,1,0:T(8,128)}), f32[64,80,128]{2,1,0:T(8,128)}, u32[]{:S(2)}, u32[]{:S(2)}) async-start(f32[64,80,128]{2,1,0:T(8,128)} %get-tuple-element.24), calls=%async_computation.2 | async-start | bytes 5242880 | tf_op jit(solution)/shard_map/all_to_all | solution.py:629
  198.0 13.4 %shard_map.150 = (f32[512,128]{1,0:T(8,128)}, f32[64,24,128]{2,1,0:T(8,128)}) custom-call(f32[8,192,512]{2,1,0:T(8,128)} %get-tuple-element.25.spec_ref, f32[8,192,512]{2,1,0:T(8,128)} %get-tuple-element.26.outer_ref, f32[8,192,512]{2,1,0:T(8,128)} %get-tuple-element.27.two_ref, f32[8,192,512]{2,1,0:T(8,128)} %get-tuple-element.22.slope_hbm.slope_ref, ...), custom_call_target="tpu_custom_call" | custom-call | flops 8000000000 | bytes 16000000 | tf_op jit(solution)/shard_map/pallas_call | solution.py:547
  211.4 0.9 constant_dynamic-slice_fusion.11
  212.4 2.4 collective-permute-start
  214.8 1.0 collective-permute-done
  215.8 0.9 dynamic-slice_add_fusion
  217.2 3.7 %collective-permute-done.1 = f32[128,128]{1,0:T(8,128)S(1)} collective-permute-done((f32[128,128]{1,0:T(8,128)S(1)}, f32[128,128]{1,0:T(8,128)S(1)}, u32[]{:S(2)}, u32[]{:S(2)}) %collective-permute-start.1) | collective-permute-done | bytes 65568 | tf_op jit(solution)/shard_map/ppermute | solution.py:606
  220.9 2.6 collective-permute-start.2
  223.5 2.4 collective-permute-done.2
  225.9 3.2 %collective-permute-start.3 = (f32[8,128]{1,0:T(8,128)S(1)}, f32[8,128]{1,0:T(8,128)S(1)}, u32[]{:S(2)}, u32[]{:S(2)}) collective-permute-start(f32[8,128]{1,0:T(8,128)S(1)} %get-tuple-element.54), channel_id=1, source_target_pairs={{0,1},{1,2},{2,3},{3,4},{4,5},{5,6},{6,7},{7,0},{8,9},{9,10},{10,1... | collective-permute-start | bytes 12296 | tf_op jit(solution)/shard_map/ppermute | solution.py:620
  229.5 3.0 collective-permute-start.8
  232.5 1.9 collective-permute-start.7
  234.4 1.9 collective-permute-start.6
  236.4 15.7 %collective-permute-done.3 = f32[8,128]{1,0:T(8,128)S(1)} collective-permute-done((f32[8,128]{1,0:T(8,128)S(1)}, f32[8,128]{1,0:T(8,128)S(1)}, u32[]{:S(2)}, u32[]{:S(2)}) %collective-permute-start.3) | collective-permute-done | bytes 4128 | tf_op jit(solution)/shard_map/ppermute | solution.py:620
  252.1 4.3 %collective-permute-start.5 = (f32[8,128]{1,0:T(8,128)S(1)}, f32[8,128]{1,0:T(8,128)S(1)}, u32[]{:S(2)}, u32[]{:S(2)}) collective-permute-start(f32[8,128]{1,0:T(8,128)S(1)} %get-tuple-element.59), channel_id=1, source_target_pairs={{0,3},{1,4},{2,5},{3,6},{4,7},{5,0},{6,1},{7,2},{8,11},{9,12},{10,... | collective-permute-start | bytes 12296 | tf_op jit(solution)/shard_map/ppermute | solution.py:620
  256.4 1.2 collective-permute-start.4
  257.6 1.2 collective-permute-done.5
  258.8 2.6 collective-permute-done.4
  262.1 26.1 %all_to_all.20 = f32[64,24,128]{2,1,0:T(8,128)S(1)} all-to-all(f32[64,24,128]{2,1,0:T(8,128)} %broadcast_dynamic-update-slice_fusion), channel_id=1, replica_groups=mesh['dp'=4,'px'=8,'py'=8] {'px','py'}, dimensions={0} | all-to-all | bytes 1572864 | tf_op jit(solution)/shard_map/all_to_all | solution.py:629
  288.7 8.2 %collective-permute-start.10 = (f32[64,8,128]{2,1,0:T(8,128)S(1)}, f32[64,8,128]{2,1,0:T(8,128)S(1)}, u32[]{:S(2)}, u32[]{:S(2)}) collective-permute-start(f32[64,8,128]{2,1,0:T(8,128)S(1)} %slice.34.refs_0_), channel_id=1, source_target_pairs={{0,64},{64,0},{128,192},{192,128},{1,65},{65,1},{129,193},{193,129... | collective-permute-start | bytes 786440 | tf_op jit(solution)/shard_map/ppermute | solution.py:625
  296.9 6.3 %shard_map.151 = bf16[2048,384]{1,0:T(8,128)(2,1)} custom-call(f32[4,16,80,128]{3,2,1,0:T(8,128)} %bitcast.31.first_hbm, f32[4,16,24,128]{3,2,1,0:T(8,128)} %bitcast.77, bf16[2048,384]{1,0:T(8,128)(2,1)} %bitcast.76, bf16[256,768]{1,0:T(8,128)(2,1)} %constant.163.clone.table_hbm), custom_call_target="tpu_custom_call" | custom-call | flops 1200000000 | bytes 7000000 | tf_op jit(solution)/shard_map/pallas_call | solution.py:512
  303.5 1.4 collective-permute-done.12.refs_3_
  304.9 1.0 shard_map.152
  (42 shorter events, 11.0 us)
Async XLA Ops:
  6.4 85.6 %all-to-all-start.1 = ((f32[64,96,128]{2,1,0:T(8,128)}), f32[64,96,128]{2,1,0:T(8,128)}, u32[]{:S(2)}, u32[]{:S(2)}) async-start(f32[64,96,128]{2,1,0:T(8,128)} %bitcast.74), calls=%async_computation.1 | async-start | bytes 6291456 | tf_op jit(solution)/shard_map/all_to_all | solution.py:629
  92.0 81.0 %all-to-all-start = ((f32[64,96,128]{2,1,0:T(8,128)}), f32[64,96,128]{2,1,0:T(8,128)}, u32[]{:S(2)}, u32[]{:S(2)}) async-start(f32[64,96,128]{2,1,0:T(8,128)} %bitcast.73), calls=%async_computation | async-start | bytes 6291456 | tf_op jit(solution)/shard_map/all_to_all | solution.py:629
  186.9 75.2 %all-to-all-start.2 = ((f32[64,80,128]{2,1,0:T(8,128)}), f32[64,80,128]{2,1,0:T(8,128)}, u32[]{:S(2)}, u32[]{:S(2)}) async-start(f32[64,80,128]{2,1,0:T(8,128)} %get-tuple-element.24), calls=%async_computation.2 | async-start | bytes 5242880 | tf_op jit(solution)/shard_map/all_to_all | solution.py:629
  212.4 3.4 %collective-permute-start = (f32[256,128]{1,0:T(8,128)S(1)}, f32[256,128]{1,0:T(8,128)S(1)}, u32[]{:S(2)}, u32[]{:S(2)}) collective-permute-start(f32[256,128]{1,0:T(8,128)S(1)} %constant_dynamic-slice_fusion.11), channel_id=1, source_target_pairs={{0,64},{64,0},{128,192},{192,128},{1,65},{65,1},{129,193},{193,129... | collective-permute-start | bytes 393224 | tf_op jit(solution)/shard_map/ppermute | solution.py:606
  216.7 4.2 %collective-permute-start.1 = (f32[128,128]{1,0:T(8,128)S(1)}, f32[128,128]{1,0:T(8,128)S(1)}, u32[]{:S(2)}, u32[]{:S(2)}) collective-permute-start(f32[128,128]{1,0:T(8,128)S(1)} %constant_dynamic-slice_fusion.10), channel_id=1, source_target_pairs={{0,128},{64,192},{128,0},{192,64},{1,129},{65,193},{129,1},{193,65... | collective-permute-start | bytes 196616 | tf_op jit(solution)/shard_map/ppermute | solution.py:606
  220.9 4.9 %collective-permute-start.2 = (f32[64,128]{1,0:T(8,128)S(1)}, f32[64,128]{1,0:T(8,128)S(1)}, u32[]{:S(2)}, u32[]{:S(2)}) collective-permute-start(f32[64,128]{1,0:T(8,128)S(1)} %constant_dynamic-slice_fusion.9), channel_id=1, source_target_pairs={{0,8},{8,0},{16,24},{24,16},{32,40},{40,32},{48,56},{56,48},{1,9},... | collective-permute-start | bytes 98312 | tf_op jit(solution)/shard_map/ppermute | solution.py:606
  225.9 26.2 %collective-permute-start.3 = (f32[8,128]{1,0:T(8,128)S(1)}, f32[8,128]{1,0:T(8,128)S(1)}, u32[]{:S(2)}, u32[]{:S(2)}) collective-permute-start(f32[8,128]{1,0:T(8,128)S(1)} %get-tuple-element.54), channel_id=1, source_target_pairs={{0,1},{1,2},{2,3},{3,4},{4,5},{5,6},{6,7},{7,0},{8,9},{9,10},{10,1... | collective-permute-start | bytes 12296 | tf_op jit(solution)/shard_map/ppermute | solution.py:620
  229.1 27.3 %collective-permute-start.9 = (f32[8,128]{1,0:T(8,128)S(1)}, f32[8,128]{1,0:T(8,128)S(1)}, u32[]{:S(2)}, u32[]{:S(2)}) collective-permute-start(f32[8,128]{1,0:T(8,128)S(1)} %get-tuple-element.55), channel_id=1, source_target_pairs={{0,7},{1,0},{2,1},{3,2},{4,3},{5,4},{6,5},{7,6},{8,15},{9,8},{10,9... | collective-permute-start | bytes 12296 | tf_op jit(solution)/shard_map/ppermute | solution.py:620
  229.5 28.1 %collective-permute-start.8 = (f32[8,128]{1,0:T(8,128)S(1)}, f32[8,128]{1,0:T(8,128)S(1)}, u32[]{:S(2)}, u32[]{:S(2)}) collective-permute-start(f32[8,128]{1,0:T(8,128)S(1)} %get-tuple-element.56), channel_id=1, source_target_pairs={{0,6},{1,7},{2,0},{3,1},{4,2},{5,3},{6,4},{7,5},{8,14},{9,15},{10,... | collective-permute-start | bytes 12296 | tf_op jit(solution)/shard_map/ppermute | solution.py:620
  232.5 25.1 %collective-permute-start.7 = (f32[8,128]{1,0:T(8,128)S(1)}, f32[8,128]{1,0:T(8,128)S(1)}, u32[]{:S(2)}, u32[]{:S(2)}) collective-permute-start(f32[8,128]{1,0:T(8,128)S(1)} %get-tuple-element.57), channel_id=1, source_target_pairs={{0,5},{1,6},{2,7},{3,0},{4,1},{5,2},{6,3},{7,4},{8,13},{9,14},{10,... | collective-permute-start | bytes 12296 | tf_op jit(solution)/shard_map/ppermute | solution.py:620
  234.4 23.2 %collective-permute-start.6 = (f32[8,128]{1,0:T(8,128)S(1)}, f32[8,128]{1,0:T(8,128)S(1)}, u32[]{:S(2)}, u32[]{:S(2)}) collective-permute-start(f32[8,128]{1,0:T(8,128)S(1)} %get-tuple-element.58), channel_id=1, source_target_pairs={{0,4},{1,5},{2,6},{3,7},{4,0},{5,1},{6,2},{7,3},{8,12},{9,13},{10,... | collective-permute-start | bytes 12296 | tf_op jit(solution)/shard_map/ppermute | solution.py:620
  252.1 6.7 %collective-permute-start.5 = (f32[8,128]{1,0:T(8,128)S(1)}, f32[8,128]{1,0:T(8,128)S(1)}, u32[]{:S(2)}, u32[]{:S(2)}) collective-permute-start(f32[8,128]{1,0:T(8,128)S(1)} %get-tuple-element.59), channel_id=1, source_target_pairs={{0,3},{1,4},{2,5},{3,6},{4,7},{5,0},{6,1},{7,2},{8,11},{9,12},{10,... | collective-permute-start | bytes 12296 | tf_op jit(solution)/shard_map/ppermute | solution.py:620
  256.4 5.0 %collective-permute-start.4 = (f32[8,128]{1,0:T(8,128)S(1)}, f32[8,128]{1,0:T(8,128)S(1)}, u32[]{:S(2)}, u32[]{:S(2)}) collective-permute-start(f32[8,128]{1,0:T(8,128)S(1)} %get-tuple-element.60), channel_id=1, source_target_pairs={{0,2},{1,3},{2,4},{3,5},{4,6},{5,7},{6,0},{7,1},{8,10},{9,11},{10,... | collective-permute-start | bytes 12296 | tf_op jit(solution)/shard_map/ppermute | solution.py:620
  288.2 8.7 %copy-start = (f32[64,24,128]{2,1,0:T(8,128)}, f32[64,24,128]{2,1,0:T(8,128)S(1)}, u32[]{:S(2)}) copy-start(f32[64,24,128]{2,1,0:T(8,128)S(1)} %all_to_all.20) | copy-start | bytes 2359300
  288.2 15.1 %collective-permute-start.11 = (f32[64,8,128]{2,1,0:T(8,128)S(1)}, f32[64,8,128]{2,1,0:T(8,128)S(1)}, u32[]{:S(2)}, u32[]{:S(2)}) collective-permute-start(f32[64,8,128]{2,1,0:T(8,128)S(1)} %slice.34.refs_0_), channel_id=1, source_target_pairs={{0,128},{64,192},{128,0},{192,64},{1,129},{65,193},{129,1},{193,65... | collective-permute-start | bytes 786440 | tf_op jit(solution)/shard_map/ppermute | solution.py:625
  288.7 14.6 %collective-permute-start.10 = (f32[64,8,128]{2,1,0:T(8,128)S(1)}, f32[64,8,128]{2,1,0:T(8,128)S(1)}, u32[]{:S(2)}, u32[]{:S(2)}) collective-permute-start(f32[64,8,128]{2,1,0:T(8,128)S(1)} %slice.34.refs_0_), channel_id=1, source_target_pairs={{0,64},{64,0},{128,192},{192,128},{1,65},{65,1},{129,193},{193,129... | collective-permute-start | bytes 786440 | tf_op jit(solution)/shard_map/ppermute | solution.py:625
  303.3 1.6 collective-permute-start.12

commit v8 on v7

--- a/solution.py
+++ b/solution.py
@@ -17,7 +17,7 @@
 KZ = 16
 C = 384
 HALF = BS // 2
-FIRST = 40
+FIRST = 32
 BATCH = 4
 SECOND = HALF - FIRST
 CELLS = 64

time: 307 us -> 307 us (level)
  blocking collectives: 26.1 us -> 37.7 us
  waiting for transfers between devices: 136 us -> 125 us
    ppermute x7, waiting for transfers between devices: 19.5 us -> 7.72 us  [owned_rows(): lax.ppermute(piece, 'py', [(n, (n + offset) % 8) for n in range(8)])]
    all_to_all x1, blocking collectives: 26.1 us -> 37.7 us  [exchange(): lax.all_to_all(value, ('px', 'py'), split_axis=0, concat_axis=0, tiled=True)]
where the time goes in v8:
time: 307 us; the launch traced here: 306 us
  waiting for transfers between devices  125 us (41%)
  starting transfers between devices  66.4 us (22%)
  Pallas kernels  63.1 us (21%)
  blocking collectives  37.7 us (12%)
  local copies, waits for them, and re-layouts  7.88 us (3%)
  other arithmetic  5.26 us (2%)
    all_to_all x3, waiting for transfers between devices, exchange(): lax.all_to_all(value, ('px', 'py'), split_axis=0, concat_axis=0, tiled=True)  108 us
    all_to_all x1, blocking collectives, exchange(): lax.all_to_all(value, ('px', 'py'), split_axis=0, concat_axis=0, tiled=True)  37.7 us
    all_to_all x3, starting transfers between devices, exchange(): lax.all_to_all(value, ('px', 'py'), split_axis=0, concat_axis=0, tiled=True)  37 us
    pallas_call x4, Pallas kernels, call(): pl.pallas_call(kernel, out_shape=out_shape, in_specs=place(len(args)), ou...  31.1 us
    pallas_call x1, Pallas kernels, shards(): pl.pallas_call(forward_kernel, out_shape=(GROUPED,) * 4, in_specs=[pl.Blo...  17.7 us
    ppermute x7, starting transfers between devices, owned_rows(): lax.ppermute(piece, 'py', [(n, (n + offset) % 8) for n in range(8)])  15.6 us
    pallas_call x1, Pallas kernels, rest(): pl.pallas_call(rest_kernel, grid=(GROUPS,), out_shape=(jax.ShapeDtypeStru...  13.2 us
    ppermute x3, starting transfers between devices, partner(): return lax.ppermute(value, 'dp', [(n, n ^ flip) for n in range(4)])  8.41 us
  transfers between devices with their start and end apart: 16, of which 9 were waited for; matrix products, arithmetic and copies ran while one was open for 4% of the time, Pallas kernels for 14%

profile of v8, /device:TPU:1, one launch (start us, length us, event | category | flops | bytes accessed | tf_op | source)
XLA Modules:
  0.0 305.8 jit_solution(7948222392825300381)
XLA Ops:
  0.6 5.8 %shard_map.147 = f32[4,16,96,128]{3,2,1,0:T(8,128)} custom-call(bf16[2048,384]{1,0:T(8,128)(2,1)} %bitcast.75, bf16[256,512]{1,0:T(8,128)(2,1)} %constant.161.clone.both_hbm), custom_call_target="tpu_custom_call" | custom-call | flops 800000000 | bytes 5000000 | tf_op jit(solution)/shard_map/pallas_call | solution.py:512
  6.4 15.4 %all-to-all-start.1 = ((f32[64,96,128]{2,1,0:T(8,128)}), f32[64,96,128]{2,1,0:T(8,128)}, u32[]{:S(2)}, u32[]{:S(2)}) async-start(f32[64,96,128]{2,1,0:T(8,128)} %bitcast.71), calls=%async_computation.1 | async-start | bytes 6291456 | tf_op jit(solution)/shard_map/all_to_all | solution.py:629
  21.8 5.8 %shard_map.146 = f32[4,16,96,128]{3,2,1,0:T(8,128)} custom-call(bf16[2048,384]{1,0:T(8,128)(2,1)} %bitcast.73, bf16[256,512]{1,0:T(8,128)(2,1)} %constant.161.clone.both_hbm), custom_call_target="tpu_custom_call" | custom-call | flops 800000000 | bytes 5000000 | tf_op jit(solution)/shard_map/pallas_call | solution.py:512
  27.5 64.5 %all-to-all-done.1.src_ref = f32[64,96,128]{2,1,0:T(8,128)} async-done(((f32[64,96,128]{2,1,0:T(8,128)}), f32[64,96,128]{2,1,0:T(8,128)}, u32[]{:S(2)}, u32[]{:S(2)}) %all-to-all-start.1) | async-done | bytes 3145760 | tf_op jit(solution)/shard_map/all_to_all | solution.py:629
  92.0 11.2 %all-to-all-start = ((f32[64,96,128]{2,1,0:T(8,128)}), f32[64,96,128]{2,1,0:T(8,128)}, u32[]{:S(2)}, u32[]{:S(2)}) async-start(f32[64,96,128]{2,1,0:T(8,128)} %bitcast.70), calls=%async_computation | async-start | bytes 6291456 | tf_op jit(solution)/shard_map/all_to_all | solution.py:629
  112.1 17.7 %shard_map.148 = (f32[8,192,512]{2,1,0:T(8,128)}, f32[8,192,512]{2,1,0:T(8,128)}, f32[8,192,512]{2,1,0:T(8,128)}, f32[8,192,512]{2,1,0:T(8,128)}) custom-call(f32[1,1]{1,0:T(1,128)} %bitcast.18.doubling_ref, f32[64,96,128]{2,1,0:T(8,128)} %all-to-all-done.1.src_ref, f32[64,2,128]{2,1,0:T(2,128)} %constant.162.clone.twiddle_ref.twiddle_hbm, ...), custom_call_target="tpu_custom_call" | custom-call | flops 8000000000 | bytes 16000000 | tf_op jit(solution)/shard_map/pallas_call | solution.py:647
  129.8 43.2 %all-to-all-done.src_hbm = f32[64,96,128]{2,1,0:T(8,128)} async-done(((f32[64,96,128]{2,1,0:T(8,128)}), f32[64,96,128]{2,1,0:T(8,128)}, u32[]{:S(2)}, u32[]{:S(2)}) %all-to-all-start) | async-done | bytes 3145760 | tf_op jit(solution)/shard_map/all_to_all | solution.py:629
  173.1 13.2 %shard_map.149 = (f32[8,192,512]{2,1,0:T(8,128)}, f32[64,64,128]{2,1,0:T(8,128)}) custom-call(f32[64,96,128]{2,1,0:T(8,128)} %all-to-all-done.src_hbm, f32[64,2,128]{2,1,0:T(2,128)} %constant.162.clone.twiddle_ref.twiddle_hbm, bf16[768,256]{1,0:T(8,128)(2,1)} %constant.163.clone.t_ref.t_hbm, bf16[768,256]{1,0:T(8,128)(2,1)} %constant.164.clone.back_hbm.back_ref, ...), custom_call_target="tpu_custom_call" | custom-call | flops 10000000000 | bytes 20000000 | tf_op jit(solution)/shard_map/pallas_call | solution.py:512
  186.3 10.4 %all-to-all-start.2 = ((f32[64,64,128]{2,1,0:T(8,128)}), f32[64,64,128]{2,1,0:T(8,128)}, u32[]{:S(2)}, u32[]{:S(2)}) async-start(f32[64,64,128]{2,1,0:T(8,128)} %get-tuple-element.24), calls=%async_computation.2 | async-start | bytes 4194304 | tf_op jit(solution)/shard_map/all_to_all | solution.py:629
  197.5 13.2 %shard_map.150 = (f32[512,128]{1,0:T(8,128)}, f32[64,40,128]{2,1,0:T(8,128)}) custom-call(f32[8,192,512]{2,1,0:T(8,128)} %get-tuple-element.25.spec_ref, f32[8,192,512]{2,1,0:T(8,128)} %get-tuple-element.26.outer_ref, f32[8,192,512]{2,1,0:T(8,128)} %get-tuple-element.27.two_ref, f32[8,192,512]{2,1,0:T(8,128)} %get-tuple-element.22.slope_hbm.slope_ref, ...), custom_call_target="tpu_custom_call" | custom-call | flops 8000000000 | bytes 16000000 | tf_op jit(solution)/shard_map/pallas_call | solution.py:547
  210.8 0.9 constant_dynamic-slice_fusion.11
  211.7 2.2 collective-permute-start
  213.9 1.0 collective-permute-done
  216.5 3.5 %collective-permute-done.1 = f32[128,128]{1,0:T(8,128)S(1)} collective-permute-done((f32[128,128]{1,0:T(8,128)S(1)}, f32[128,128]{1,0:T(8,128)S(1)}, u32[]{:S(2)}, u32[]{:S(2)}) %collective-permute-start.1) | collective-permute-done | bytes 65568 | tf_op jit(solution)/shard_map/ppermute | solution.py:606
  220.0 2.5 collective-permute-start.2
  222.5 3.1 %collective-permute-done.2 = f32[64,128]{1,0:T(8,128)S(1)} collective-permute-done((f32[64,128]{1,0:T(8,128)S(1)}, f32[64,128]{1,0:T(8,128)S(1)}, u32[]{:S(2)}, u32[]{:S(2)}) %collective-permute-start.2) | collective-permute-done | bytes 32800 | tf_op jit(solution)/shard_map/ppermute | solution.py:606
  225.7 1.4 collective-permute-start.3
  227.0 1.4 collective-permute-start.9
  228.4 2.5 collective-permute-start.8
  231.0 2.7 collective-permute-start.7
  233.7 1.6 collective-permute-start.6
  235.2 4.9 %collective-permute-done.3 = f32[8,128]{1,0:T(8,128)S(1)} collective-permute-done((f32[8,128]{1,0:T(8,128)S(1)}, f32[8,128]{1,0:T(8,128)S(1)}, u32[]{:S(2)}, u32[]{:S(2)}) %collective-permute-start.3) | collective-permute-done | bytes 4128 | tf_op jit(solution)/shard_map/ppermute | solution.py:620
  240.1 3.9 %collective-permute-start.5 = (f32[8,128]{1,0:T(8,128)S(1)}, f32[8,128]{1,0:T(8,128)S(1)}, u32[]{:S(2)}, u32[]{:S(2)}) collective-permute-start(f32[8,128]{1,0:T(8,128)S(1)} %get-tuple-element.59), channel_id=1, source_target_pairs={{0,3},{1,4},{2,5},{3,6},{4,7},{5,0},{6,1},{7,2},{8,11},{9,12},{10,... | collective-permute-start | bytes 12296 | tf_op jit(solution)/shard_map/ppermute | solution.py:620
  244.0 2.1 collective-permute-start.4
  246.1 0.9 collective-permute-done.5
  247.1 1.9 collective-permute-done.4
  249.7 37.7 %all_to_all.20 = f32[64,40,128]{2,1,0:T(8,128)S(1)} all-to-all(f32[64,40,128]{2,1,0:T(8,128)} %broadcast_dynamic-update-slice_fusion), channel_id=1, replica_groups=mesh['dp'=4,'px'=8,'py'=8] {'px','py'}, dimensions={0} | all-to-all | bytes 2621440 | tf_op jit(solution)/shard_map/all_to_all | solution.py:629
  287.5 1.0 copy-done
  288.9 7.9 %collective-permute-start.10 = (f32[64,8,128]{2,1,0:T(8,128)S(1)}, f32[64,8,128]{2,1,0:T(8,128)S(1)}, u32[]{:S(2)}, u32[]{:S(2)}) collective-permute-start(f32[64,8,128]{2,1,0:T(8,128)S(1)} %slice.34.refs_0_), channel_id=1, source_target_pairs={{0,64},{64,0},{128,192},{192,128},{1,65},{65,1},{129,193},{193,129... | collective-permute-start | bytes 786440 | tf_op jit(solution)/shard_map/ppermute | solution.py:625
  296.8 6.3 %shard_map.151 = bf16[2048,384]{1,0:T(8,128)(2,1)} custom-call(f32[4,16,64,128]{3,2,1,0:T(8,128)} %bitcast.31.first_hbm, f32[4,16,40,128]{3,2,1,0:T(8,128)} %bitcast.72, bf16[2048,384]{1,0:T(8,128)(2,1)} %bitcast.74, bf16[256,768]{1,0:T(8,128)(2,1)} %constant.165.clone.table_hbm), custom_call_target="tpu_custom_call" | custom-call | flops 1200000000 | bytes 7000000 | tf_op jit(solution)/shard_map/pallas_call | solution.py:512
  303.3 1.5 collective-permute-done.12.refs_3_
  304.8 1.0 shard_map.152
  (43 shorter events, 12.4 us)
Async XLA Ops:
  6.4 85.6 %all-to-all-start.1 = ((f32[64,96,128]{2,1,0:T(8,128)}), f32[64,96,128]{2,1,0:T(8,128)}, u32[]{:S(2)}, u32[]{:S(2)}) async-start(f32[64,96,128]{2,1,0:T(8,128)} %bitcast.71), calls=%async_computation.1 | async-start | bytes 6291456 | tf_op jit(solution)/shard_map/all_to_all | solution.py:629
  92.0 81.0 %all-to-all-start = ((f32[64,96,128]{2,1,0:T(8,128)}), f32[64,96,128]{2,1,0:T(8,128)}, u32[]{:S(2)}, u32[]{:S(2)}) async-start(f32[64,96,128]{2,1,0:T(8,128)} %bitcast.70), calls=%async_computation | async-start | bytes 6291456 | tf_op jit(solution)/shard_map/all_to_all | solution.py:629
  186.3 63.4 %all-to-all-start.2 = ((f32[64,64,128]{2,1,0:T(8,128)}), f32[64,64,128]{2,1,0:T(8,128)}, u32[]{:S(2)}, u32[]{:S(2)}) async-start(f32[64,64,128]{2,1,0:T(8,128)} %get-tuple-element.24), calls=%async_computation.2 | async-start | bytes 4194304 | tf_op jit(solution)/shard_map/all_to_all | solution.py:629
  211.7 3.2 %collective-permute-start = (f32[256,128]{1,0:T(8,128)S(1)}, f32[256,128]{1,0:T(8,128)S(1)}, u32[]{:S(2)}, u32[]{:S(2)}) collective-permute-start(f32[256,128]{1,0:T(8,128)S(1)} %constant_dynamic-slice_fusion.11), channel_id=1, source_target_pairs={{0,64},{64,0},{128,192},{192,128},{1,65},{65,1},{129,193},{193,129... | collective-permute-start | bytes 393224 | tf_op jit(solution)/shard_map/ppermute | solution.py:606
  215.8 4.2 %collective-permute-start.1 = (f32[128,128]{1,0:T(8,128)S(1)}, f32[128,128]{1,0:T(8,128)S(1)}, u32[]{:S(2)}, u32[]{:S(2)}) collective-permute-start(f32[128,128]{1,0:T(8,128)S(1)} %constant_dynamic-slice_fusion.10), channel_id=1, source_target_pairs={{0,128},{64,192},{128,0},{192,64},{1,129},{65,193},{129,1},{193,65... | collective-permute-start | bytes 196616 | tf_op jit(solution)/shard_map/ppermute | solution.py:606
  220.0 5.6 %collective-permute-start.2 = (f32[64,128]{1,0:T(8,128)S(1)}, f32[64,128]{1,0:T(8,128)S(1)}, u32[]{:S(2)}, u32[]{:S(2)}) collective-permute-start(f32[64,128]{1,0:T(8,128)S(1)} %constant_dynamic-slice_fusion.9), channel_id=1, source_target_pairs={{0,8},{8,0},{16,24},{24,16},{32,40},{40,32},{48,56},{56,48},{1,9},... | collective-permute-start | bytes 98312 | tf_op jit(solution)/shard_map/ppermute | solution.py:606
  225.7 14.4 %collective-permute-start.3 = (f32[8,128]{1,0:T(8,128)S(1)}, f32[8,128]{1,0:T(8,128)S(1)}, u32[]{:S(2)}, u32[]{:S(2)}) collective-permute-start(f32[8,128]{1,0:T(8,128)S(1)} %get-tuple-element.54), channel_id=1, source_target_pairs={{0,1},{1,2},{2,3},{3,4},{4,5},{5,6},{6,7},{7,0},{8,9},{9,10},{10,1... | collective-permute-start | bytes 12296 | tf_op jit(solution)/shard_map/ppermute | solution.py:620
  227.0 17.0 %collective-permute-start.9 = (f32[8,128]{1,0:T(8,128)S(1)}, f32[8,128]{1,0:T(8,128)S(1)}, u32[]{:S(2)}, u32[]{:S(2)}) collective-permute-start(f32[8,128]{1,0:T(8,128)S(1)} %get-tuple-element.55), channel_id=1, source_target_pairs={{0,7},{1,0},{2,1},{3,2},{4,3},{5,4},{6,5},{7,6},{8,15},{9,8},{10,9... | collective-permute-start | bytes 12296 | tf_op jit(solution)/shard_map/ppermute | solution.py:620
  228.4 17.7 %collective-permute-start.8 = (f32[8,128]{1,0:T(8,128)S(1)}, f32[8,128]{1,0:T(8,128)S(1)}, u32[]{:S(2)}, u32[]{:S(2)}) collective-permute-start(f32[8,128]{1,0:T(8,128)S(1)} %get-tuple-element.56), channel_id=1, source_target_pairs={{0,6},{1,7},{2,0},{3,1},{4,2},{5,3},{6,4},{7,5},{8,14},{9,15},{10,... | collective-permute-start | bytes 12296 | tf_op jit(solution)/shard_map/ppermute | solution.py:620
  231.0 15.1 %collective-permute-start.7 = (f32[8,128]{1,0:T(8,128)S(1)}, f32[8,128]{1,0:T(8,128)S(1)}, u32[]{:S(2)}, u32[]{:S(2)}) collective-permute-start(f32[8,128]{1,0:T(8,128)S(1)} %get-tuple-element.57), channel_id=1, source_target_pairs={{0,5},{1,6},{2,7},{3,0},{4,1},{5,2},{6,3},{7,4},{8,13},{9,14},{10,... | collective-permute-start | bytes 12296 | tf_op jit(solution)/shard_map/ppermute | solution.py:620
  233.7 12.5 %collective-permute-start.6 = (f32[8,128]{1,0:T(8,128)S(1)}, f32[8,128]{1,0:T(8,128)S(1)}, u32[]{:S(2)}, u32[]{:S(2)}) collective-permute-start(f32[8,128]{1,0:T(8,128)S(1)} %get-tuple-element.58), channel_id=1, source_target_pairs={{0,4},{1,5},{2,6},{3,7},{4,0},{5,1},{6,2},{7,3},{8,12},{9,13},{10,... | collective-permute-start | bytes 12296 | tf_op jit(solution)/shard_map/ppermute | solution.py:620
  240.1 6.9 %collective-permute-start.5 = (f32[8,128]{1,0:T(8,128)S(1)}, f32[8,128]{1,0:T(8,128)S(1)}, u32[]{:S(2)}, u32[]{:S(2)}) collective-permute-start(f32[8,128]{1,0:T(8,128)S(1)} %get-tuple-element.59), channel_id=1, source_target_pairs={{0,3},{1,4},{2,5},{3,6},{4,7},{5,0},{6,1},{7,2},{8,11},{9,12},{10,... | collective-permute-start | bytes 12296 | tf_op jit(solution)/shard_map/ppermute | solution.py:620
  244.0 5.0 %collective-permute-start.4 = (f32[8,128]{1,0:T(8,128)S(1)}, f32[8,128]{1,0:T(8,128)S(1)}, u32[]{:S(2)}, u32[]{:S(2)}) collective-permute-start(f32[8,128]{1,0:T(8,128)S(1)} %get-tuple-element.60), channel_id=1, source_target_pairs={{0,2},{1,3},{2,4},{3,5},{4,6},{5,7},{6,0},{7,1},{8,10},{9,11},{10,... | collective-permute-start | bytes 12296 | tf_op jit(solution)/shard_map/ppermute | solution.py:620
  287.4 1.1 copy-start
  288.5 14.6 %collective-permute-start.11 = (f32[64,8,128]{2,1,0:T(8,128)S(1)}, f32[64,8,128]{2,1,0:T(8,128)S(1)}, u32[]{:S(2)}, u32[]{:S(2)}) collective-permute-start(f32[64,8,128]{2,1,0:T(8,128)S(1)} %slice.34.refs_0_), channel_id=1, source_target_pairs={{0,128},{64,192},{128,0},{192,64},{1,129},{65,193},{129,1},{193,65... | collective-permute-start | bytes 786440 | tf_op jit(solution)/shard_map/ppermute | solution.py:625
  288.9 14.3 %collective-permute-start.10 = (f32[64,8,128]{2,1,0:T(8,128)S(1)}, f32[64,8,128]{2,1,0:T(8,128)S(1)}, u32[]{:S(2)}, u32[]{:S(2)}) collective-permute-start(f32[64,8,128]{2,1,0:T(8,128)S(1)} %slice.34.refs_0_), channel_id=1, source_target_pairs={{0,64},{64,0},{128,192},{192,128},{1,65},{65,1},{129,193},{193,129... | collective-permute-start | bytes 786440 | tf_op jit(solution)/shard_map/ppermute | solution.py:625
  303.2 1.6 collective-permute-start.12

commit v9 on v7

--- a/solution.py
+++ b/solution.py
@@ -308,14 +308,15 @@
     two_ref, out_ref, work_ref, part_ref, src_sems, sems, square_sems, slope_sems,
     two_sems, out_sems,
 ):
-    for p in range(8):
-        block_of(src_hbm, src_ref, src_sems, p).start()
     pairs = (
         (twiddle_hbm, twiddle_ref), (t_hbm, t_ref), (w2_hbm, w2),
         (w1_hbm, w1), (back_hbm, back_ref),
     )
     loads = [pltpu.make_async_copy(a, b, sems.at[n]) for n, (a, b) in enumerate(pairs)]
-    for load in loads:
+    loads[0].start()
+    for p in range(8):
+        block_of(src_hbm, src_ref, src_sems, p).start()
+    for load in loads[1:]:
         load.start()
     loads[0].wait()
 

time: 307 us -> 307 us (level)
  no operation moved by 1% of the time
where the time goes in v9:
time: 307 us; the launch traced here: 306 us
  waiting for transfers between devices  136 us (44%)
  starting transfers between devices  67.3 us (22%)
  Pallas kernels  63.8 us (21%)
  blocking collectives  26.1 us (9%)
  local copies, waits for them, and re-layouts  6.83 us (2%)
  other arithmetic  5.29 us (2%)
    all_to_all x3, waiting for transfers between devices, exchange(): lax.all_to_all(value, ('px', 'py'), split_axis=0, concat_axis=0, tiled=True)  108 us
    all_to_all x3, starting transfers between devices, exchange(): lax.all_to_all(value, ('px', 'py'), split_axis=0, concat_axis=0, tiled=True)  37 us
    pallas_call x4, Pallas kernels, call(): pl.pallas_call(kernel, out_shape=out_shape, in_specs=place(len(args)), ou...  31.7 us
    all_to_all x1, blocking collectives, exchange(): lax.all_to_all(value, ('px', 'py'), split_axis=0, concat_axis=0, tiled=True)  26.1 us
    ppermute x7, waiting for transfers between devices, owned_rows(): lax.ppermute(piece, 'py', [(n, (n + offset) % 8) for n in range(8)])  19.5 us
    pallas_call x1, Pallas kernels, shards(): pl.pallas_call(forward_kernel, out_shape=(GROUPED,) * 4, in_specs=[pl.Blo...  17.7 us
    ppermute x7, starting transfers between devices, owned_rows(): lax.ppermute(piece, 'py', [(n, (n + offset) % 8) for n in range(8)])  16 us
    pallas_call x1, Pallas kernels, rest(): pl.pallas_call(rest_kernel, grid=(GROUPS,), out_shape=(jax.ShapeDtypeStru...  13.4 us
  transfers between devices with their start and end apart: 16, of which 9 were waited for; matrix products, arithmetic and copies ran while one was open for 4% of the time, Pallas kernels for 14%

profile of v9, /device:TPU:1, one launch (start us, length us, event | category | flops | bytes accessed | tf_op | source)
XLA Modules:
  0.0 305.9 jit_solution(528916213529219754)
XLA Ops:
  0.6 5.8 %shard_map.147 = f32[4,16,96,128]{3,2,1,0:T(8,128)} custom-call(bf16[2048,384]{1,0:T(8,128)(2,1)} %bitcast.78, bf16[256,512]{1,0:T(8,128)(2,1)} %constant.159.clone.both_hbm), custom_call_target="tpu_custom_call" | custom-call | flops 800000000 | bytes 5000000 | tf_op jit(solution)/shard_map/pallas_call | solution.py:513
  6.4 15.4 %all-to-all-start.1 = ((f32[64,96,128]{2,1,0:T(8,128)}), f32[64,96,128]{2,1,0:T(8,128)}, u32[]{:S(2)}, u32[]{:S(2)}) async-start(f32[64,96,128]{2,1,0:T(8,128)} %bitcast.74), calls=%async_computation.1 | async-start | bytes 6291456 | tf_op jit(solution)/shard_map/all_to_all | solution.py:630
  21.8 5.8 %shard_map.146 = f32[4,16,96,128]{3,2,1,0:T(8,128)} custom-call(bf16[2048,384]{1,0:T(8,128)(2,1)} %bitcast.75, bf16[256,512]{1,0:T(8,128)(2,1)} %constant.159.clone.both_hbm), custom_call_target="tpu_custom_call" | custom-call | flops 800000000 | bytes 5000000 | tf_op jit(solution)/shard_map/pallas_call | solution.py:513
  27.5 64.5 %all-to-all-done.1.src_ref = f32[64,96,128]{2,1,0:T(8,128)} async-done(((f32[64,96,128]{2,1,0:T(8,128)}), f32[64,96,128]{2,1,0:T(8,128)}, u32[]{:S(2)}, u32[]{:S(2)}) %all-to-all-start.1) | async-done | bytes 3145760 | tf_op jit(solution)/shard_map/all_to_all | solution.py:630
  92.0 11.2 %all-to-all-start = ((f32[64,96,128]{2,1,0:T(8,128)}), f32[64,96,128]{2,1,0:T(8,128)}, u32[]{:S(2)}, u32[]{:S(2)}) async-start(f32[64,96,128]{2,1,0:T(8,128)} %bitcast.73), calls=%async_computation | async-start | bytes 6291456 | tf_op jit(solution)/shard_map/all_to_all | solution.py:630
  108.4 0.9 copy.23.w2
  112.1 17.7 %shard_map.148 = (f32[8,192,512]{2,1,0:T(8,128)}, f32[8,192,512]{2,1,0:T(8,128)}, f32[8,192,512]{2,1,0:T(8,128)}, f32[8,192,512]{2,1,0:T(8,128)}) custom-call(f32[1,1]{1,0:T(1,128)} %bitcast.18.doubling_ref, f32[64,96,128]{2,1,0:T(8,128)} %all-to-all-done.1.src_ref, f32[64,2,128]{2,1,0:T(2,128)} %constant.160.clone.twiddle_ref.twiddle_hbm, ...), custom_call_target="tpu_custom_call" | custom-call | flops 8000000000 | bytes 16000000 | tf_op jit(solution)/shard_map/pallas_call | solution.py:648
  129.9 43.2 %all-to-all-done.src_hbm = f32[64,96,128]{2,1,0:T(8,128)} async-done(((f32[64,96,128]{2,1,0:T(8,128)}), f32[64,96,128]{2,1,0:T(8,128)}, u32[]{:S(2)}, u32[]{:S(2)}) %all-to-all-start) | async-done | bytes 3145760 | tf_op jit(solution)/shard_map/all_to_all | solution.py:630
  173.1 13.8 %shard_map.149 = (f32[8,192,512]{2,1,0:T(8,128)}, f32[64,80,128]{2,1,0:T(8,128)}) custom-call(f32[64,96,128]{2,1,0:T(8,128)} %all-to-all-done.src_hbm, f32[64,2,128]{2,1,0:T(2,128)} %constant.160.clone.twiddle_ref.twiddle_hbm, bf16[768,256]{1,0:T(8,128)(2,1)} %constant.161.clone.t_ref.t_hbm, bf16[768,256]{1,0:T(8,128)(2,1)} %constant.162.clone.back_hbm.back_ref, ...), custom_call_target="tpu_custom_call" | custom-call | flops 10000000000 | bytes 20000000 | tf_op jit(solution)/shard_map/pallas_call | solution.py:513
  186.9 10.4 %all-to-all-start.2 = ((f32[64,80,128]{2,1,0:T(8,128)}), f32[64,80,128]{2,1,0:T(8,128)}, u32[]{:S(2)}, u32[]{:S(2)}) async-start(f32[64,80,128]{2,1,0:T(8,128)} %get-tuple-element.24), calls=%async_computation.2 | async-start | bytes 5242880 | tf_op jit(solution)/shard_map/all_to_all | solution.py:630
  198.0 13.4 %shard_map.150 = (f32[512,128]{1,0:T(8,128)}, f32[64,24,128]{2,1,0:T(8,128)}) custom-call(f32[8,192,512]{2,1,0:T(8,128)} %get-tuple-element.25.spec_ref, f32[8,192,512]{2,1,0:T(8,128)} %get-tuple-element.26.outer_ref, f32[8,192,512]{2,1,0:T(8,128)} %get-tuple-element.27.two_ref, f32[8,192,512]{2,1,0:T(8,128)} %get-tuple-element.22.slope_hbm.slope_ref, ...), custom_call_target="tpu_custom_call" | custom-call | flops 8000000000 | bytes 16000000 | tf_op jit(solution)/shard_map/pallas_call | solution.py:548
  211.4 0.9 constant_dynamic-slice_fusion.11
  212.4 2.4 collective-permute-start
  214.8 1.0 collective-permute-done
  215.8 0.9 dynamic-slice_add_fusion
  217.2 3.7 %collective-permute-done.1 = f32[128,128]{1,0:T(8,128)S(1)} collective-permute-done((f32[128,128]{1,0:T(8,128)S(1)}, f32[128,128]{1,0:T(8,128)S(1)}, u32[]{:S(2)}, u32[]{:S(2)}) %collective-permute-start.1) | collective-permute-done | bytes 65568 | tf_op jit(solution)/shard_map/ppermute | solution.py:607
  220.9 2.6 collective-permute-start.2
  223.5 2.4 collective-permute-done.2
  225.9 3.2 %collective-permute-start.3 = (f32[8,128]{1,0:T(8,128)S(1)}, f32[8,128]{1,0:T(8,128)S(1)}, u32[]{:S(2)}, u32[]{:S(2)}) collective-permute-start(f32[8,128]{1,0:T(8,128)S(1)} %get-tuple-element.54), channel_id=1, source_target_pairs={{0,1},{1,2},{2,3},{3,4},{4,5},{5,6},{6,7},{7,0},{8,9},{9,10},{10,1... | collective-permute-start | bytes 12296 | tf_op jit(solution)/shard_map/ppermute | solution.py:621
  229.5 3.0 collective-permute-start.8
  232.5 1.9 collective-permute-start.7
  234.4 1.9 collective-permute-start.6
  236.4 15.7 %collective-permute-done.3 = f32[8,128]{1,0:T(8,128)S(1)} collective-permute-done((f32[8,128]{1,0:T(8,128)S(1)}, f32[8,128]{1,0:T(8,128)S(1)}, u32[]{:S(2)}, u32[]{:S(2)}) %collective-permute-start.3) | collective-permute-done | bytes 4128 | tf_op jit(solution)/shard_map/ppermute | solution.py:621
  252.1 4.3 %collective-permute-start.5 = (f32[8,128]{1,0:T(8,128)S(1)}, f32[8,128]{1,0:T(8,128)S(1)}, u32[]{:S(2)}, u32[]{:S(2)}) collective-permute-start(f32[8,128]{1,0:T(8,128)S(1)} %get-tuple-element.59), channel_id=1, source_target_pairs={{0,3},{1,4},{2,5},{3,6},{4,7},{5,0},{6,1},{7,2},{8,11},{9,12},{10,... | collective-permute-start | bytes 12296 | tf_op jit(solution)/shard_map/ppermute | solution.py:621
  256.4 1.2 collective-permute-start.4
  257.6 1.2 collective-permute-done.5
  258.8 2.6 collective-permute-done.4
  262.1 26.1 %all_to_all.20 = f32[64,24,128]{2,1,0:T(8,128)S(1)} all-to-all(f32[64,24,128]{2,1,0:T(8,128)} %broadcast_dynamic-update-slice_fusion), channel_id=1, replica_groups=mesh['dp'=4,'px'=8,'py'=8] {'px','py'}, dimensions={0} | all-to-all | bytes 1572864 | tf_op jit(solution)/shard_map/all_to_all | solution.py:630
  288.7 8.2 %collective-permute-start.10 = (f32[64,8,128]{2,1,0:T(8,128)S(1)}, f32[64,8,128]{2,1,0:T(8,128)S(1)}, u32[]{:S(2)}, u32[]{:S(2)}) collective-permute-start(f32[64,8,128]{2,1,0:T(8,128)S(1)} %slice.34.refs_0_), channel_id=1, source_target_pairs={{0,64},{64,0},{128,192},{192,128},{1,65},{65,1},{129,193},{193,129... | collective-permute-start | bytes 786440 | tf_op jit(solution)/shard_map/ppermute | solution.py:626
  296.9 6.3 %shard_map.151 = bf16[2048,384]{1,0:T(8,128)(2,1)} custom-call(f32[4,16,80,128]{3,2,1,0:T(8,128)} %bitcast.31.first_hbm, f32[4,16,24,128]{3,2,1,0:T(8,128)} %bitcast.77, bf16[2048,384]{1,0:T(8,128)(2,1)} %bitcast.76, bf16[256,768]{1,0:T(8,128)(2,1)} %constant.163.clone.table_hbm), custom_call_target="tpu_custom_call" | custom-call | flops 1200000000 | bytes 7000000 | tf_op jit(solution)/shard_map/pallas_call | solution.py:513
  303.5 1.4 collective-permute-done.12.refs_3_
  304.9 1.0 shard_map.152
  (42 shorter events, 11.0 us)
Async XLA Ops:
  6.4 85.6 %all-to-all-start.1 = ((f32[64,96,128]{2,1,0:T(8,128)}), f32[64,96,128]{2,1,0:T(8,128)}, u32[]{:S(2)}, u32[]{:S(2)}) async-start(f32[64,96,128]{2,1,0:T(8,128)} %bitcast.74), calls=%async_computation.1 | async-start | bytes 6291456 | tf_op jit(solution)/shard_map/all_to_all | solution.py:630
  92.0 81.0 %all-to-all-start = ((f32[64,96,128]{2,1,0:T(8,128)}), f32[64,96,128]{2,1,0:T(8,128)}, u32[]{:S(2)}, u32[]{:S(2)}) async-start(f32[64,96,128]{2,1,0:T(8,128)} %bitcast.73), calls=%async_computation | async-start | bytes 6291456 | tf_op jit(solution)/shard_map/all_to_all | solution.py:630
  186.9 75.2 %all-to-all-start.2 = ((f32[64,80,128]{2,1,0:T(8,128)}), f32[64,80,128]{2,1,0:T(8,128)}, u32[]{:S(2)}, u32[]{:S(2)}) async-start(f32[64,80,128]{2,1,0:T(8,128)} %get-tuple-element.24), calls=%async_computation.2 | async-start | bytes 5242880 | tf_op jit(solution)/shard_map/all_to_all | solution.py:630
  212.4 3.4 %collective-permute-start = (f32[256,128]{1,0:T(8,128)S(1)}, f32[256,128]{1,0:T(8,128)S(1)}, u32[]{:S(2)}, u32[]{:S(2)}) collective-permute-start(f32[256,128]{1,0:T(8,128)S(1)} %constant_dynamic-slice_fusion.11), channel_id=1, source_target_pairs={{0,64},{64,0},{128,192},{192,128},{1,65},{65,1},{129,193},{193,129... | collective-permute-start | bytes 393224 | tf_op jit(solution)/shard_map/ppermute | solution.py:607
  216.7 4.2 %collective-permute-start.1 = (f32[128,128]{1,0:T(8,128)S(1)}, f32[128,128]{1,0:T(8,128)S(1)}, u32[]{:S(2)}, u32[]{:S(2)}) collective-permute-start(f32[128,128]{1,0:T(8,128)S(1)} %constant_dynamic-slice_fusion.10), channel_id=1, source_target_pairs={{0,128},{64,192},{128,0},{192,64},{1,129},{65,193},{129,1},{193,65... | collective-permute-start | bytes 196616 | tf_op jit(solution)/shard_map/ppermute | solution.py:607
  220.9 4.9 %collective-permute-start.2 = (f32[64,128]{1,0:T(8,128)S(1)}, f32[64,128]{1,0:T(8,128)S(1)}, u32[]{:S(2)}, u32[]{:S(2)}) collective-permute-start(f32[64,128]{1,0:T(8,128)S(1)} %constant_dynamic-slice_fusion.9), channel_id=1, source_target_pairs={{0,8},{8,0},{16,24},{24,16},{32,40},{40,32},{48,56},{56,48},{1,9},... | collective-permute-start | bytes 98312 | tf_op jit(solution)/shard_map/ppermute | solution.py:607
  225.9 26.2 %collective-permute-start.3 = (f32[8,128]{1,0:T(8,128)S(1)}, f32[8,128]{1,0:T(8,128)S(1)}, u32[]{:S(2)}, u32[]{:S(2)}) collective-permute-start(f32[8,128]{1,0:T(8,128)S(1)} %get-tuple-element.54), channel_id=1, source_target_pairs={{0,1},{1,2},{2,3},{3,4},{4,5},{5,6},{6,7},{7,0},{8,9},{9,10},{10,1... | collective-permute-start | bytes 12296 | tf_op jit(solution)/shard_map/ppermute | solution.py:621
  229.1 27.3 %collective-permute-start.9 = (f32[8,128]{1,0:T(8,128)S(1)}, f32[8,128]{1,0:T(8,128)S(1)}, u32[]{:S(2)}, u32[]{:S(2)}) collective-permute-start(f32[8,128]{1,0:T(8,128)S(1)} %get-tuple-element.55), channel_id=1, source_target_pairs={{0,7},{1,0},{2,1},{3,2},{4,3},{5,4},{6,5},{7,6},{8,15},{9,8},{10,9... | collective-permute-start | bytes 12296 | tf_op jit(solution)/shard_map/ppermute | solution.py:621
  229.5 28.1 %collective-permute-start.8 = (f32[8,128]{1,0:T(8,128)S(1)}, f32[8,128]{1,0:T(8,128)S(1)}, u32[]{:S(2)}, u32[]{:S(2)}) collective-permute-start(f32[8,128]{1,0:T(8,128)S(1)} %get-tuple-element.56), channel_id=1, source_target_pairs={{0,6},{1,7},{2,0},{3,1},{4,2},{5,3},{6,4},{7,5},{8,14},{9,15},{10,... | collective-permute-start | bytes 12296 | tf_op jit(solution)/shard_map/ppermute | solution.py:621
  232.5 25.1 %collective-permute-start.7 = (f32[8,128]{1,0:T(8,128)S(1)}, f32[8,128]{1,0:T(8,128)S(1)}, u32[]{:S(2)}, u32[]{:S(2)}) collective-permute-start(f32[8,128]{1,0:T(8,128)S(1)} %get-tuple-element.57), channel_id=1, source_target_pairs={{0,5},{1,6},{2,7},{3,0},{4,1},{5,2},{6,3},{7,4},{8,13},{9,14},{10,... | collective-permute-start | bytes 12296 | tf_op jit(solution)/shard_map/ppermute | solution.py:621
  234.4 23.2 %collective-permute-start.6 = (f32[8,128]{1,0:T(8,128)S(1)}, f32[8,128]{1,0:T(8,128)S(1)}, u32[]{:S(2)}, u32[]{:S(2)}) collective-permute-start(f32[8,128]{1,0:T(8,128)S(1)} %get-tuple-element.58), channel_id=1, source_target_pairs={{0,4},{1,5},{2,6},{3,7},{4,0},{5,1},{6,2},{7,3},{8,12},{9,13},{10,... | collective-permute-start | bytes 12296 | tf_op jit(solution)/shard_map/ppermute | solution.py:621
  252.1 6.7 %collective-permute-start.5 = (f32[8,128]{1,0:T(8,128)S(1)}, f32[8,128]{1,0:T(8,128)S(1)}, u32[]{:S(2)}, u32[]{:S(2)}) collective-permute-start(f32[8,128]{1,0:T(8,128)S(1)} %get-tuple-element.59), channel_id=1, source_target_pairs={{0,3},{1,4},{2,5},{3,6},{4,7},{5,0},{6,1},{7,2},{8,11},{9,12},{10,... | collective-permute-start | bytes 12296 | tf_op jit(solution)/shard_map/ppermute | solution.py:621
  256.4 5.0 %collective-permute-start.4 = (f32[8,128]{1,0:T(8,128)S(1)}, f32[8,128]{1,0:T(8,128)S(1)}, u32[]{:S(2)}, u32[]{:S(2)}) collective-permute-start(f32[8,128]{1,0:T(8,128)S(1)} %get-tuple-element.60), channel_id=1, source_target_pairs={{0,2},{1,3},{2,4},{3,5},{4,6},{5,7},{6,0},{7,1},{8,10},{9,11},{10,... | collective-permute-start | bytes 12296 | tf_op jit(solution)/shard_map/ppermute | solution.py:621
  288.2 8.7 %copy-start = (f32[64,24,128]{2,1,0:T(8,128)}, f32[64,24,128]{2,1,0:T(8,128)S(1)}, u32[]{:S(2)}) copy-start(f32[64,24,128]{2,1,0:T(8,128)S(1)} %all_to_all.20) | copy-start | bytes 2359300
  288.2 15.1 %collective-permute-start.11 = (f32[64,8,128]{2,1,0:T(8,128)S(1)}, f32[64,8,128]{2,1,0:T(8,128)S(1)}, u32[]{:S(2)}, u32[]{:S(2)}) collective-permute-start(f32[64,8,128]{2,1,0:T(8,128)S(1)} %slice.34.refs_0_), channel_id=1, source_target_pairs={{0,128},{64,192},{128,0},{192,64},{1,129},{65,193},{129,1},{193,65... | collective-permute-start | bytes 786440 | tf_op jit(solution)/shard_map/ppermute | solution.py:626
  288.7 14.6 %collective-permute-start.10 = (f32[64,8,128]{2,1,0:T(8,128)S(1)}, f32[64,8,128]{2,1,0:T(8,128)S(1)}, u32[]{:S(2)}, u32[]{:S(2)}) collective-permute-start(f32[64,8,128]{2,1,0:T(8,128)S(1)} %slice.34.refs_0_), channel_id=1, source_target_pairs={{0,64},{64,0},{128,192},{192,128},{1,65},{65,1},{129,193},{193,129... | collective-permute-start | bytes 786440 | tf_op jit(solution)/shard_map/ppermute | solution.py:626
  303.3 1.6 collective-permute-start.12
